TPU v7x, 512 devices: a whole 4x4x16 slice. The times are simulated.
512 devices in a mesh: ctx: 64 (over x, z_lo, core), tp: 8 (over z_hi, y).
Axes of the slice: x: 4, y: 4, z: 16 (z_hi: 2, z_lo: 8; z = z_hi * 8 + z_lo), core: 2. Of those that a mesh axis runs over, the one named last changes fastest.
Arguments:
- queries: bfloat16 [8192, 8192], P('ctx', 'tp'), may hold values from -200 to 200
- keys: bfloat16 [8192, 1024], P('ctx', 'tp'), may hold values from -8 to 8
- values: bfloat16 [8192, 1024], P('ctx', 'tp'), may hold values from -6 to 6
- out_weight: bfloat16 [5120, 8192], P('ctx', 'tp'), may hold values from -0.25 to 0.25
- residual: bfloat16 [5120, 256], P('ctx'), may hold values from -200 to 200
- norm_gain: float32 [5120], replicated, may hold values from 0.5 to 1.5
- head_weight: bfloat16 [131072, 5120], P(('ctx', 'tp')), may hold values from -10 to 10
- sampled_ids: int32 [8192], replicated, may hold values from 0 to 131071
- loss_mask: int32 [8192], replicated, may hold values from 0 to 1, as said below
- doc_lengths: int32 [32], replicated, may hold values from 1 to 4224, 8192 in all
Outputs:
- context: bfloat16 [8192, 8192], P('ctx', 'tp')
- logprobs: float32 [8192], P('ctx')
Inputs may be any that keep to these rules, and one draw needn't show every extreme that they name: `loss_mask`: each aligned block of 128 positions holds exactly 4 ones. `doc_lengths`: one document has exactly 4224 positions.
All inputs are finite; a program needn't handle non-finite values.
Results may differ from a plain program's by a relative error of at most 0.0045.
Values may be sent and summed in bfloat16 or wider, within the bound.
No kernel may reach another device: no remote copies, remote signals or barrier semaphores. Data moves between devices by JAX's collectives and lax.ppermute only.
A program may use at most 128 MiB of HBM per device.

v0:
```python
import math

import jax
import jax.numpy as jnp
from jax import lax
from jax.sharding import PartitionSpec as P

HEAD_DIM = 128
SCORED = 4


neg_fill = -1e30
norm_eps = 1e-06


def document_index(positions, bounds):
    return jnp.sum((positions[:, None] >= bounds[None, :]).astype(jnp.int32), axis=1)


def body(
    queries,
    keys,
    values,
    out_weight,
    residual,
    norm_gain,
    head_weight,
    sampled_ids,
    loss_mask,
    doc_lengths,
):
    ctx_size = lax.axis_size("ctx")
    my_slab = lax.axis_index("ctx")
    row_count = queries.shape[0]
    local_kv = keys.shape[1] // HEAD_DIM
    local_heads = queries.shape[1] // HEAD_DIM
    group_size = local_heads // local_kv
    score_scale = 1.0 / math.sqrt(HEAD_DIM)
    bounds = jnp.cumsum(doc_lengths)
    query_pos = my_slab * row_count + jnp.arange(row_count, dtype=jnp.int32)
    query_doc = document_index(query_pos, bounds)
    doc_begin = jnp.max(jnp.where(bounds <= query_pos[0], bounds, 0))
    query_grid = queries.reshape(row_count, local_kv, group_size, HEAD_DIM)
    key_value = jnp.stack((keys, values), axis=0)
    initial = (
        jnp.full((row_count, local_kv, group_size), neg_fill, jnp.float32),
        jnp.zeros((row_count, local_kv, group_size), jnp.float32),
        jnp.zeros((row_count, local_kv, group_size, HEAD_DIM), jnp.float32),
    )
    portion = lax.all_gather(key_value, "ctx", axis=1, tiled=True)
    offset = jnp.int32(0)
    piece_len = portion.shape[1]

    def update(loop_state):
        run_max, weight_sum, weighted = loop_state
        key_pos = jnp.arange(piece_len, dtype=jnp.int32)
        key_doc = document_index(key_pos, bounds)
        visible = (
            (key_pos[None, :] <= query_pos[:, None]) & (key_doc[None, :] == query_doc[:, None])
        )[:, None, None, :]
        key_grid = portion[0].reshape(piece_len, local_kv, HEAD_DIM)
        value_grid = portion[1].reshape(piece_len, local_kv, HEAD_DIM)
        scores = (
            jnp.einsum("qkgd,pkd->qkgp", query_grid, key_grid, preferred_element_type=jnp.float32)
            * score_scale
        )
        scores = jnp.where(visible, scores, neg_fill)
        new_max = jnp.maximum(run_max, jnp.max(scores, axis=3))
        weights = jnp.where(visible, jnp.exp(scores - new_max[..., None]), 0.0)
        weight_sum = jnp.sum(weights, axis=3)
        weighted = jnp.einsum(
            "qkgp,pkd->qkgd",
            weights.astype(jnp.bfloat16),
            value_grid,
            preferred_element_type=jnp.float32,
        )
        return (new_max, weight_sum, weighted)

    unused = (offset + piece_len - 1 < doc_begin) | (offset > query_pos[row_count - 1])
    running = lax.cond(unused, lambda loop_state: loop_state, update, initial)
    run_max, weight_sum, weighted = running
    context = (
        (weighted / weight_sum[..., None])
        .astype(jnp.bfloat16)
        .reshape(row_count, local_heads * HEAD_DIM)
    )
    own_mask = lax.dynamic_slice_in_dim(loss_mask, my_slab * row_count, row_count, 0)
    own_rank = jnp.cumsum(own_mask) - 1
    chosen = (own_mask[None, :] == 1) & (
        own_rank[None, :] == jnp.arange(SCORED, dtype=jnp.int32)[:, None]
    )
    scored = jnp.dot(
        chosen.astype(jnp.bfloat16), context, preferred_element_type=jnp.float32
    ).astype(jnp.bfloat16)
    partial_value = lax.dot_general(
        out_weight,
        lax.all_gather(scored, "ctx", axis=0, tiled=True),
        (((1,), (1,)), ((), ())),
        preferred_element_type=jnp.float32,
    )
    summed = lax.psum(partial_value, "tp")
    hidden = (residual.astype(jnp.float32) + summed).astype(jnp.bfloat16)
    all_slabs = loss_mask.reshape(ctx_size, row_count)
    all_rank = jnp.cumsum(all_slabs, axis=1) - 1
    all_chosen = (all_slabs[:, None, :] == 1) & (
        all_rank[:, None, :] == jnp.arange(SCORED, dtype=jnp.int32)[None, :, None]
    )
    chosen_ids = jnp.sum(
        jnp.where(all_chosen, sampled_ids.reshape(ctx_size, row_count)[:, None, :], 0), axis=2
    ).reshape(ctx_size * SCORED)
    vocab_rows = head_weight.shape[0]
    vocab_ids = lax.axis_index(("ctx", "tp")) * vocab_rows + jnp.arange(vocab_rows, dtype=jnp.int32)
    gathered = lax.all_gather(hidden, "ctx", axis=0, tiled=True)
    mean_square = jnp.mean(jnp.square(gathered.astype(jnp.float32)), axis=0)
    normed = (
        gathered.astype(jnp.float32)
        * lax.rsqrt(mean_square + norm_eps)[None, :]
        * norm_gain[:, None]
    ).astype(jnp.bfloat16)
    logits = jnp.dot(head_weight, normed, preferred_element_type=jnp.float32)
    local_max = jnp.max(logits, axis=0)
    local_target = jnp.sum(
        jnp.where(vocab_ids[:, None] == chosen_ids[None, :], logits, 0.0), axis=0
    )
    global_max = lax.pmax(local_max, ("ctx", "tp"))
    exp_total, target = lax.psum(
        (jnp.sum(jnp.exp(logits - global_max[None, :]), axis=0), local_target), ("ctx", "tp")
    )
    logprob = target - global_max - jnp.log(exp_total)
    own_logprob = lax.dynamic_slice_in_dim(logprob, my_slab * SCORED, SCORED, 0)
    per_token = jnp.sum(jnp.where(chosen, own_logprob[:, None], 0.0), axis=0)
    return (context, per_token)


def solution(mesh):
    placed = (
        P("ctx", "tp"),
        P("ctx", "tp"),
        P("ctx", "tp"),
        P("ctx", "tp"),
        P("ctx", None),
        P(),
        P(("ctx", "tp"), None),
        P(),
        P(),
        P(),
    )
    return jax.shard_map(
        body, mesh=mesh, in_specs=placed, out_specs=(P("ctx", "tp"), P("ctx")), check_vma=False
    )
```

profile of v0, /device:TPU:1, one launch (start us, length us, event | category | flops | bytes accessed | tf_op | source)
XLA Modules:
  0.0 779.0 jit_solution(8627079114680486918)
XLA Ops:
  7.2 1.6 pad_maximum_fusion
  8.9 0.7 copy.32
  9.8 0.6 fusion.40
  10.4 1.3 fusion.39
  12.9 0.8 dynamic-slice_bitcast_fusion
  14.0 0.8 broadcast_compare_fusion.1
  14.9 124.5 %all-gather.4.cloned.1.call-done = bf16[2,8192,128]{2,1,0:T(8,128)(2,1)} async-done(((bf16[2,128,128]{2,1,0:T(8,128)(2,1)}), bf16[2,8192,128]{2,1,0:T(8,128)(2,1)}) %all-gather.4.cloned.1.call-update) | async-done | bytes 4194320 | tf_op jit(solution)/shard_map/all_gather | solution.py:50
  139.5 49.9 %conditional.1 = (f32[128,1,8]{0,2,1:T(8,128)S(1)}, f32[128,1,8,128]{3,0,2,1:T(8,128)S(1)}) conditional(s32[]{:T(128)} %convert_element_type.32, (s32[128]{0:T(128)S(1)}, s32[32]{0:T(128)S(1)}, s32[128,32]{1,0:T(8,128)S(1)}, bf16[2,8192,128]{2,1,0:T(8,128)(2,1)}, bf16[128,1024]{1,0:T(8,128)(2,1)}) %tuple.16, () %tuple.17), branch_computations={%region_2.7_spmd, %region_7.8_spmd} | conditional | flops 4407946240 | bytes 114140848 | solution.py:80
  139.8 3.7 fusion.7
  143.6 14.9 %fusion = (f32[128,8]{0,1:T(8,128)S(1)}, f32[8192,128,8]{1,0,2:T(8,128)}) fusion(pred[128,8192]{0,1:T(8,128)(4,1)S(1)} %fusion.7, bf16[2,8192,128]{2,1,0:T(8,128)(2,1)} %get-tuple-element.16, bf16[128,1024]{1,0:T(8,128)(2,1)} %get-tuple-element.25), kind=kOutput, calls=%fused_computation.2 | convolution fusion | flops 2172648448 | bytes 36966400 | tf_op jit(solution)/shard_map/cond/branch_0_fun/qkgd,pkd->qkgp/dot_general | solution.py:64
  158.5 16.1 %fusion.13 = f32[128,1,8,128]{3,0,2,1:T(8,128)S(1)} fusion(bf16[2,8192,128]{2,1,0:T(8,128)(2,1)} %get-tuple-element.16, f32[8192,128,8]{1,0,2:T(8,128)} %get-tuple-element.31, f32[128,8]{0,1:T(8,128)S(1)} %broadcast_maximum_fusion, pred[128,8192]{0,1:T(8,128)(4,1)} %copy-done.1), kind=kOutput, calls=%fused_computation.15 | convolution fusion | flops 2189426688 | bytes 37228544 | tf_op jit(solution)/shard_map/cond/branch_0_fun/qkgp,pkd->qkgd/dot_general | solution.py:71
  174.6 14.8 %fusion.2 = f32[128,8]{0,1:T(8,128)S(1)} fusion(f32[8192,128,8]{1,0,2:T(8,128)} %get-tuple-element.31, f32[128,8]{0,1:T(8,128)S(1)} %broadcast_maximum_fusion, pred[128,8192]{0,1:T(8,128)(4,1)} %copy-done.1), kind=kLoop, calls=%fused_computation.4 | loop fusion | flops 41942016 | bytes 34611200 | tf_op jit(solution)/shard_map/cond/branch_0_fun/reduce_sum | solution.py:70
  190.0 118.9 %all-gather = bf16[64,4,1024]{2,1,0:T(4,128)(2,1)S(1)} all-gather(bf16[1,4,1024]{2,1,0:T(4,128)(2,1)S(1)} %fusion.30), channel_id=1, replica_groups=mesh['ctx'=64,'tp'=8] {'ctx'}, dimensions={0}, use_global_device_ids=true | all-gather | bytes 532480 | tf_op jit(solution)/shard_map/all_gather | solution.py:97
  308.9 0.9 reshape.178
  309.8 2.0 convolution_bitcast_fusion
  312.0 132.3 %all-reduce.3.cloned.1.call-done = f32[80,256]{1,0:T(8,128)} async-done(((f32[80,256]{1,0:T(8,128)}), f32[80,256]{1,0:T(8,128)}) %all-reduce.3.cloned.1.call-update) | async-done | bytes 81936 | tf_op jit(solution)/shard_map/psum | solution.py:101
  444.4 1.5 add_convert_fusion
  445.9 0.3 reduce_window_sum.25
  446.6 118.1 %all-gather.6.cloned.1.call-done = bf16[5120,256]{1,0:T(8,128)(2,1)} async-done(((bf16[80,256]{1,0:T(8,128)(2,1)}), bf16[5120,256]{1,0:T(8,128)(2,1)}) %all-gather.6.cloned.1.call-update) | async-done | bytes 2621456 | tf_op jit(solution)/shard_map/all_gather | solution.py:113
  564.7 2.4 fusion.23
  567.2 2.7 fusion.41
  569.9 102.4 %pmax.7 = f32[256]{0:T(256)S(1)} all-reduce(f32[256]{0:T(256)S(1)} %get-tuple-element.34), channel_id=1, replica_groups=mesh['ctx'=64,'tp'=8] {'ctx','tp'}, use_global_device_ids=true, to_apply=%region_16.17 | all-reduce | flops 256 | bytes 2048 | tf_op jit(solution)/shard_map/pmax | solution.py:125
  672.4 99.4 %all-reduce = (f32[256]{0:T(256)S(1)}, f32[256]{0:T(256)S(1)}) all-reduce(f32[256]{0:T(256)S(1)} %get-tuple-element.27, f32[256]{0:T(256)S(1)} %get-tuple-element.26), channel_id=1, replica_groups=mesh['ctx'=64,'tp'=8] {'ctx','tp'}, use_global_device_ids=true, to_apply=%region_18.19 | all-reduce | flops 512 | bytes 4096 | tf_op jit(solution)/shard_map/psum | solution.py:126
  771.9 0.6 select_reduce_fusion.1
  (44 shorter events, 2.5 us)
Async XLA Ops:
  7.2 560.0 %copy-start = (bf16[256,5120]{1,0:T(8,128)(2,1)S(1)}, bf16[256,5120]{1,0:T(8,128)(2,1)}, u32[]{:S(2)}) copy-start(bf16[256,5120]{1,0:T(8,128)(2,1)} %param.18) | copy-start | bytes 7864324
  7.2 132.3 %all-gather.4.cloned.1.call-start = ((), (), s32[]{:S(2)}) async-start(), calls=%async_computation | async-start | bytes 4259840 | tf_op jit(solution)/shard_map/all_gather | solution.py:50
  8.8 435.6 %all-reduce.3.cloned.1.call-start = ((), (), s32[]{:S(2)}) async-start(), calls=%async_computation.1 | async-start | bytes 163840 | tf_op jit(solution)/shard_map/psum | solution.py:101
  139.5 304.9 %copy-start.4 = (bf16[80,256]{1,0:T(8,128)(2,1)S(1)}, bf16[80,256]{1,0:T(8,128)(2,1)}, u32[]{:S(2)}) copy-start(bf16[80,256]{1,0:T(8,128)(2,1)} %param.16) | copy-start | bytes 122884
  139.5 306.5 %copy-start.3 = (s32[8192]{0:T(1024)S(1)}, s32[8192]{0:T(1024)}, u32[]{:S(2)}) copy-start(s32[8192]{0:T(1024)} %param.20) | copy-start | bytes 98308
  139.5 306.8 %copy-start.5 = (s32[8192]{0:T(1024)S(1)}, s32[8192]{0:T(1024)}, u32[]{:S(2)}) copy-start(s32[8192]{0:T(1024)} %param.19) | copy-start | bytes 98308
  139.5 427.7 %copy-start.6 = (f32[5120]{0:T(1024)S(1)}, f32[5120]{0:T(1024)}, u32[]{:S(2)}) copy-start(f32[5120]{0:T(1024)} %param.17) | copy-start | bytes 61444
  143.6 14.9 %copy-start.1 = (pred[128,8192]{0,1:T(8,128)(4,1)}, pred[128,8192]{0,1:T(8,128)(4,1)S(1)}, u32[]{:S(2)}) copy-start(pred[128,8192]{0,1:T(8,128)(4,1)S(1)} %fusion.7) | copy-start | bytes 3145732 | tf_op jit(solution)/shard_map/cond
  189.8 582.7 %copy-start.2 = (bf16[16,8,8,128]{3,1,2,0:T(8,128)(2,1)}, bf16[16,8,8,128]{3,1,2,0:T(8,128)(2,1)S(1)}, u32[]{:S(2)}) copy-start(bf16[16,8,8,128]{3,1,2,0:T(8,128)(2,1)S(1)} %copy.46) | copy-start | bytes 786436
  311.8 252.9 %all-gather.6.cloned.1.call-start = ((), (), s32[]{:S(2)}) async-start(), calls=%async_computation.2 | async-start | bytes 2662400 | tf_op jit(solution)/shard_map/all_gather | solution.py:113
Sparse Core Ops, SparseCore 0:
  10.8 128.6 all-gather.3
  311.9 132.3 all-reduce.2
  446.8 117.8 all-gather.5
where the time goes:
time: 780 us; the launch traced here: 779 us
  waiting for transfers between devices  375 us (48%)
  blocking collectives  321 us (41%)
  matrix products  35.8 us (5%)
  other arithmetic  28.4 us (4%)
  between operations  15.1 us (2%)
    psum x1, waiting for transfers between devices, body(): summed = lax.psum(partial_value, 'tp')  132 us
    all_gather x1, waiting for transfers between devices, body(): portion = lax.all_gather(key_value, 'ctx', axis=1, tiled=True)  125 us
    all_gather x1, blocking collectives, body(): lax.all_gather(scored, 'ctx', axis=0, tiled=True)  119 us
    all_gather x1, waiting for transfers between devices, body(): gathered = lax.all_gather(hidden, 'ctx', axis=0, tiled=True)  118 us
    pmax x1, blocking collectives, body(): global_max = lax.pmax(local_max, ('ctx', 'tp'))  102 us
    psum x1, blocking collectives, body(): lax.psum((jnp.sum(jnp.exp(logits - global_max[None, :]), axis=0), local_t...  99.4 us
    dot_general x1, matrix products, update(): jnp.einsum('qkgp,pkd->qkgd', weights.astype(jnp.bfloat16), value_grid, pr...  16.1 us
  transfers between devices with their start and end apart: 3, of which 3 were waited for; matrix products, arithmetic and copies ran while one was open for 1% of the time, Pallas kernels for 0%

commit v1 on v0

v1 whole, which is shorter than its diff:
```python
import functools
import math

import jax
import jax.numpy as jnp
import numpy as np
from jax import lax
from jax.experimental import pallas as pl
from jax.experimental.pallas import tpu as pltpu
from jax.sharding import Mesh
from jax.sharding import PartitionSpec as P

HEAD_DIM = 128
SCORED = 4
HEADS_DEV = 8
SLAB = 128
CHIPS = 32
BLOCK = 2 * SLAB + SCORED * HEADS_DEV
FEATS = 80
HALF = 40
D = 5120

masked_fill = -1e30
start_max = -5e29
norm_eps = 1e-06
LOG2E = 1.4426950408889634
SCALE2 = LOG2E / math.sqrt(HEAD_DIM)
NT = (((1,), (1,)), ((), ()))
TN = (((0,), (0,)), ((), ()))
SMEM = pl.BlockSpec(memory_space=pltpu.SMEM)
VMEM = pl.BlockSpec(memory_space=pltpu.VMEM)
PARAMS = pltpu.CompilerParams(vmem_limit_bytes=50 * 2**20)


def iota(shape, axis):
    return lax.broadcasted_iota(jnp.int32, shape, axis)


def pack_kernel(rank_ref, q_ref, k_ref, v_ref, out_ref, rows):
    chosen = (iota((8, SLAB), 0) == rank_ref[...]).astype(jnp.bfloat16)
    picked = jnp.dot(chosen, q_ref[...], preferred_element_type=jnp.float32)
    for h in range(HEADS_DEV):
        rows[pl.ds(h, SCORED, stride=HEADS_DEV), :] = picked[:SCORED, h * 128 : (h + 1) * 128]
    scored = rows[...].astype(jnp.bfloat16)
    for i in range(out_ref.shape[0]):
        out_ref[i, :SLAB, :] = k_ref[...]
        out_ref[i, SLAB : 2 * SLAB, :] = v_ref[...]
        out_ref[i, 2 * SLAB :, :] = scored


def weight_kernel(source_ref, gain_ref, w_ref, out_ref):
    width = 1280
    move = (iota((width, width), 0) == source_ref[...]).astype(jnp.bfloat16)
    for x in range(4):
        part = w_ref[:, x * width : (x + 1) * width].astype(jnp.float32)
        part = (part * gain_ref[:, x * width : (x + 1) * width]).astype(jnp.bfloat16)
        moved = jnp.dot(part, move, preferred_element_type=jnp.float32).astype(jnp.bfloat16)
        for c in range(2):
            out_ref[:, (c * 4 + x) * 640 : (c * 4 + x + 1) * 640] = moved[:, c * 640 : (c + 1) * 640]


def attend(own_ref, other_ref, key0, q, low, high, first, last):
    columns = q.shape[0]

    def step(j, carry):
        top, total, acc = carry
        k = jnp.concatenate((own_ref[j, :SLAB, :], other_ref[j, :SLAB, :]), axis=0)
        v = jnp.concatenate(
            (own_ref[j, SLAB : 2 * SLAB, :], other_ref[j, SLAB : 2 * SLAB, :]), axis=0
        )
        s = lax.dot_general(k, q, NT, preferred_element_type=jnp.float32) * SCALE2
        visible = (key0 >= low - j * 256) & (key0 <= high - j * 256)
        s = jnp.where(visible, s, masked_fill)
        new_top = jnp.maximum(top, jnp.max(s, axis=0, keepdims=True))
        p = jnp.exp2(s - new_top)
        keep = jnp.exp2(top - new_top)
        total = total * keep + jnp.sum(p, axis=0, keepdims=True)
        pv = lax.dot_general(v, p.astype(jnp.bfloat16), TN, preferred_element_type=jnp.float32)
        return new_top, total, acc * keep + pv

    start = (
        jnp.full((1, columns), start_max, jnp.float32),
        jnp.zeros((1, columns), jnp.float32),
        jnp.zeros((HEAD_DIM, columns), jnp.float32),
    )
    _, total, acc = lax.fori_loop(first, last + 1, step, start)
    return acc / total


def key_positions(core, columns):
    row = iota((2 * SLAB, columns), 0)
    return jnp.where(row < SLAB, row + core * SLAB, row - core * SLAB)


def scored_kernel(core_ref, first_ref, low_ref, high_ref, own_ref, other_ref, w_ref, out_ref, rows, scored):
    core = core_ref[0]
    key0 = key_positions(core, 256)
    for t in range(8):
        q = jnp.concatenate(
            (
                own_ref[4 * t : 4 * t + 4, 2 * SLAB :, :].reshape(128, HEAD_DIM),
                other_ref[4 * t : 4 * t + 4, 2 * SLAB :, :].reshape(128, HEAD_DIM),
            ),
            axis=0,
        )
        mixed = attend(
            own_ref, other_ref, key0, q, low_ref[t : t + 1, :], high_ref[t : t + 1, :], first_ref[t], 4 * t + 3
        )
        rows[...] = mixed.T
        for h in range(HEADS_DEV):
            part = rows[pl.ds(h, 32, stride=HEADS_DEV), :].astype(jnp.bfloat16)
            lanes = slice(h * 128, (h + 1) * 128)
            scored[pl.ds(pl.multiple_of(core * 128 + t * 16, 16), 16), lanes] = part[:16]
            scored[pl.ds(pl.multiple_of((1 - core) * 128 + t * 16, 16), 16), lanes] = part[16:]
    partial = lax.dot_general(w_ref[...], scored[...], NT, preferred_element_type=jnp.float32)
    for half in range(2):
        for feats in range(2):
            out_ref[half * 2 + feats] = partial[
                feats * HALF : (feats + 1) * HALF, half * 128 : (half + 1) * 128
            ]


def context_kernel(at_ref, low_ref, high_ref, own_ref, other_ref, q_ref, out_ref):
    key0 = key_positions(at_ref[0], 256)
    for pair in range(HEADS_DEV // 2):
        q = jnp.concatenate(
            [q_ref[:, h * 128 : (h + 1) * 128] for h in (2 * pair, 2 * pair + 1)], axis=0
        )
        mixed = attend(own_ref, other_ref, key0, q, low_ref[...], high_ref[...], at_ref[1], at_ref[2])
        for i in range(2):
            h = 2 * pair + i
            out_ref[:, h * 128 : (h + 1) * 128] = mixed[:, i * 128 : (i + 1) * 128].T.astype(jnp.bfloat16)


def add_kernel(parts_ref, residual_ref, out_ref):
    total = residual_ref[...]
    for i in range(parts_ref.shape[0]):
        total = total + parts_ref[i]
    total = total.astype(jnp.bfloat16)
    for i in range(out_ref.shape[0]):
        out_ref[i] = total


def hidden_kernel(parts_ref, out_ref):
    for z in range(8):
        total = parts_ref[z].astype(jnp.float32) + parts_ref[8 + z].astype(jnp.float32)
        out_ref[z] = total.astype(jnp.bfloat16)


def logits_kernel(at_ref, ids_ref, own_ref, other_ref, w_ref, out_ref):
    core, base = at_ref[0], at_ref[1]
    logits = []
    tops, targets = [], []
    for half in range(2):
        total = jnp.zeros((256, 128), jnp.float32)
        square = jnp.zeros((8, 128), jnp.float32)
        for ref, c in ((own_ref, core), (other_ref, 1 - core)):
            for x in range(4):
                part = ref[x, half]
                lanes = pl.ds(pl.multiple_of((c * 4 + x) * 640, 128), 640)
                total = total + jnp.dot(w_ref[:, lanes], part, preferred_element_type=jnp.float32)
                wide = part.astype(jnp.float32)
                square = square + jnp.sum((wide * wide).reshape(80, 8, 128), axis=0)
        mean = jnp.sum(square, axis=0, keepdims=True) * (1.0 / D)
        total = total * lax.rsqrt(mean + norm_eps)
        top = jnp.max(total, axis=0, keepdims=True)
        tops.append(top + jnp.log(jnp.sum(jnp.exp(total - top), axis=0, keepdims=True)))
        hit = iota((256, 128), 0) + base == ids_ref[half : half + 1, :]
        targets.append(jnp.sum(jnp.where(hit, total, 0.0), axis=0, keepdims=True))
    tile = jnp.concatenate(tops + targets + [jnp.zeros((4, 128), jnp.float32)], axis=0)
    for i in range(out_ref.shape[0]):
        out_ref[i] = tile


def merge(parts_ref):
    parts = parts_ref[...]
    top = jnp.max(parts, axis=0)
    lse = top + jnp.log(jnp.sum(jnp.exp(parts - top[None]), axis=0))
    return jnp.where(iota((8, 128), 0) < 2, lse, jnp.sum(parts, axis=0))


def merge_kernel(parts_ref, out_ref):
    tile = merge(parts_ref)
    for i in range(out_ref.shape[0]):
        out_ref[i] = tile


def final_kernel(at_ref, rank_ref, parts_ref, out_ref):
    core, chip = at_ref[0], at_ref[1]
    tile = merge(parts_ref)
    logprob = jnp.where(core == 0, tile[2:3] - tile[0:1], tile[3:4] - tile[1:2])
    lane = iota((1, 128), 1)
    result = jnp.zeros((1, 128), jnp.float32)
    for k in range(SCORED):
        value = jnp.sum(jnp.where(lane == chip * SCORED + k, logprob, 0.0), axis=1, keepdims=True)
        result = jnp.where(rank_ref[...] == k, value, result)
    out_ref[...] = result


def call(kernel, shape, dtype, specs, scratch=(), flops=0, size=0, name=None):
    return pl.pallas_call(
        kernel,
        out_shape=jax.ShapeDtypeStruct(shape, dtype),
        in_specs=specs,
        out_specs=VMEM,
        scratch_shapes=list(scratch),
        compiler_params=PARAMS,
        cost_estimate=pl.CostEstimate(flops=flops, bytes_accessed=size, transcendentals=0),
        name=name,
    )


def source_columns():
    c, yf, z, k = np.meshgrid(np.arange(2), np.arange(2), np.arange(8), np.arange(40), indexing="ij")
    return (((z * 2 + c) * 2 + yf) * 40 + k).reshape(1, 1280).astype(np.int32)


def body(
    queries,
    keys,
    values,
    out_weight,
    residual,
    norm_gain,
    head_weight,
    sampled_ids,
    loss_mask,
    doc_lengths,
):
    x, z, core = lax.axis_index("x"), lax.axis_index("z"), lax.axis_index("c")
    h, y = lax.axis_index("h"), lax.axis_index("y")
    chip = x * 8 + z
    slab = chip * 2 + core
    slabs = loss_mask.reshape(64, SLAB)
    upto = jnp.tril(jnp.ones((SLAB, SLAB), jnp.float32)).T
    rank = jnp.dot(slabs.astype(jnp.float32), upto, preferred_element_type=jnp.float32).astype(jnp.int32)
    rank = jnp.where(slabs == 1, rank - 1, -1)
    own_rank = lax.dynamic_slice_in_dim(rank, slab, 1, 0)
    packed = call(
        pack_kernel, (8, BLOCK, 128), jnp.bfloat16, [VMEM] * 4, [pltpu.VMEM((32, 128), jnp.float32)], name="pack"
    )(own_rank, queries, keys, values)
    along_z = lax.all_to_all(packed, "z", 0, 0)
    along_x = lax.all_to_all(jnp.broadcast_to(along_z[None], (4, 8, BLOCK, 128)), "x", 0, 0)
    own = along_x.reshape(CHIPS, BLOCK, 128)
    other = lax.ppermute(own, "c", [(0, 1), (1, 0)])

    bounds = jnp.cumsum(doc_lengths)
    position = jnp.arange(64 * SLAB, dtype=jnp.int32)
    begin = jnp.max(jnp.where(bounds[None, :] <= position[:, None], bounds[None, :], 0), axis=1)
    chosen = rank[:, None, :] == jnp.arange(SCORED, dtype=jnp.int32)[None, :, None]

    def pick(values_of):
        return jnp.sum(jnp.where(chosen, values_of.reshape(64, 1, SLAB), 0), axis=2)

    def columns(of_scored):
        pairs = of_scored.reshape(CHIPS, 2, SCORED)
        pairs = jnp.where(core == 0, pairs, pairs[:, ::-1])
        tiles = pairs.reshape(8, 4, 2, SCORED).transpose(0, 2, 1, 3)
        return jnp.repeat(tiles.reshape(8, 32), HEADS_DEV, axis=1)

    high = columns(pick(position))
    low = columns(pick(begin))
    ids = pick(sampled_ids).reshape(CHIPS, 2, SCORED).transpose(1, 0, 2).reshape(2, 128)
    first = jnp.min(low, axis=1) // 256
    core_at = core[None]

    source = jnp.asarray(source_columns())
    weight = call(weight_kernel, (256, D), jnp.bfloat16, [VMEM] * 3, flops=2 * 256 * D * 1280, name="weight")(
        source, norm_gain[None, :], head_weight
    )
    mine = residual.reshape(2, HALF, CHIPS, 2, SCORED).transpose(3, 0, 1, 2, 4).reshape(4, HALF, 128)
    mine = lax.dynamic_index_in_dim(mine, y, 0, keepdims=False).astype(jnp.float32)
    mine = jnp.where(h == 0, mine, 0.0)

    parts = call(
        scored_kernel,
        (4, HALF, 128),
        jnp.float32,
        [SMEM, SMEM] + [VMEM] * 5,
        [pltpu.VMEM((256, 128), jnp.float32), pltpu.VMEM((256, 1024), jnp.bfloat16)],
        name="scored",
    )(core_at, first, low, high, own, other, out_weight)

    own_begin = lax.dynamic_slice_in_dim(begin, slab * SLAB, SLAB, 0)
    own_position = slab * SLAB + jnp.arange(SLAB, dtype=jnp.int32)
    at = jnp.stack((core, own_begin[0] // 256, chip))
    context = call(
        context_kernel,
        (SLAB, 1024),
        jnp.bfloat16,
        [SMEM] + [VMEM] * 5,
        flops=4 * 1024 * 4224 * 128,
        size=6 * 2**20,
        name="context",
    )(at, jnp.tile(own_begin, 2)[None, :], jnp.tile(own_position, 2)[None, :], own, other, queries)

    parts = lax.all_to_all(parts, "y", 0, 0)
    sums = call(add_kernel, (16, HALF, 128), jnp.bfloat16, [VMEM] * 2, name="add")(parts, mine)
    sums = lax.all_to_all(sums, ("h", "z"), 0, 0)
    hidden = call(hidden_kernel, (8, HALF, 128), jnp.bfloat16, [VMEM], name="hidden")(sums)
    hidden = jnp.broadcast_to(hidden.reshape(1, 8 * HALF, 128), (16, 8 * HALF, 128))
    hidden = lax.all_to_all(hidden, ("x", "y"), 0, 0).reshape(4, 2, 640, 128)
    hidden_other = lax.ppermute(hidden, "c", [(0, 1), (1, 0)])
    base = ((slab * 2 + h) * 4 + y) * 256
    tiles = call(logits_kernel, (32, 8, 128), jnp.float32, [SMEM] + [VMEM] * 4, name="logits")(
        jnp.stack((core, base)), ids, hidden, hidden_other, weight
    )
    tiles = lax.all_to_all(tiles, ("x", "y", "c"), 0, 0)
    tiles = call(merge_kernel, (16, 8, 128), jnp.float32, [VMEM], name="merge")(tiles)
    tiles = lax.all_to_all(tiles, ("h", "z"), 0, 0)
    logprob = call(final_kernel, (1, 128), jnp.float32, [SMEM, VMEM, VMEM], name="final")(
        jnp.stack((core, chip)), own_rank, tiles
    )
    return context, logprob.reshape(128)


def solution(mesh):
    fine = Mesh(mesh.devices.reshape(4, 8, 2, 2, 4), ("x", "z", "c", "h", "y"))
    ctx, tp = ("x", "z", "c"), ("h", "y")
    placed = (
        P(ctx, tp),
        P(ctx, tp),
        P(ctx, tp),
        P(ctx, tp),
        P(ctx, None),
        P(),
        P(ctx + tp, None),
        P(),
        P(),
        P(),
    )
    return jax.shard_map(
        body, mesh=fine, in_specs=placed, out_specs=(P(ctx, tp), P(ctx)), check_vma=False
    )
```

time: 780 us -> 239 us (0.31)
  the two profiles are of different devices: /device:TPU:1 before, /device:TPU:132 now
where the time goes in v1:
time: 239 us; the launch traced here: 238 us
  blocking collectives  111 us (46%)
  Pallas kernels  81 us (34%)
  starting transfers between devices  23.8 us (10%)
  waiting for transfers between devices  12.6 us (5%)
  local copies, waits for them, and re-layouts  6.93 us (3%)
    all_to_all x1, blocking collectives, body(): along_z = lax.all_to_all(packed, 'z', 0, 0)  36.9 us
    pallas_call x1, Pallas kernels, body(): call(scored_kernel, (4, HALF, 128), jnp.float32, [SMEM, SMEM] + [VMEM] *...  35.9 us
    pallas_call x1, Pallas kernels, body(): call(context_kernel, (SLAB, 1024), jnp.bfloat16, [SMEM] + [VMEM] * 5, flo...  32.6 us
    all_to_all x1, blocking collectives, body(): lax.all_to_all(jnp.broadcast_to(along_z[None], (4, 8, BLOCK, 128)), 'x',...  30.7 us
    all_to_all x1, blocking collectives, body(): sums = lax.all_to_all(sums, ('h', 'z'), 0, 0)  22.1 us
    all_to_all x1, blocking collectives, body(): hidden = lax.all_to_all(hidden, ('x', 'y'), 0, 0).reshape(4, 2, 640, 128)  20.9 us
    all_to_all x1, starting transfers between devices, body(): tiles = lax.all_to_all(tiles, ('h', 'z'), 0, 0)  9.43 us
    all_to_all x1, starting transfers between devices, body(): tiles = lax.all_to_all(tiles, ('x', 'y', 'c'), 0, 0)  6.05 us
  transfers between devices with their start and end apart: 5, of which 3 were waited for; matrix products, arithmetic and copies ran while one was open for 2% of the time, Pallas kernels for 16%

profile of v1, /device:TPU:132, one launch (start us, length us, event | category | flops | bytes accessed | tf_op | source)
XLA Modules:
  0.0 238.3 jit_solution(16927682902543311232)
XLA Ops:
  0.6 1.0 fusion.2
  1.7 0.9 copy-done.1
  2.6 0.8 copy-done.4
  3.4 0.8 copy-done.5
  4.3 36.9 %all_to_all.35 = bf16[8,288,128]{2,1,0:T(8,128)(2,1)S(1)} all-to-all(bf16[8,288,128]{2,1,0:T(8,128)(2,1)S(1)} %pack.1), channel_id=1, replica_groups=mesh['x'=4,'z'=8,'c'=2,'h'=2,'y'=4] {'z'}, dimensions={0} | all-to-all | bytes 1179648 | tf_op jit(solution)/shard_map/all_to_all | solution.py:242
  41.2 0.3 broadcast_in_dim.82
  41.6 30.7 %all_to_all.36 = bf16[4,8,288,128]{3,2,1,0:T(8,128)(2,1)S(1)} all-to-all(bf16[4,8,288,128]{3,2,1,0:T(8,128)(2,1)S(1)} %broadcast_in_dim.82), channel_id=1, replica_groups=mesh['x'=4,'z'=8,'c'=2,'h'=2,'y'=4] {'x'}, dimensions={0} | all-to-all | bytes 4718592 | tf_op jit(solution)/shard_map/all_to_all | solution.py:243
  72.2 1.9 collective-permute-start
  77.4 1.4 collective-permute-done.other_ref
  78.8 35.9 %scored.1 = f32[4,40,128]{2,1,0:T(8,128)} custom-call(s32[1]{0:T(128)} %bitcast.core_ref, s32[8]{0:T(128)S(1)} %and_select_fusion.first_ref, s32[8,256]{1,0:T(8,128)S(1)} %reshape.122.low_ref, s32[8,256]{1,0:T(8,128)S(1)} %reshape.129.high_ref, bf16[32,288,128]{2,1,0:T(8,128)(2,1)S(1)} %bitcast.49, bf16[32,288,128]{2,1,0:T(8,128)(2,1)} %collective-permute-done.other_ref, ...), custom_call_target="tpu_custom_call" | custom-call | tf_op jit(solution)/shard_map/scored/pallas_call | solution.py:275
  114.7 4.5 %all-to-all-start.2 = ((f32[4,40,128]{2,1,0:T(8,128)}), f32[4,40,128]{2,1,0:T(8,128)S(1)}, u32[]{:S(2)}, u32[]{:S(2)}) async-start(f32[4,40,128]{2,1,0:T(8,128)} %scored.1), calls=%async_computation.2 | async-start | bytes 163840 | tf_op jit(solution)/shard_map/all_to_all | solution.py:297
  119.2 5.7 %all-to-all-done.2.parts_ref = f32[4,40,128]{2,1,0:T(8,128)S(1)} async-done(((f32[4,40,128]{2,1,0:T(8,128)}), f32[4,40,128]{2,1,0:T(8,128)S(1)}, u32[]{:S(2)}, u32[]{:S(2)}) %all-to-all-start.2) | async-done | bytes 81952 | tf_op jit(solution)/shard_map/all_to_all | solution.py:297
  124.9 22.1 %all_to_all.37.parts_ref = bf16[16,40,128]{2,1,0:T(8,128)(2,1)S(1)} all-to-all(bf16[16,40,128]{2,1,0:T(8,128)(2,1)S(1)} %add.66), channel_id=1, replica_groups=mesh['x'=4,'z'=8,'c'=2,'h'=2,'y'=4] {'h','z'}, dimensions={0} | all-to-all | bytes 327680 | tf_op jit(solution)/shard_map/all_to_all | solution.py:299
  147.4 20.9 %all_to_all.38 = bf16[16,320,128]{2,1,0:T(8,128)(2,1)} all-to-all(bf16[16,320,128]{2,1,0:T(8,128)(2,1)S(1)} %broadcast_in_dim.93), channel_id=1, replica_groups=mesh['x'=4,'z'=8,'c'=2,'h'=2,'y'=4] {'x','y'}, dimensions={0} | all-to-all | bytes 2621440 | tf_op jit(solution)/shard_map/all_to_all | solution.py:302
  168.3 1.9 collective-permute-start.1
  170.5 5.5 %weight.1.w_ref = bf16[256,5120]{1,0:T(8,128)(2,1)S(1)} custom-call(s32[1,1280]{1,0:T(1,128)S(1)} %copy-done.7, f32[1,5120]{1,0:T(1,128)S(1)} %bitcast.52, bf16[256,5120]{1,0:T(8,128)(2,1)} %w_ref.3), custom_call_target="tpu_custom_call" | custom-call | flops 3355443200 | tf_op jit(solution)/shard_map/weight/pallas_call | solution.py:268
  176.0 1.5 copy-done
  177.5 4.9 %logits.1 = f32[32,8,128]{2,1,0:T(8,128)} custom-call(s32[2]{0:T(128)S(1)} %pad_add_fusion.2.at_ref, s32[2,128]{1,0:T(2,128)S(1)} %reshape.118.ids_ref, bf16[4,2,640,128]{3,2,1,0:T(8,128)(2,1)} %bitcast.28.own_ref, bf16[4,2,640,128]{3,2,1,0:T(8,128)(2,1)} %collective-permute-done.1.other_ref, bf16[256,5120]{1,0:T(8,128)(2,1)} %copy-done), custom_call_target="tpu_custom_call" | custom-call | tf_op jit(solution)/shard_map/logits/pallas_call | solution.py:305
  182.4 6.1 %all-to-all-start.5 = ((f32[32,8,128]{2,1,0:T(8,128)}), f32[32,8,128]{2,1,0:T(8,128)S(1)}, u32[]{:S(2)}, u32[]{:S(2)}) async-start(f32[32,8,128]{2,1,0:T(8,128)} %logits.1), calls=%async_computation.5 | async-start | bytes 262144 | tf_op jit(solution)/shard_map/all_to_all | solution.py:308
  188.8 5.5 %all-to-all-done.5.parts_ref = f32[32,8,128]{2,1,0:T(8,128)S(1)} async-done(((f32[32,8,128]{2,1,0:T(8,128)}), f32[32,8,128]{2,1,0:T(8,128)S(1)}, u32[]{:S(2)}, u32[]{:S(2)}) %all-to-all-start.5) | async-done | bytes 131104 | tf_op jit(solution)/shard_map/all_to_all | solution.py:308
  194.3 0.7 merge.1
  195.0 9.4 %all-to-all-start.6 = ((f32[16,8,128]{2,1,0:T(8,128)}), f32[16,8,128]{2,1,0:T(8,128)S(1)}, u32[]{:S(2)}, u32[]{:S(2)}) async-start(f32[16,8,128]{2,1,0:T(8,128)} %merge.1), calls=%async_computation.6 | async-start | bytes 131072 | tf_op jit(solution)/shard_map/all_to_all | solution.py:310
  204.5 32.6 %context.1 = bf16[128,1024]{1,0:T(8,128)(2,1)} custom-call(s32[3]{0:T(128)S(1)} %pad_add_fusion.at_ref, s32[1,256]{1,0:T(1,128)S(1)} %bitcast.54, s32[1,256]{1,0:T(1,128)S(1)} %bitcast.53, bf16[32,288,128]{2,1,0:T(8,128)(2,1)S(1)} %bitcast.50, bf16[32,288,128]{2,1,0:T(8,128)(2,1)} %collective-permute-done.other_ref, bf16[128,1024]{1,0:T(8,128)(2,1)S(1)} %copy-done.2), custom_call_target="tpu_custom_call" | custom-call | flops 2214592512 | bytes 6291456 | tf_op jit(solution)/shard_map/context/pallas_call | solution.py:287
  237.1 1.2 final.1
  (64 shorter events, 4.2 us)
Async XLA Ops:
  1.6 1.0 copy-start.1
  2.6 0.8 copy-start.4
  3.4 0.8 copy-start.5
  41.5 32.6 %copy-start.10 = (s32[32]{0:T(128)S(1)}, s32[32]{0:T(128)}, u32[]{:S(2)}) copy-start(s32[32]{0:T(128)} %param.20) | copy-start | bytes 388
  41.5 33.2 %copy-start.9 = (s32[8192]{0:T(1024)S(1)}, s32[8192]{0:T(1024)}, u32[]{:S(2)}) copy-start(s32[8192]{0:T(1024)} %param.18) | copy-start | bytes 98308
  41.5 34.6 %copy-start.8 = (bf16[80,256]{1,0:T(8,128)(2,1)S(1)}, bf16[80,256]{1,0:T(8,128)(2,1)}, u32[]{:S(2)}) copy-start(bf16[80,256]{1,0:T(8,128)(2,1)} %param.15) | copy-start | bytes 122884
  41.6 37.2 %copy-start.3 = (bf16[80,1024]{1,0:T(8,128)(2,1)S(1)}, bf16[80,1024]{1,0:T(8,128)(2,1)}, u32[]{:S(2)}) copy-start(bf16[80,1024]{1,0:T(8,128)(2,1)} %w_ref.2) | copy-start | bytes 491524
  72.2 6.5 %collective-permute-start = (bf16[32,288,128]{2,1,0:T(8,128)(2,1)S(1)}, bf16[32,288,128]{2,1,0:T(8,128)(2,1)}, u32[]{:S(2)}, u32[]{:S(2)}) collective-permute-start(bf16[32,288,128]{2,1,0:T(8,128)(2,1)S(1)} %bitcast.48), channel_id=1, source_target_pairs={{0,8},{8,0},{1,9},{9,1},{2,10},{10,2},{3,11},{11,3},{4,12},{12,4},... | collective-permute-start | bytes 7077896 | tf_op jit(solution)/shard_map/ppermute | solution.py:245
  114.7 10.2 %all-to-all-start.2 = ((f32[4,40,128]{2,1,0:T(8,128)}), f32[4,40,128]{2,1,0:T(8,128)S(1)}, u32[]{:S(2)}, u32[]{:S(2)}) async-start(f32[4,40,128]{2,1,0:T(8,128)} %scored.1), calls=%async_computation.2 | async-start | bytes 163840 | tf_op jit(solution)/shard_map/all_to_all | solution.py:297
  124.9 45.6 %copy-start.6 = (f32[5120]{0:T(1024)S(1)}, f32[5120]{0:T(1024)}, u32[]{:S(2)}) copy-start(f32[5120]{0:T(1024)} %param.16) | copy-start | bytes 61444
  124.9 45.6 %copy-start.7 = (s32[1,1280]{1,0:T(1,128)S(1)}, s32[1,1280]{1,0:T(1,128)}, u32[]{:S(2)}) copy-start(s32[1,1280]{1,0:T(1,128)} %constant.83.clone.source_ref) | copy-start | bytes 15364
  168.3 9.2 %collective-permute-start.1 = (bf16[4,2,640,128]{3,2,1,0:T(8,128)(2,1)}, bf16[4,2,640,128]{3,2,1,0:T(8,128)(2,1)}, u32[]{:S(2)}, u32[]{:S(2)}) collective-permute-start(bf16[4,2,640,128]{3,2,1,0:T(8,128)(2,1)} %bitcast.28.own_ref), channel_id=1, source_target_pairs={{0,8},{8,0},{1,9},{9,1},{2,10},{10,2},{3,11},{11,3},{4,12},{12,4},... | collective-permute-start | bytes 3932168 | tf_op jit(solution)/shard_map/ppermute | solution.py:303
  176.0 1.5 copy-start
  177.5 27.0 %copy-start.2 = (bf16[128,1024]{1,0:T(8,128)(2,1)S(1)}, bf16[128,1024]{1,0:T(8,128)(2,1)}, u32[]{:S(2)}) copy-start(bf16[128,1024]{1,0:T(8,128)(2,1)} %q_ref.3) | copy-start | bytes 786436
  182.4 11.9 %all-to-all-start.5 = ((f32[32,8,128]{2,1,0:T(8,128)}), f32[32,8,128]{2,1,0:T(8,128)S(1)}, u32[]{:S(2)}, u32[]{:S(2)}) async-start(f32[32,8,128]{2,1,0:T(8,128)} %logits.1), calls=%async_computation.5 | async-start | bytes 262144 | tf_op jit(solution)/shard_map/all_to_all | solution.py:308
  195.0 42.2 %all-to-all-start.6 = ((f32[16,8,128]{2,1,0:T(8,128)}), f32[16,8,128]{2,1,0:T(8,128)S(1)}, u32[]{:S(2)}, u32[]{:S(2)}) async-start(f32[16,8,128]{2,1,0:T(8,128)} %merge.1), calls=%async_computation.6 | async-start | bytes 131072 | tf_op jit(solution)/shard_map/all_to_all | solution.py:310

commit v2 on v1

v2 whole, which is shorter than its diff:
```python
import functools
import math

import jax
import jax.numpy as jnp
import numpy as np
from jax import lax
from jax.experimental import pallas as pl
from jax.experimental.pallas import tpu as pltpu
from jax.sharding import Mesh
from jax.sharding import PartitionSpec as P

HEAD_DIM = 128
SCORED = 4
HEADS_DEV = 8
SLAB = 128
CHIPS = 32
BLOCK = 2 * SLAB + SCORED * HEADS_DEV
FEATS = 80
HALF = 40
D = 5120

masked_fill = -1e30
start_max = -5e29
norm_eps = 1e-06
LOG2E = 1.4426950408889634
SCALE2 = LOG2E / math.sqrt(HEAD_DIM)
NT = (((1,), (1,)), ((), ()))
TN = (((0,), (0,)), ((), ()))
SMEM = pl.BlockSpec(memory_space=pltpu.SMEM)
VMEM = pl.BlockSpec(memory_space=pltpu.VMEM)
ANY = pl.BlockSpec(memory_space=pl.ANY)
HBM = pl.BlockSpec(memory_space=pltpu.HBM)


def iota(shape, axis):
    return lax.broadcasted_iota(jnp.int32, shape, axis)


def send_copies(source, out_ref, sems):
    copies = [pltpu.make_async_copy(source, out_ref.at[i], sems.at[i]) for i in range(out_ref.shape[0])]
    for copy in copies:
        copy.start()
    for copy in copies:
        copy.wait()


def pack_kernel(at_ref, mask_ref, q_ref, k_ref, v_ref, out_ref, block, queries, rows, sems):
    copies = [
        pltpu.make_async_copy(k_ref, block.at[pl.ds(0, SLAB)], sems.at[0]),
        pltpu.make_async_copy(v_ref, block.at[pl.ds(SLAB, SLAB)], sems.at[1]),
        pltpu.make_async_copy(q_ref, queries, sems.at[2]),
    ]
    for copy in copies:
        copy.start()
    mask = mask_ref[pl.ds(at_ref[0], 1), :]
    upto = (iota((SLAB, SLAB), 0) <= iota((SLAB, SLAB), 1)).astype(jnp.bfloat16)
    ones = jnp.broadcast_to(mask.astype(jnp.float32), (8, SLAB)).astype(jnp.bfloat16)
    rank = jnp.dot(ones, upto, preferred_element_type=jnp.float32).astype(jnp.int32) - 1
    chosen = jnp.where((iota((8, SLAB), 0) == rank) & (mask == 1), 1.0, 0.0).astype(jnp.bfloat16)
    for copy in copies:
        copy.wait()
    picked = jnp.dot(chosen, queries[...], preferred_element_type=jnp.float32)
    for h in range(HEADS_DEV):
        rows[pl.ds(h, SCORED, stride=HEADS_DEV), :] = picked[:SCORED, h * 128 : (h + 1) * 128]
    block[2 * SLAB :, :] = rows[...].astype(jnp.bfloat16)
    send_copies(block, out_ref, sems)


def spread_kernel(*refs):
    send_copies(refs[0], refs[-2], refs[-1])


def weight_kernel(source_ref, gain_ref, w_ref, out_ref):
    width = 1280
    move = (iota((width, width), 0) == source_ref[...]).astype(jnp.bfloat16)
    for x in range(4):
        part = w_ref[:, x * width : (x + 1) * width].astype(jnp.float32)
        part = (part * gain_ref[:, x * width : (x + 1) * width]).astype(jnp.bfloat16)
        moved = jnp.dot(part, move, preferred_element_type=jnp.float32).astype(jnp.bfloat16)
        for c in range(2):
            out_ref[:, (c * 4 + x) * 640 : (c * 4 + x + 1) * 640] = moved[:, c * 640 : (c + 1) * 640]


def attend(own_ref, other_ref, core, q, low, high, bounds, group):
    columns = q.shape[0]
    half = group * SLAB
    row = iota((2 * half, 1), 0)
    inside = jnp.where(row < half, row, row - half)
    key0 = (inside // SLAB) * (2 * SLAB) + inside % SLAB + jnp.where(row < half, core, 1 - core) * SLAB

    def step(edge, g, carry):
        top, total, acc = carry
        chips = pl.ds(pl.multiple_of(g * group, group), group)

        def rows(at):
            parts = [ref[chips, at : at + SLAB, :].reshape(half, HEAD_DIM) for ref in (own_ref, other_ref)]
            return jnp.concatenate(parts, axis=0)

        s = lax.dot_general(rows(0), q, NT, preferred_element_type=jnp.float32) * SCALE2
        if edge:
            offset = g * (2 * half)
            s = jnp.where((key0 >= low - offset) & (key0 <= high - offset), s, masked_fill)
        new_top = jnp.maximum(top, jnp.max(s, axis=0, keepdims=True))
        p = jnp.exp2(s - new_top)
        keep = jnp.exp2(top - new_top)
        total = total * keep + jnp.sum(p, axis=0, keepdims=True)
        pv = lax.dot_general(rows(SLAB), p.astype(jnp.bfloat16), TN, preferred_element_type=jnp.float32)
        return new_top, total, acc * keep + pv

    carry = (
        jnp.full((1, columns), start_max, jnp.float32),
        jnp.zeros((1, columns), jnp.float32),
        jnp.zeros((HEAD_DIM, columns), jnp.float32),
    )
    for i, edge in enumerate((True, False, True)):
        carry = lax.fori_loop(bounds[i], bounds[i + 1], functools.partial(step, edge), carry)
    _, total, acc = carry
    return acc / total


def group_bounds(first, low, high, last_chip, group):
    size = group * 2 * SLAB
    begin, end = first // size, last_chip // group + 1
    whole = jnp.clip((low + size - 1) // size, begin, end)
    return begin, whole, jnp.clip((high + 1) // size, whole, end), end


def scored_kernel(core_ref, span_ref, low_ref, high_ref, own_ref, other_ref, w_ref, out_ref, rows, scored):
    core = core_ref[0]
    for t in range(8):
        q = jnp.concatenate(
            (
                own_ref[4 * t : 4 * t + 4, 2 * SLAB :, :].reshape(128, HEAD_DIM),
                other_ref[4 * t : 4 * t + 4, 2 * SLAB :, :].reshape(128, HEAD_DIM),
            ),
            axis=0,
        )
        bounds = group_bounds(span_ref[0, t], span_ref[1, t], span_ref[2, t], 4 * t + 3, 4)
        mixed = attend(own_ref, other_ref, core, q, low_ref[t : t + 1, :], high_ref[t : t + 1, :], bounds, 4)
        rows[...] = mixed.T
        for h in range(HEADS_DEV):
            part = rows[pl.ds(h, 32, stride=HEADS_DEV), :].astype(jnp.bfloat16)
            lanes = slice(h * 128, (h + 1) * 128)
            scored[pl.ds(pl.multiple_of(core * 128 + t * 16, 16), 16), lanes] = part[:16]
            scored[pl.ds(pl.multiple_of((1 - core) * 128 + t * 16, 16), 16), lanes] = part[16:]
    partial = lax.dot_general(w_ref[...], scored[...], NT, preferred_element_type=jnp.float32)
    for half in range(2):
        for feats in range(2):
            out_ref[half * 2 + feats] = partial[
                feats * HALF : (feats + 1) * HALF, half * 128 : (half + 1) * 128
            ]


def context_kernel(start_head, at_ref, low_ref, high_ref, own_ref, other_ref, q_ref, *refs):
    out_ref = refs[-1]
    heads = range(start_head, start_head + 4)
    q = jnp.concatenate([q_ref[:, h * 128 : (h + 1) * 128] for h in heads], axis=0)
    low, high = jnp.tile(low_ref[...], (1, 4)), jnp.tile(high_ref[...], (1, 4))
    bounds = group_bounds(at_ref[1], at_ref[2], at_ref[3] * 256, at_ref[3], 4)
    mixed = attend(own_ref, other_ref, at_ref[0], q, low, high, bounds, 4)
    for i in range(4):
        out_ref[:, i * 128 : (i + 1) * 128] = mixed[:, i * 128 : (i + 1) * 128].T.astype(jnp.bfloat16)


def add_kernel(parts_ref, residual_ref, out_ref, block, sems):
    total = residual_ref[...]
    for i in range(parts_ref.shape[0]):
        total = total + parts_ref[i]
    block[...] = total.astype(jnp.bfloat16)
    send_copies(block, out_ref, sems)


def hidden_kernel(parts_ref, dep_ref, out_ref, block, sems):
    total = parts_ref[:8].astype(jnp.float32) + parts_ref[8:].astype(jnp.float32)
    block[...] = total.reshape(8 * HALF, 128).astype(jnp.bfloat16)
    send_copies(block, out_ref, sems)


def add_logits(core, hidden_ref, w_ref, half):
    total = jnp.zeros((256, 128), jnp.float32)
    square = jnp.zeros((8, 128), jnp.float32)
    for x in range(4):
        part = hidden_ref[x, half]
        lanes = pl.ds(pl.multiple_of((core * 4 + x) * 640, 128), 640)
        total = total + jnp.dot(w_ref[:, lanes], part, preferred_element_type=jnp.float32)
        wide = part.astype(jnp.float32)
        square = square + jnp.sum((wide * wide).reshape(80, 8, 128), axis=0)
    return total, square


def own_logits_kernel(at_ref, own_ref, w_ref, out_ref, square_ref):
    for half in range(2):
        out_ref[half], square_ref[half] = add_logits(at_ref[0], own_ref, w_ref, half)


def logits_kernel(at_ref, ids_ref, sum_ref, square_ref, other_ref, w_ref, dep_ref, out_ref):
    core, base = at_ref[0], at_ref[1]
    tops, targets = [], []
    for half in range(2):
        total, square = add_logits(1 - core, other_ref, w_ref, half)
        total, square = total + sum_ref[half], square + square_ref[half]
        mean = jnp.sum(square, axis=0, keepdims=True) * (1.0 / D)
        total = total * lax.rsqrt(mean + norm_eps)
        top = jnp.max(total, axis=0, keepdims=True)
        tops.append(top + jnp.log(jnp.sum(jnp.exp(total - top), axis=0, keepdims=True)))
        hit = iota((256, 128), 0) + base == ids_ref[half : half + 1, :]
        targets.append(jnp.sum(jnp.where(hit, total, 0.0), axis=0, keepdims=True))
    tile = jnp.concatenate(tops + targets + [jnp.zeros((4, 128), jnp.float32)], axis=0)
    for i in range(out_ref.shape[0]):
        out_ref[i] = tile


def merge(parts_ref):
    parts = parts_ref[...]
    top = jnp.max(parts, axis=0)
    lse = top + jnp.log(jnp.sum(jnp.exp(parts - top[None]), axis=0))
    return jnp.where(iota((8, 128), 0) < 2, lse, jnp.sum(parts, axis=0))


def merge_kernel(parts_ref, out_ref):
    tile = merge(parts_ref)
    for i in range(out_ref.shape[0]):
        out_ref[i] = tile


def final_kernel(at_ref, rank_ref, parts_ref, out_ref):
    core, chip = at_ref[0], at_ref[1]
    tile = merge(parts_ref)
    logprob = jnp.where(core == 0, tile[2:3] - tile[0:1], tile[3:4] - tile[1:2])
    lane = iota((1, 128), 1)
    result = jnp.zeros((1, 128), jnp.float32)
    for k in range(SCORED):
        value = jnp.sum(jnp.where(lane == chip * SCORED + k, logprob, 0.0), axis=1, keepdims=True)
        result = jnp.where(rank_ref[...] == k, value, result)
    out_ref[...] = result


def call(kernel, shape, dtype, specs, scratch=(), flops=0, size=0, name=None, out=VMEM, more=None, vmem=16):
    shapes = jax.ShapeDtypeStruct(shape, dtype)
    return pl.pallas_call(
        kernel,
        out_shape=shapes if more is None else (shapes, more),
        in_specs=specs,
        out_specs=out if more is None else (out, out),
        scratch_shapes=list(scratch),
        compiler_params=pltpu.CompilerParams(vmem_limit_bytes=vmem * 2**20),
        cost_estimate=pl.CostEstimate(flops=flops, bytes_accessed=size, transcendentals=0),
        name=name,
    )


def source_columns():
    c, yf, z, k = np.meshgrid(np.arange(2), np.arange(2), np.arange(8), np.arange(40), indexing="ij")
    return (((z * 2 + c) * 2 + yf) * 40 + k).reshape(1, 1280).astype(np.int32)


def body(
    queries,
    keys,
    values,
    out_weight,
    residual,
    norm_gain,
    head_weight,
    sampled_ids,
    loss_mask,
    doc_lengths,
):
    x, z, core = lax.axis_index("x"), lax.axis_index("z"), lax.axis_index("c")
    h, y = lax.axis_index("h"), lax.axis_index("y")
    chip = x * 8 + z
    slab = chip * 2 + core
    slabs = loss_mask.reshape(64, SLAB)
    upto = jnp.tril(jnp.ones((SLAB, SLAB), jnp.float32)).T
    rank = jnp.dot(slabs.astype(jnp.float32), upto, preferred_element_type=jnp.float32).astype(jnp.int32)
    rank = jnp.where(slabs == 1, rank - 1, -1)
    own_rank = lax.dynamic_slice_in_dim(rank, slab, 1, 0)
    packed = call(
        pack_kernel,
        (8, BLOCK, 128),
        jnp.bfloat16,
        [SMEM, VMEM, ANY, ANY, ANY],
        [
            pltpu.VMEM((BLOCK, 128), jnp.bfloat16),
            pltpu.VMEM((SLAB, 1024), jnp.bfloat16),
            pltpu.VMEM((32, 128), jnp.float32),
            pltpu.SemaphoreType.DMA((8,)),
        ],
        name="pack",
        out=HBM,
    )(slab[None], slabs, queries, keys, values)
    along_z = lax.all_to_all(packed, "z", 0, 0)

    bounds = jnp.cumsum(doc_lengths)
    position = jnp.arange(64 * SLAB, dtype=jnp.int32)
    begin = jnp.max(jnp.where(bounds[None, :] <= position[:, None], bounds[None, :], 0), axis=1)
    chosen = rank[:, None, :] == jnp.arange(SCORED, dtype=jnp.int32)[None, :, None]

    def pick(values_of):
        return jnp.sum(jnp.where(chosen, values_of.reshape(64, 1, SLAB), 0), axis=2)

    def columns(of_scored):
        pairs = of_scored.reshape(CHIPS, 2, SCORED)
        pairs = jnp.where(core == 0, pairs, pairs[:, ::-1])
        tiles = pairs.reshape(8, 4, 2, SCORED).transpose(0, 2, 1, 3)
        return jnp.repeat(tiles.reshape(8, 32), HEADS_DEV, axis=1)

    high = columns(pick(position))
    low = columns(pick(begin))
    ids = pick(sampled_ids).reshape(CHIPS, 2, SCORED).transpose(1, 0, 2).reshape(2, 128)
    span = jnp.stack((jnp.min(low, axis=1), jnp.max(low, axis=1), jnp.min(high, axis=1)))
    core_at = core[None]

    source = jnp.asarray(source_columns())
    weight = call(weight_kernel, (256, D), jnp.bfloat16, [VMEM] * 3, flops=2 * 256 * D * 1280, name="weight", vmem=28)(
        source, norm_gain[None, :], head_weight
    )
    mine = residual.reshape(2, HALF, CHIPS, 2, SCORED).transpose(3, 0, 1, 2, 4).reshape(4, HALF, 128)
    mine = lax.dynamic_index_in_dim(mine, y, 0, keepdims=False).astype(jnp.float32)
    mine = jnp.where(h == 0, mine, 0.0)

    own_begin = lax.dynamic_slice_in_dim(begin, slab * SLAB, SLAB, 0)
    own_position = slab * SLAB + jnp.arange(SLAB, dtype=jnp.int32)
    at = jnp.stack((core, own_begin[0], own_begin[SLAB - 1], chip))
    base = ((slab * 2 + h) * 4 + y) * 256

    early = (weight, mine, low, high, span, ids, own_begin)
    spread = call(
        spread_kernel,
        (4, 8, BLOCK, 128),
        jnp.bfloat16,
        [VMEM] + [ANY] * len(early),
        [pltpu.SemaphoreType.DMA((4,))],
        name="spread",
        out=HBM,
    )(along_z, *early)
    own = lax.all_to_all(spread, "x", 0, 0).reshape(CHIPS, BLOCK, 128)
    other = lax.ppermute(own, "c", [(0, 1), (1, 0)])
    parts = call(
        scored_kernel,
        (4, HALF, 128),
        jnp.float32,
        [SMEM, SMEM] + [VMEM] * 5,
        [pltpu.VMEM((256, 128), jnp.float32), pltpu.VMEM((256, 1024), jnp.bfloat16)],
        name="scored",
        vmem=28,
    )(core_at, span, low, high, own, other, out_weight)

    def context_of(start_head, after):
        return call(
            functools.partial(context_kernel, start_head),
            (SLAB, 512),
            jnp.bfloat16,
            [SMEM] + [VMEM] * 5 + [ANY],
            flops=4 * 1024 * 4224 * 128,
            size=6 * 2**20,
            name="context",
            vmem=28,
        )(at, own_begin[None, :], own_position[None, :], own, other, queries, after)

    parts = lax.all_to_all(parts, "y", 0, 0)
    block = pltpu.VMEM((HALF, 128), jnp.bfloat16)
    sums = call(
        add_kernel,
        (16, HALF, 128),
        jnp.bfloat16,
        [VMEM] * 2,
        [block, pltpu.SemaphoreType.DMA((16,))],
        name="add",
        out=HBM,
    )(parts, mine)
    context_a = context_of(0, sums)
    sums = lax.all_to_all(sums, ("h", "z"), 0, 0)
    block = pltpu.VMEM((8 * HALF, 128), jnp.bfloat16)
    hidden = call(
        hidden_kernel,
        (16, 8 * HALF, 128),
        jnp.bfloat16,
        [VMEM, ANY],
        [block, pltpu.SemaphoreType.DMA((16,))],
        name="hidden",
        out=HBM,
    )(sums, context_a)
    context_b = context_of(4, hidden)
    hidden = lax.all_to_all(hidden, ("x", "y"), 0, 0).reshape(4, 2, 640, 128)
    hidden, context_b = lax.optimization_barrier((hidden, context_b))
    hidden_other = lax.ppermute(hidden, "c", [(0, 1), (1, 0)])
    at_logits = jnp.stack((core, base))
    shares, squares = call(
        own_logits_kernel,
        (2, 256, 128),
        jnp.float32,
        [SMEM] + [VMEM] * 2,
        name="own_logits",
        more=jax.ShapeDtypeStruct((2, 8, 128), jnp.float32),
    )(at_logits, hidden, weight)
    tiles = call(logits_kernel, (32, 8, 128), jnp.float32, [SMEM] + [VMEM] * 5 + [ANY], name="logits")(
        at_logits, ids, shares, squares, hidden_other, weight, context_b
    )
    context = jnp.concatenate((context_a, context_b), axis=1)
    tiles = lax.all_to_all(tiles, ("x", "y", "c"), 0, 0)
    tiles = call(merge_kernel, (16, 8, 128), jnp.float32, [VMEM], name="merge")(tiles)
    tiles = lax.all_to_all(tiles, ("h", "z"), 0, 0)
    logprob = call(final_kernel, (1, 128), jnp.float32, [SMEM, VMEM, VMEM], name="final")(
        jnp.stack((core, chip)), own_rank, tiles
    )
    return context, logprob.reshape(128)


def solution(mesh):
    fine = Mesh(mesh.devices.reshape(4, 8, 2, 2, 4), ("x", "z", "c", "h", "y"))
    ctx, tp = ("x", "z", "c"), ("h", "y")
    placed = (
        P(ctx, tp),
        P(ctx, tp),
        P(ctx, tp),
        P(ctx, tp),
        P(ctx, None),
        P(),
        P(ctx + tp, None),
        P(),
        P(),
        P(),
    )
    return jax.shard_map(
        body, mesh=fine, in_specs=placed, out_specs=(P(ctx, tp), P(ctx)), check_vma=False
    )
```

time: 239 us -> 206 us (0.86)
  the two profiles are of different devices: /device:TPU:132 before, /device:TPU:1 now
where the time goes in v2:
time: 206 us; the launch traced here: 205 us
  starting transfers between devices  63.1 us (31%)
  blocking collectives  42.5 us (21%)
  waiting for transfers between devices  39.6 us (19%)
  Pallas kernels  36.5 us (18%)
  local copies, waits for them, and re-layouts  17.7 us (9%)
  other arithmetic  3.92 us (2%)
    all_to_all x1, blocking collectives, body(): own = lax.all_to_all(spread, 'x', 0, 0).reshape(CHIPS, BLOCK, 128)  23 us
    pallas_call x1, Pallas kernels, body(): call(scored_kernel, (4, HALF, 128), jnp.float32, [SMEM, SMEM] + [VMEM] *...  17.9 us
    unnamed x40, local copies, waits for them, and re-layouts  14.3 us
    all_to_all x1, starting transfers between devices, body(): sums = lax.all_to_all(sums, ('h', 'z'), 0, 0)  13.5 us
    all_to_all x1, starting transfers between devices, body(): along_z = lax.all_to_all(packed, 'z', 0, 0)  13.1 us
    ppermute x1, starting transfers between devices, body(): other = lax.ppermute(own, 'c', [(0, 1), (1, 0)])  12.9 us
    all_to_all x1, waiting for transfers between devices, body(): along_z = lax.all_to_all(packed, 'z', 0, 0)  11.5 us
    all_to_all x1, blocking collectives, body(): tiles = lax.all_to_all(tiles, ('x', 'y', 'c'), 0, 0)  10.9 us
  transfers between devices with their start and end apart: 6, of which 6 were waited for; matrix products, arithmetic and copies ran while one was open for 4% of the time, Pallas kernels for 5%

profile of v2, /device:TPU:1, one launch (start us, length us, event | category | flops | bytes accessed | tf_op | source)
XLA Modules:
  0.0 205.2 jit_solution(18151119988500631470)
XLA Ops:
  5.2 13.1 %all-to-all-start = ((bf16[8,288,128]{2,1,0:T(8,128)(2,1)}), bf16[8,288,128]{2,1,0:T(8,128)(2,1)S(1)}, u32[]{:S(2)}, u32[]{:S(2)}) async-start(bf16[8,288,128]{2,1,0:T(8,128)(2,1)} %pack.1), calls=%async_computation | async-start | bytes 1179648 | tf_op jit(solution)/shard_map/all_to_all | solution.py:293
  23.9 1.7 copy-done.14
  25.7 3.7 %weight.1.refs_1_.w_ref = bf16[256,5120]{1,0:T(8,128)(2,1)S(1)} custom-call(s32[1,1280]{1,0:T(1,128)S(1)} %copy-done.16, f32[1,5120]{1,0:T(1,128)S(1)} %bitcast.53, bf16[256,5120]{1,0:T(8,128)(2,1)S(1)} %copy-done.14), custom_call_target="tpu_custom_call" | custom-call | flops 3355443200 | tf_op jit(solution)/shard_map/weight/pallas_call | solution.py:316
  29.4 11.5 %all-to-all-done.refs_0_ = bf16[8,288,128]{2,1,0:T(8,128)(2,1)S(1)} async-done(((bf16[8,288,128]{2,1,0:T(8,128)(2,1)}), bf16[8,288,128]{2,1,0:T(8,128)(2,1)S(1)}, u32[]{:S(2)}, u32[]{:S(2)}) %all-to-all-start) | async-done | bytes 589856 | tf_op jit(solution)/shard_map/all_to_all | solution.py:293
  41.5 23.0 %all_to_all.35 = bf16[4,8,288,128]{3,2,1,0:T(8,128)(2,1)S(1)} all-to-all(bf16[4,8,288,128]{3,2,1,0:T(8,128)(2,1)S(1)} %spread.1), channel_id=1, replica_groups=mesh['x'=4,'z'=8,'c'=2,'h'=2,'y'=4] {'x'}, dimensions={0} | all-to-all | bytes 4718592 | tf_op jit(solution)/shard_map/all_to_all | solution.py:338
  64.4 12.9 %collective-permute-start = (bf16[32,288,128]{2,1,0:T(8,128)(2,1)S(1)}, bf16[32,288,128]{2,1,0:T(8,128)(2,1)S(1)}, u32[]{:S(2)}, u32[]{:S(2)}) collective-permute-start(bf16[32,288,128]{2,1,0:T(8,128)(2,1)S(1)} %bitcast.48), channel_id=1, source_target_pairs={{0,8},{8,0},{1,9},{9,1},{2,10},{10,2},{3,11},{11,3},{4,12},{12,4},... | collective-permute-start | bytes 7077896 | tf_op jit(solution)/shard_map/ppermute | solution.py:339
  77.4 4.1 %collective-permute-done.other_ref = bf16[32,288,128]{2,1,0:T(8,128)(2,1)S(1)} collective-permute-done((bf16[32,288,128]{2,1,0:T(8,128)(2,1)S(1)}, bf16[32,288,128]{2,1,0:T(8,128)(2,1)S(1)}, u32[]{:S(2)}, u32[]{:S(2)}) %collective-permute-start) | collective-permute-done | bytes 2359328 | tf_op jit(solution)/shard_map/ppermute | solution.py:339
  81.5 17.9 %scored.1 = f32[4,40,128]{2,1,0:T(8,128)S(1)} custom-call(s32[1]{0:T(128)} %bitcast.core_ref, s32[3,8]{1,0:T(4,128)S(1)} %pad_add_fusion.refs_5_.span_ref, s32[8,256]{1,0:T(8,128)S(1)} %reshape.120.refs_3_.low_ref, s32[8,256]{1,0:T(8,128)S(1)} %reshape.127.refs_4_.high_ref, bf16[32,288,128]{2,1,0:T(8,128)(2,1)S(1)} %bitcast.49, ...), custom_call_target="tpu_custom_call" | custom-call | tf_op jit(solution)/shard_map/scored/pallas_call | solution.py:340
  99.4 8.6 %all_to_all.36.parts_ref = f32[4,40,128]{2,1,0:T(8,128)S(1)} all-to-all(f32[4,40,128]{2,1,0:T(8,128)S(1)} %scored.1), channel_id=1, replica_groups=mesh['x'=4,'z'=8,'c'=2,'h'=2,'y'=4] {'y'}, dimensions={0} | all-to-all | bytes 163840 | tf_op jit(solution)/shard_map/all_to_all | solution.py:362
  108.8 13.5 %all-to-all-start.3 = ((bf16[16,40,128]{2,1,0:T(8,128)(2,1)}), bf16[16,40,128]{2,1,0:T(8,128)(2,1)S(1)}, u32[]{:S(2)}, u32[]{:S(2)}) async-start(bf16[16,40,128]{2,1,0:T(8,128)(2,1)} %add.73.refs_0_), calls=%async_computation.3 | async-start | bytes 327680 | tf_op jit(solution)/shard_map/all_to_all | solution.py:374
  124.6 1.7 copy-done.1
  126.2 1.7 copy-done.6
  127.9 2.2 %context.2.dep_ref = bf16[128,512]{1,0:T(8,128)(2,1)S(1)} custom-call(s32[4]{0:T(128)S(1)} %pad_add_fusion.1.at_ref, s32[1,128]{1,0:T(1,128)S(1)} %dynamic-slice_bitcast_fusion.low_ref, s32[1,128]{1,0:T(1,128)S(1)} %iota_add_fusion.high_ref, bf16[32,288,128]{2,1,0:T(8,128)(2,1)S(1)} %bitcast.50, bf16[32,288,128]{2,1,0:T(8,128)(2,1)S(1)} %copy-done.6, ...), custom_call_target="tpu_custom_call" | custom-call | flops 2214592512 | bytes 6291456 | tf_op jit(solution)/shard_map/context/pallas_call | solution.py:351
  130.1 4.5 %all-to-all-done.3.parts_ref = bf16[16,40,128]{2,1,0:T(8,128)(2,1)S(1)} async-done(((bf16[16,40,128]{2,1,0:T(8,128)(2,1)}), bf16[16,40,128]{2,1,0:T(8,128)(2,1)S(1)}, u32[]{:S(2)}, u32[]{:S(2)}) %all-to-all-start.3) | async-done | bytes 163872 | tf_op jit(solution)/shard_map/all_to_all | solution.py:374
  134.5 1.9 hidden.1.refs_0_
  137.5 4.4 %all-to-all-start.4 = ((bf16[16,320,128]{2,1,0:T(8,128)(2,1)}), bf16[16,320,128]{2,1,0:T(8,128)(2,1)}, u32[]{:S(2)}, u32[]{:S(2)}) async-start(bf16[16,320,128]{2,1,0:T(8,128)(2,1)} %copy-done.3), calls=%async_computation.4 | async-start | bytes 2621440 | tf_op jit(solution)/shard_map/all_to_all | solution.py:386
  146.5 2.0 context.3.dep_ref
  148.5 8.0 %all-to-all-done.4 = bf16[16,320,128]{2,1,0:T(8,128)(2,1)} async-done(((bf16[16,320,128]{2,1,0:T(8,128)(2,1)}), bf16[16,320,128]{2,1,0:T(8,128)(2,1)}, u32[]{:S(2)}, u32[]{:S(2)}) %all-to-all-start.4) | async-done | bytes 1310752 | tf_op jit(solution)/shard_map/all_to_all | solution.py:386
  156.5 8.9 %collective-permute-start.1 = (bf16[4,2,640,128]{3,2,1,0:T(8,128)(2,1)}, bf16[4,2,640,128]{3,2,1,0:T(8,128)(2,1)}, u32[]{:S(2)}, u32[]{:S(2)}) collective-permute-start(bf16[4,2,640,128]{3,2,1,0:T(8,128)(2,1)} %bitcast.27.own_ref), channel_id=1, source_target_pairs={{0,8},{8,0},{1,9},{9,1},{2,10},{10,2},{3,11},{11,3},{4,12},{12,4},... | collective-permute-start | bytes 3932168 | tf_op jit(solution)/shard_map/ppermute | solution.py:388
  165.5 2.2 %own_logits.1 = (f32[2,256,128]{2,1,0:T(8,128)S(1)}, f32[2,8,128]{2,1,0:T(8,128)S(1)}) custom-call(s32[2]{0:T(128)S(1)} %pad_add_fusion.3.at_ref, bf16[4,2,640,128]{3,2,1,0:T(8,128)(2,1)} %bitcast.27.own_ref, bf16[256,5120]{1,0:T(8,128)(2,1)S(1)} %weight.1.refs_1_.w_ref), custom_call_target="tpu_custom_call" | custom-call | tf_op jit(solution)/shard_map/own_logits/pallas_call | solution.py:390
  168.4 2.3 %logits.1 = f32[32,8,128]{2,1,0:T(8,128)S(1)} custom-call(s32[2]{0:T(128)S(1)} %pad_add_fusion.3.at_ref, s32[2,128]{1,0:T(2,128)S(1)} %reshape.129.refs_6_.ids_ref, f32[2,256,128]{2,1,0:T(8,128)S(1)} %get-tuple-element.8.sum_ref, f32[2,8,128]{2,1,0:T(8,128)S(1)} %get-tuple-element.9.square_ref, bf16[4,2,640,128]{3,2,1,0:T(8,128)(2,1)} %collective-permute-done.1.other_ref, ...), custom_call_target="tpu_custom_call" | custom-call | tf_op jit(solution)/shard_map/logits/pallas_call | solution.py:398
  170.7 10.9 %all_to_all.37.parts_ref = f32[32,8,128]{2,1,0:T(8,128)S(1)} all-to-all(f32[32,8,128]{2,1,0:T(8,128)S(1)} %logits.1), channel_id=1, replica_groups=mesh['x'=4,'z'=8,'c'=2,'h'=2,'y'=4] {'x','y','c'}, dimensions={0} | all-to-all | bytes 262144 | tf_op jit(solution)/shard_map/all_to_all | solution.py:402
  182.3 10.2 %all-to-all-start.6 = ((f32[16,8,128]{2,1,0:T(8,128)}), f32[16,8,128]{2,1,0:T(8,128)S(1)}, u32[]{:S(2)}, u32[]{:S(2)}) async-start(f32[16,8,128]{2,1,0:T(8,128)} %merge.1), calls=%async_computation.6 | async-start | bytes 131072 | tf_op jit(solution)/shard_map/all_to_all | solution.py:404
  193.3 10.8 %all-to-all-done.6.parts_ref = f32[16,8,128]{2,1,0:T(8,128)S(1)} async-done(((f32[16,8,128]{2,1,0:T(8,128)}), f32[16,8,128]{2,1,0:T(8,128)S(1)}, u32[]{:S(2)}, u32[]{:S(2)}) %all-to-all-start.6) | async-done | bytes 65568 | tf_op jit(solution)/shard_map/all_to_all | solution.py:404
  (84 shorter events, 22.7 us)
Async XLA Ops:
  0.6 23.3 %copy-start.16 = (s32[1,1280]{1,0:T(1,128)S(1)}, s32[1,1280]{1,0:T(1,128)}, u32[]{:S(2)}) copy-start(s32[1,1280]{1,0:T(1,128)} %constant.63.clone.source_ref) | copy-start | bytes 15364
  0.6 23.3 %copy-start.15 = (f32[5120]{0:T(1024)S(1)}, f32[5120]{0:T(1024)}, u32[]{:S(2)}) copy-start(f32[5120]{0:T(1024)} %param.16) | copy-start | bytes 61444
  0.7 1.0 copy-start.8
  1.6 0.8 copy-start.11
  2.4 0.8 copy-start.12
  3.9 16.6 %copy-start.18 = (s32[8192]{0:T(1024)S(1)}, s32[8192]{0:T(1024)}, u32[]{:S(2)}) copy-start(s32[8192]{0:T(1024)} %param.18) | copy-start | bytes 98308
  3.9 18.3 %copy-start.17 = (bf16[80,256]{1,0:T(8,128)(2,1)S(1)}, bf16[80,256]{1,0:T(8,128)(2,1)}, u32[]{:S(2)}) copy-start(bf16[80,256]{1,0:T(8,128)(2,1)} %param.15) | copy-start | bytes 122884
  5.2 35.7 %all-to-all-start = ((bf16[8,288,128]{2,1,0:T(8,128)(2,1)}), bf16[8,288,128]{2,1,0:T(8,128)(2,1)S(1)}, u32[]{:S(2)}, u32[]{:S(2)}) async-start(bf16[8,288,128]{2,1,0:T(8,128)(2,1)} %pack.1), calls=%async_computation | async-start | bytes 1179648 | tf_op jit(solution)/shard_map/all_to_all | solution.py:293
  23.9 1.7 copy-start.14
  41.4 40.1 %copy-start.10 = (bf16[80,1024]{1,0:T(8,128)(2,1)S(1)}, bf16[80,1024]{1,0:T(8,128)(2,1)}, u32[]{:S(2)}) copy-start(bf16[80,1024]{1,0:T(8,128)(2,1)} %w_ref.3) | copy-start | bytes 491524
  64.4 35.0 %copy-start = (bf16[4,8,288,128]{3,2,1,0:T(8,128)(2,1)}, bf16[4,8,288,128]{3,2,1,0:T(8,128)(2,1)S(1)}, u32[]{:S(2)}) copy-start(bf16[4,8,288,128]{3,2,1,0:T(8,128)(2,1)S(1)} %all_to_all.35) | copy-start | bytes 7077892
  64.4 17.1 %collective-permute-start = (bf16[32,288,128]{2,1,0:T(8,128)(2,1)S(1)}, bf16[32,288,128]{2,1,0:T(8,128)(2,1)S(1)}, u32[]{:S(2)}, u32[]{:S(2)}) collective-permute-start(bf16[32,288,128]{2,1,0:T(8,128)(2,1)S(1)} %bitcast.48), channel_id=1, source_target_pairs={{0,8},{8,0},{1,9},{9,1},{2,10},{10,2},{3,11},{11,3},{4,12},{12,4},... | collective-permute-start | bytes 7077896 | tf_op jit(solution)/shard_map/ppermute | solution.py:339
  81.5 17.9 %copy-start.5 = (bf16[32,288,128]{2,1,0:T(8,128)(2,1)}, bf16[32,288,128]{2,1,0:T(8,128)(2,1)S(1)}, u32[]{:S(2)}) copy-start(bf16[32,288,128]{2,1,0:T(8,128)(2,1)S(1)} %collective-permute-done.other_ref) | copy-start | bytes 7077892
  81.5 43.0 %copy-start.9 = (bf16[128,1024]{1,0:T(8,128)(2,1)S(1)}, bf16[128,1024]{1,0:T(8,128)(2,1)}, u32[]{:S(2)}) copy-start(bf16[128,1024]{1,0:T(8,128)(2,1)} %q_ref.5) | copy-start | bytes 786436
  108.8 25.7 %all-to-all-start.3 = ((bf16[16,40,128]{2,1,0:T(8,128)(2,1)}), bf16[16,40,128]{2,1,0:T(8,128)(2,1)S(1)}, u32[]{:S(2)}, u32[]{:S(2)}) async-start(bf16[16,40,128]{2,1,0:T(8,128)(2,1)} %add.73.refs_0_), calls=%async_computation.3 | async-start | bytes 327680 | tf_op jit(solution)/shard_map/all_to_all | solution.py:374
  124.5 1.7 copy-start.1
  126.2 1.7 copy-start.6
  136.4 1.1 copy-start.3
  137.5 19.0 %all-to-all-start.4 = ((bf16[16,320,128]{2,1,0:T(8,128)(2,1)}), bf16[16,320,128]{2,1,0:T(8,128)(2,1)}, u32[]{:S(2)}, u32[]{:S(2)}) async-start(bf16[16,320,128]{2,1,0:T(8,128)(2,1)} %copy-done.3), calls=%async_computation.4 | async-start | bytes 2621440 | tf_op jit(solution)/shard_map/all_to_all | solution.py:386
  141.9 1.7 copy-start.2
  143.5 1.3 copy-start.4
  144.9 1.7 copy-start.7
  156.5 11.9 %collective-permute-start.1 = (bf16[4,2,640,128]{3,2,1,0:T(8,128)(2,1)}, bf16[4,2,640,128]{3,2,1,0:T(8,128)(2,1)}, u32[]{:S(2)}, u32[]{:S(2)}) collective-permute-start(bf16[4,2,640,128]{3,2,1,0:T(8,128)(2,1)} %bitcast.27.own_ref), channel_id=1, source_target_pairs={{0,8},{8,0},{1,9},{9,1},{2,10},{10,2},{3,11},{11,3},{4,12},{12,4},... | collective-permute-start | bytes 3932168 | tf_op jit(solution)/shard_map/ppermute | solution.py:388
  182.3 21.8 %all-to-all-start.6 = ((f32[16,8,128]{2,1,0:T(8,128)}), f32[16,8,128]{2,1,0:T(8,128)S(1)}, u32[]{:S(2)}, u32[]{:S(2)}) async-start(f32[16,8,128]{2,1,0:T(8,128)} %merge.1), calls=%async_computation.6 | async-start | bytes 131072 | tf_op jit(solution)/shard_map/all_to_all | solution.py:404
  (1 other events, 0.8 us)

commit v3 on v2

--- a/solution.py
+++ b/solution.py
@@ -14,6 +14,7 @@
 SCORED = 4
 HEADS_DEV = 8
 SLAB = 128
+GROUP = 2
 CHIPS = 32
 BLOCK = 2 * SLAB + SCORED * HEADS_DEV
 FEATS = 80
@@ -45,7 +46,7 @@
         copy.wait()
 
 
-def pack_kernel(at_ref, mask_ref, q_ref, k_ref, v_ref, out_ref, block, queries, rows, sems):
+def pack_kernel(at_ref, mask_ref, q_ref, k_ref, v_ref, block_ref, out_ref, block, queries, rows, sems):
     copies = [
         pltpu.make_async_copy(k_ref, block.at[pl.ds(0, SLAB)], sems.at[0]),
         pltpu.make_async_copy(v_ref, block.at[pl.ds(SLAB, SLAB)], sems.at[1]),
@@ -64,11 +65,22 @@
     for h in range(HEADS_DEV):
         rows[pl.ds(h, SCORED, stride=HEADS_DEV), :] = picked[:SCORED, h * 128 : (h + 1) * 128]
     block[2 * SLAB :, :] = rows[...].astype(jnp.bfloat16)
+    single = pltpu.make_async_copy(block, block_ref, sems.at[4])
+    single.start()
     send_copies(block, out_ref, sems)
-
-
-def spread_kernel(*refs):
-    send_copies(refs[0], refs[-2], refs[-1])
+    single.wait()
+
+
+def spread_kernel(at_ref, near_ref, far_ref, out_ref, sems):
+    copies = []
+    for i in range(4):
+        for j, (ref, half) in enumerate(((near_ref, at_ref[0]), (far_ref, 1 - at_ref[0]))):
+            target = out_ref.at[i, pl.ds(half * 4, 4)]
+            copies.append(pltpu.make_async_copy(ref, target, sems.at[2 * i + j]))
+    for copy in copies:
+        copy.start()
+    for copy in copies:
+        copy.wait()
 
 
 def weight_kernel(source_ref, gain_ref, w_ref, out_ref):
@@ -82,51 +94,55 @@
             out_ref[:, (c * 4 + x) * 640 : (c * 4 + x + 1) * 640] = moved[:, c * 640 : (c + 1) * 640]
 
 
-def attend(own_ref, other_ref, core, q, low, high, bounds, group):
+def attend(own_ref, other_ref, core, q, low, high, first, last, bufs):
     columns = q.shape[0]
-    half = group * SLAB
+    half = GROUP * SLAB
     row = iota((2 * half, 1), 0)
     inside = jnp.where(row < half, row, row - half)
     key0 = (inside // SLAB) * (2 * SLAB) + inside % SLAB + jnp.where(row < half, core, 1 - core) * SLAB
-
-    def step(edge, g, carry):
+    turned = q.T
+
+    def rows(g, at):
+        chips = pl.ds(pl.multiple_of(jnp.minimum(g * GROUP, CHIPS - GROUP), GROUP), GROUP)
+        parts = [ref[chips, at : at + SLAB, :].reshape(half, HEAD_DIM) for ref in (own_ref, other_ref)]
+        return jnp.concatenate(parts, axis=0)
+
+    def scores(g):
+        return jnp.dot(rows(g, 0), turned, preferred_element_type=jnp.float32)
+
+    def soften(g, buf, carry):
         top, total, acc = carry
-        chips = pl.ds(pl.multiple_of(g * group, group), group)
-
-        def rows(at):
-            parts = [ref[chips, at : at + SLAB, :].reshape(half, HEAD_DIM) for ref in (own_ref, other_ref)]
-            return jnp.concatenate(parts, axis=0)
-
-        s = lax.dot_general(rows(0), q, NT, preferred_element_type=jnp.float32) * SCALE2
-        if edge:
-            offset = g * (2 * half)
-            s = jnp.where((key0 >= low - offset) & (key0 <= high - offset), s, masked_fill)
+        offset = g * (2 * half)
+        s = jnp.where((key0 >= low - offset) & (key0 <= high - offset), buf[...] * SCALE2, masked_fill)
         new_top = jnp.maximum(top, jnp.max(s, axis=0, keepdims=True))
         p = jnp.exp2(s - new_top)
         keep = jnp.exp2(top - new_top)
         total = total * keep + jnp.sum(p, axis=0, keepdims=True)
-        pv = lax.dot_general(rows(SLAB), p.astype(jnp.bfloat16), TN, preferred_element_type=jnp.float32)
+        pv = lax.dot_general(rows(g, SLAB), p.astype(jnp.bfloat16), TN, preferred_element_type=jnp.float32)
         return new_top, total, acc * keep + pv
 
-    carry = (
+    begin = first // GROUP
+    steps = (last // GROUP + 2 - begin) // 2
+
+    def step(i, carry):
+        g = begin + 2 * i
+        bufs[1][...] = scores(g + 1)
+        carry = soften(g, bufs[0], carry)
+        bufs[0][...] = scores(g + 2)
+        return soften(g + 1, bufs[1], carry)
+
+    bufs[0][...] = scores(begin)
+    start = (
         jnp.full((1, columns), start_max, jnp.float32),
         jnp.zeros((1, columns), jnp.float32),
         jnp.zeros((HEAD_DIM, columns), jnp.float32),
     )
-    for i, edge in enumerate((True, False, True)):
-        carry = lax.fori_loop(bounds[i], bounds[i + 1], functools.partial(step, edge), carry)
-    _, total, acc = carry
+    _, total, acc = lax.fori_loop(0, steps, step, start)
     return acc / total
 
 
-def group_bounds(first, low, high, last_chip, group):
-    size = group * 2 * SLAB
-    begin, end = first // size, last_chip // group + 1
-    whole = jnp.clip((low + size - 1) // size, begin, end)
-    return begin, whole, jnp.clip((high + 1) // size, whole, end), end
-
-
-def scored_kernel(core_ref, span_ref, low_ref, high_ref, own_ref, other_ref, w_ref, out_ref, rows, scored):
+def scored_kernel(core_ref, first_ref, low_ref, high_ref, own_ref, other_ref, w_ref, *refs):
+    out_ref, rows, scored = refs[-5:-2]
     core = core_ref[0]
     for t in range(8):
         q = jnp.concatenate(
@@ -136,8 +152,17 @@
             ),
             axis=0,
         )
-        bounds = group_bounds(span_ref[0, t], span_ref[1, t], span_ref[2, t], 4 * t + 3, 4)
-        mixed = attend(own_ref, other_ref, core, q, low_ref[t : t + 1, :], high_ref[t : t + 1, :], bounds, 4)
+        mixed = attend(
+            own_ref,
+            other_ref,
+            core,
+            q,
+            low_ref[t : t + 1, :],
+            high_ref[t : t + 1, :],
+            first_ref[t],
+            4 * t + 3,
+            refs[-2:],
+        )
         rows[...] = mixed.T
         for h in range(HEADS_DEV):
             part = rows[pl.ds(h, 32, stride=HEADS_DEV), :].astype(jnp.bfloat16)
@@ -153,12 +178,11 @@
 
 
 def context_kernel(start_head, at_ref, low_ref, high_ref, own_ref, other_ref, q_ref, *refs):
-    out_ref = refs[-1]
+    out_ref = refs[-3]
     heads = range(start_head, start_head + 4)
     q = jnp.concatenate([q_ref[:, h * 128 : (h + 1) * 128] for h in heads], axis=0)
     low, high = jnp.tile(low_ref[...], (1, 4)), jnp.tile(high_ref[...], (1, 4))
-    bounds = group_bounds(at_ref[1], at_ref[2], at_ref[3] * 256, at_ref[3], 4)
-    mixed = attend(own_ref, other_ref, at_ref[0], q, low, high, bounds, 4)
+    mixed = attend(own_ref, other_ref, at_ref[0], q, low, high, at_ref[1], at_ref[2], refs[-2:])
     for i in range(4):
         out_ref[:, i * 128 : (i + 1) * 128] = mixed[:, i * 128 : (i + 1) * 128].T.astype(jnp.bfloat16)
 
@@ -171,10 +195,11 @@
     send_copies(block, out_ref, sems)
 
 
-def hidden_kernel(parts_ref, dep_ref, out_ref, block, sems):
+def hidden_kernel(parts_ref, dep_ref, out_ref):
     total = parts_ref[:8].astype(jnp.float32) + parts_ref[8:].astype(jnp.float32)
-    block[...] = total.reshape(8 * HALF, 128).astype(jnp.bfloat16)
-    send_copies(block, out_ref, sems)
+    total = total.reshape(8 * HALF, 128).astype(jnp.bfloat16)
+    for i in range(out_ref.shape[0]):
+        out_ref[i] = total
 
 
 def add_logits(core, hidden_ref, w_ref, half):
@@ -267,7 +292,7 @@
     loss_mask,
     doc_lengths,
 ):
-    x, z, core = lax.axis_index("x"), lax.axis_index("z"), lax.axis_index("c")
+    x, z, core = lax.axis_index("x"), lax.axis_index(("zh", "zl")), lax.axis_index("c")
     h, y = lax.axis_index("h"), lax.axis_index("y")
     chip = x * 8 + z
     slab = chip * 2 + core
@@ -276,21 +301,25 @@
     rank = jnp.dot(slabs.astype(jnp.float32), upto, preferred_element_type=jnp.float32).astype(jnp.int32)
     rank = jnp.where(slabs == 1, rank - 1, -1)
     own_rank = lax.dynamic_slice_in_dim(rank, slab, 1, 0)
-    packed = call(
+    block, packed = call(
         pack_kernel,
-        (8, BLOCK, 128),
+        (BLOCK, 128),
         jnp.bfloat16,
-        [SMEM, VMEM, ANY, ANY, ANY],
+        [SMEM, VMEM, HBM, HBM, HBM],
         [
             pltpu.VMEM((BLOCK, 128), jnp.bfloat16),
             pltpu.VMEM((SLAB, 1024), jnp.bfloat16),
             pltpu.VMEM((32, 128), jnp.float32),
-            pltpu.SemaphoreType.DMA((8,)),
+            pltpu.SemaphoreType.DMA((5,)),
         ],
         name="pack",
-        out=HBM,
+        out=ANY,
+        more=jax.ShapeDtypeStruct((4, BLOCK, 128), jnp.bfloat16),
     )(slab[None], slabs, queries, keys, values)
-    along_z = lax.all_to_all(packed, "z", 0, 0)
+    block = lax.ppermute(block, ("zh", "zl"), [(i, i ^ 4) for i in range(8)])
+    near = lax.all_to_all(packed, "zl", 0, 0)
+    near, block = lax.optimization_barrier((near, block))
+    far = lax.all_to_all(jnp.broadcast_to(block[None], (4, BLOCK, 128)), "zl", 0, 0)
 
     bounds = jnp.cumsum(doc_lengths)
     position = jnp.arange(64 * SLAB, dtype=jnp.int32)
@@ -309,7 +338,7 @@
     high = columns(pick(position))
     low = columns(pick(begin))
     ids = pick(sampled_ids).reshape(CHIPS, 2, SCORED).transpose(1, 0, 2).reshape(2, 128)
-    span = jnp.stack((jnp.min(low, axis=1), jnp.max(low, axis=1), jnp.min(high, axis=1)))
+    first = jnp.min(low, axis=1) // 256
     core_at = core[None]
 
     source = jnp.asarray(source_columns())
@@ -322,30 +351,33 @@
 
     own_begin = lax.dynamic_slice_in_dim(begin, slab * SLAB, SLAB, 0)
     own_position = slab * SLAB + jnp.arange(SLAB, dtype=jnp.int32)
-    at = jnp.stack((core, own_begin[0], own_begin[SLAB - 1], chip))
+    at = jnp.stack((core, own_begin[0] // 256, chip))
     base = ((slab * 2 + h) * 4 + y) * 256
 
-    early = (weight, mine, low, high, span, ids, own_begin)
     spread = call(
         spread_kernel,
         (4, 8, BLOCK, 128),
         jnp.bfloat16,
-        [VMEM] + [ANY] * len(early),
-        [pltpu.SemaphoreType.DMA((4,))],
+        [SMEM, VMEM, VMEM],
+        [pltpu.SemaphoreType.DMA((8,))],
         name="spread",
-        out=HBM,
-    )(along_z, *early)
+        out=ANY,
+    )(lax.axis_index("zh")[None], near, far)
     own = lax.all_to_all(spread, "x", 0, 0).reshape(CHIPS, BLOCK, 128)
+    own, weight, mine, low, high, first, ids, own_begin = lax.optimization_barrier(
+        (own, weight, mine, low, high, first, ids, own_begin)
+    )
     other = lax.ppermute(own, "c", [(0, 1), (1, 0)])
+    scores = pltpu.VMEM((2 * GROUP * SLAB, 256), jnp.float32)
     parts = call(
         scored_kernel,
         (4, HALF, 128),
         jnp.float32,
         [SMEM, SMEM] + [VMEM] * 5,
-        [pltpu.VMEM((256, 128), jnp.float32), pltpu.VMEM((256, 1024), jnp.bfloat16)],
+        [pltpu.VMEM((256, 128), jnp.float32), pltpu.VMEM((256, 1024), jnp.bfloat16), scores, scores],
         name="scored",
         vmem=28,
-    )(core_at, span, low, high, own, other, out_weight)
+    )(core_at, first, low, high, own, other, out_weight)
 
     def context_of(start_head, after):
         return call(
@@ -353,6 +385,7 @@
             (SLAB, 512),
             jnp.bfloat16,
             [SMEM] + [VMEM] * 5 + [ANY],
+            [pltpu.VMEM((2 * GROUP * SLAB, 512), jnp.float32)] * 2,
             flops=4 * 1024 * 4224 * 128,
             size=6 * 2**20,
             name="context",
@@ -371,17 +404,8 @@
         out=HBM,
     )(parts, mine)
     context_a = context_of(0, sums)
-    sums = lax.all_to_all(sums, ("h", "z"), 0, 0)
-    block = pltpu.VMEM((8 * HALF, 128), jnp.bfloat16)
-    hidden = call(
-        hidden_kernel,
-        (16, 8 * HALF, 128),
-        jnp.bfloat16,
-        [VMEM, ANY],
-        [block, pltpu.SemaphoreType.DMA((16,))],
-        name="hidden",
-        out=HBM,
-    )(sums, context_a)
+    sums = lax.all_to_all(sums, ("h", "zh", "zl"), 0, 0)
+    hidden = call(hidden_kernel, (16, 8 * HALF, 128), jnp.bfloat16, [VMEM, ANY], name="hidden")(sums, context_a)
     context_b = context_of(4, hidden)
     hidden = lax.all_to_all(hidden, ("x", "y"), 0, 0).reshape(4, 2, 640, 128)
     hidden, context_b = lax.optimization_barrier((hidden, context_b))
@@ -401,7 +425,7 @@
     context = jnp.concatenate((context_a, context_b), axis=1)
     tiles = lax.all_to_all(tiles, ("x", "y", "c"), 0, 0)
     tiles = call(merge_kernel, (16, 8, 128), jnp.float32, [VMEM], name="merge")(tiles)
-    tiles = lax.all_to_all(tiles, ("h", "z"), 0, 0)
+    tiles = lax.all_to_all(tiles, ("h", "zh", "zl"), 0, 0)
     logprob = call(final_kernel, (1, 128), jnp.float32, [SMEM, VMEM, VMEM], name="final")(
         jnp.stack((core, chip)), own_rank, tiles
     )
@@ -409,8 +433,8 @@
 
 
 def solution(mesh):
-    fine = Mesh(mesh.devices.reshape(4, 8, 2, 2, 4), ("x", "z", "c", "h", "y"))
-    ctx, tp = ("x", "z", "c"), ("h", "y")
+    fine = Mesh(mesh.devices.reshape(4, 2, 4, 2, 2, 4), ("x", "zh", "zl", "c", "h", "y"))
+    ctx, tp = ("x", "zh", "zl", "c"), ("h", "y")
     placed = (
         P(ctx, tp),
         P(ctx, tp),

time: 206 us -> 198 us (0.961)
  blocking collectives: 42.5 us -> 19.4 us
  waiting for transfers between devices: 39.6 us -> 53.7 us
  starting transfers between devices: 63.1 us -> 67.8 us
  local copies, waits for them, and re-layouts: 17.7 us -> 14.4 us
    all_to_all x1 -> x0, blocking collectives: 23 us -> none  [body(): own = lax.all_to_all(spread, 'x', 0, 0).reshape(CHIPS, BLOCK, 128)]
    all_to_all x3 -> x5, waiting for transfers between devices: 26.8 us -> 38.5 us  [the longest x1 15.6 us: body(): own = lax.all_to_all(spread, 'x', 0, 0).reshape(CHIPS, BLOCK, 128)]
    ppermute x0 -> x1, starting transfers between devices: none -> 8.81 us  [body(): block = lax.ppermute(block, ('zh', 'zl'), [(i, i ^ 4) for i in range(8)])]
    ppermute x1, starting transfers between devices: 12.9 us -> 7.49 us  [body(): other = lax.ppermute(own, 'c', [(0, 1), (1, 0)])]
    unnamed x40 -> x36, local copies, waits for them, and re-layouts: 14.3 us -> 11 us
    pallas_call x2, Pallas kernels: 4.14 us -> 6.49 us  [context_of(): call(functools.partial(context_kernel, start_head), (SLAB, 512), jnp.bflo...]
    all_to_all x3 -> x5, starting transfers between devices: 36.8 us -> 38.2 us  [the longest x1 11 us: body(): sums = lax.all_to_all(sums, ('h', 'zh', 'zl'), 0, 0)]
  transfers between devices with their start and end apart: 6 -> 9, of which waited for: 6 -> 8; matrix products, arithmetic and copies ran while one was open for 4% -> 3% of each run, Pallas kernels for 5% -> 6%
where the time goes in v3:
time: 198 us; the launch traced here: 197 us
  starting transfers between devices  67.8 us (34%)
  waiting for transfers between devices  53.7 us (27%)
  Pallas kernels  38 us (19%)
  blocking collectives  19.4 us (10%)
  local copies, waits for them, and re-layouts  14.4 us (7%)
  other arithmetic  2.1 us (1%)
    pallas_call x1, Pallas kernels, body(): call(scored_kernel, (4, HALF, 128), jnp.float32, [SMEM, SMEM] + [VMEM] *...  17.8 us
    all_to_all x1, waiting for transfers between devices, body(): own = lax.all_to_all(spread, 'x', 0, 0).reshape(CHIPS, BLOCK, 128)  15.6 us
    all_to_all x1, starting transfers between devices, body(): sums = lax.all_to_all(sums, ('h', 'zh', 'zl'), 0, 0)  11 us
    unnamed x36, local copies, waits for them, and re-layouts  11 us
    all_to_all x1, blocking collectives, body(): tiles = lax.all_to_all(tiles, ('x', 'y', 'c'), 0, 0)  10.9 us
    all_to_all x1, waiting for transfers between devices, body(): tiles = lax.all_to_all(tiles, ('h', 'zh', 'zl'), 0, 0)  10.8 us
    all_to_all x1, starting transfers between devices, body(): lax.all_to_all(jnp.broadcast_to(block[None], (4, BLOCK, 128)), 'zl', 0, 0)  9.52 us
    ppermute x1, starting transfers between devices, body(): hidden_other = lax.ppermute(hidden, 'c', [(0, 1), (1, 0)])  8.9 us
  transfers between devices with their start and end apart: 9, of which 8 were waited for; matrix products, arithmetic and copies ran while one was open for 3% of the time, Pallas kernels for 6%

profile of v3, /device:TPU:1, one launch (start us, length us, event | category | flops | bytes accessed | tf_op | source)
XLA Modules:
  0.0 196.7 jit_solution(2172070855024932855)
XLA Ops:
  5.1 6.5 %all-to-all-start = ((bf16[4,288,128]{2,1,0:T(8,128)(2,1)}), bf16[4,288,128]{2,1,0:T(8,128)(2,1)S(1)}, u32[]{:S(2)}, u32[]{:S(2)}) async-start(bf16[4,288,128]{2,1,0:T(8,128)(2,1)} %get-tuple-element.18), calls=%async_computation | async-start | bytes 589824 | tf_op jit(solution)/shard_map/all_to_all | solution.py:320
  11.5 8.8 %collective-permute-start = (bf16[288,128]{1,0:T(8,128)(2,1)S(1)}, bf16[288,128]{1,0:T(8,128)(2,1)S(1)}, u32[]{:S(2)}, u32[]{:S(2)}) collective-permute-start(bf16[288,128]{1,0:T(8,128)(2,1)S(1)} %get-tuple-element.19), channel_id=1, source_target_pairs={{0,64},{16,80},{32,96},{48,112},{64,0},{80,16},{96,32},{112,48},{1... | collective-permute-start | bytes 221192 | tf_op jit(solution)/shard_map/ppermute | solution.py:319
  20.3 1.8 collective-permute-done
  22.9 9.5 %all-to-all-start.1 = ((bf16[4,288,128]{2,1,0:T(8,128)(2,1)}), bf16[4,288,128]{2,1,0:T(8,128)(2,1)S(1)}, u32[]{:S(2)}, u32[]{:S(2)}) async-start(bf16[4,288,128]{2,1,0:T(8,128)(2,1)} %broadcast_in_dim.87), calls=%async_computation.1 | async-start | bytes 589824 | tf_op jit(solution)/shard_map/all_to_all | solution.py:322
  33.3 5.1 %all-to-all-done.1.far_ref = bf16[4,288,128]{2,1,0:T(8,128)(2,1)S(1)} async-done(((bf16[4,288,128]{2,1,0:T(8,128)(2,1)}), bf16[4,288,128]{2,1,0:T(8,128)(2,1)S(1)}, u32[]{:S(2)}, u32[]{:S(2)}) %all-to-all-start.1) | async-done | bytes 294944 | tf_op jit(solution)/shard_map/all_to_all | solution.py:322
  39.9 4.6 %all-to-all-start.2 = ((bf16[4,8,288,128]{3,2,1,0:T(8,128)(2,1)}), bf16[4,8,288,128]{3,2,1,0:T(8,128)(2,1)}, u32[]{:S(2)}, u32[]{:S(2)}) async-start(bf16[4,8,288,128]{3,2,1,0:T(8,128)(2,1)} %spread.1), calls=%async_computation.2 | async-start | bytes 4718592 | tf_op jit(solution)/shard_map/all_to_all | solution.py:366
  49.8 3.7 %weight.1.w_ref = bf16[256,5120]{1,0:T(8,128)(2,1)S(1)} custom-call(s32[1,1280]{1,0:T(1,128)S(1)} %copy-done.14, f32[1,5120]{1,0:T(1,128)S(1)} %bitcast.55, bf16[256,5120]{1,0:T(8,128)(2,1)S(1)} %copy-done.12), custom_call_target="tpu_custom_call" | custom-call | flops 3355443200 | tf_op jit(solution)/shard_map/weight/pallas_call | solution.py:345
  53.5 15.6 %all-to-all-done.2 = bf16[4,8,288,128]{3,2,1,0:T(8,128)(2,1)} async-done(((bf16[4,8,288,128]{3,2,1,0:T(8,128)(2,1)}), bf16[4,8,288,128]{3,2,1,0:T(8,128)(2,1)}, u32[]{:S(2)}, u32[]{:S(2)}) %all-to-all-start.2) | async-done | bytes 2359328 | tf_op jit(solution)/shard_map/all_to_all | solution.py:366
  69.1 7.5 %collective-permute-start.1 = (bf16[32,288,128]{2,1,0:T(8,128)(2,1)}, bf16[32,288,128]{2,1,0:T(8,128)(2,1)S(1)}, u32[]{:S(2)}, u32[]{:S(2)}) collective-permute-start(bf16[32,288,128]{2,1,0:T(8,128)(2,1)} %bitcast.8.own_ref), channel_id=1, source_target_pairs={{0,8},{8,0},{1,9},{9,1},{2,10},{10,2},{3,11},{11,3},{4,12},{12,4},... | collective-permute-start | bytes 7077896 | tf_op jit(solution)/shard_map/ppermute | solution.py:370
  76.6 4.3 %collective-permute-done.1.other_ref = bf16[32,288,128]{2,1,0:T(8,128)(2,1)S(1)} collective-permute-done((bf16[32,288,128]{2,1,0:T(8,128)(2,1)}, bf16[32,288,128]{2,1,0:T(8,128)(2,1)S(1)}, u32[]{:S(2)}, u32[]{:S(2)}) %collective-permute-start.1) | collective-permute-done | bytes 2359328 | tf_op jit(solution)/shard_map/ppermute | solution.py:370
  81.0 17.8 %scored.1 = f32[4,40,128]{2,1,0:T(8,128)S(1)} custom-call(s32[1]{0:T(128)} %bitcast.core_ref, s32[8]{0:T(128)S(1)} %and_select_fusion.first_ref, s32[8,256]{1,0:T(8,128)S(1)} %reshape.122.low_ref, s32[8,256]{1,0:T(8,128)S(1)} %reshape.129.high_ref, bf16[32,288,128]{2,1,0:T(8,128)(2,1)} %bitcast.8.own_ref, ...), custom_call_target="tpu_custom_call" | custom-call | tf_op jit(solution)/shard_map/scored/pallas_call | solution.py:372
  98.8 8.6 %all_to_all.40.parts_ref = f32[4,40,128]{2,1,0:T(8,128)S(1)} all-to-all(f32[4,40,128]{2,1,0:T(8,128)S(1)} %scored.1), channel_id=1, replica_groups=mesh['x'=4,'zh'=2,'zl'=4,'c'=2,'h'=2,'y'=4] {'y'}, dimensions={0} | all-to-all | bytes 163840 | tf_op jit(solution)/shard_map/all_to_all | solution.py:395
  108.2 11.0 %all-to-all-start.4 = ((bf16[16,40,128]{2,1,0:T(8,128)(2,1)}), bf16[16,40,128]{2,1,0:T(8,128)(2,1)S(1)}, u32[]{:S(2)}, u32[]{:S(2)}) async-start(bf16[16,40,128]{2,1,0:T(8,128)(2,1)} %add.73.refs_0_), calls=%async_computation.4 | async-start | bytes 327680 | tf_op jit(solution)/shard_map/all_to_all | solution.py:407
  121.2 3.3 %context.2.dep_ref = bf16[128,512]{1,0:T(8,128)(2,1)S(1)} custom-call(s32[3]{0:T(128)S(1)} %pad_add_fusion.at_ref, s32[1,128]{1,0:T(1,128)S(1)} %bitcast.53, s32[1,128]{1,0:T(1,128)S(1)} %iota_add_fusion.high_ref, bf16[32,288,128]{2,1,0:T(8,128)(2,1)} %bitcast.8.own_ref, bf16[32,288,128]{2,1,0:T(8,128)(2,1)S(1)} %copy-done.3, ...), custom_call_target="tpu_custom_call" | custom-call | flops 2214592512 | bytes 6291456 | tf_op jit(solution)/shard_map/context/pallas_call | solution.py:383
  124.4 7.0 %all-to-all-done.4.parts_ref = bf16[16,40,128]{2,1,0:T(8,128)(2,1)S(1)} async-done(((bf16[16,40,128]{2,1,0:T(8,128)(2,1)}), bf16[16,40,128]{2,1,0:T(8,128)(2,1)S(1)}, u32[]{:S(2)}, u32[]{:S(2)}) %all-to-all-start.4) | async-done | bytes 163872 | tf_op jit(solution)/shard_map/all_to_all | solution.py:407
  132.6 4.4 %all-to-all-start.5 = ((bf16[16,320,128]{2,1,0:T(8,128)(2,1)}), bf16[16,320,128]{2,1,0:T(8,128)(2,1)}, u32[]{:S(2)}, u32[]{:S(2)}) async-start(bf16[16,320,128]{2,1,0:T(8,128)(2,1)} %copy-done), calls=%async_computation.5 | async-start | bytes 2621440 | tf_op jit(solution)/shard_map/all_to_all | solution.py:410
  140.0 3.2 %context.3.dep_ref = bf16[128,512]{1,0:T(8,128)(2,1)S(1)} custom-call(s32[3]{0:T(128)S(1)} %pad_add_fusion.at_ref, s32[1,128]{1,0:T(1,128)S(1)} %bitcast.54, s32[1,128]{1,0:T(1,128)S(1)} %iota_add_fusion.high_ref, bf16[32,288,128]{2,1,0:T(8,128)(2,1)} %bitcast.8.own_ref, bf16[32,288,128]{2,1,0:T(8,128)(2,1)S(1)} %copy-done.4, ...), custom_call_target="tpu_custom_call" | custom-call | flops 2214592512 | bytes 6291456 | tf_op jit(solution)/shard_map/context/pallas_call | solution.py:383
  143.3 8.4 %all-to-all-done.5 = bf16[16,320,128]{2,1,0:T(8,128)(2,1)} async-done(((bf16[16,320,128]{2,1,0:T(8,128)(2,1)}), bf16[16,320,128]{2,1,0:T(8,128)(2,1)}, u32[]{:S(2)}, u32[]{:S(2)}) %all-to-all-start.5) | async-done | bytes 1310752 | tf_op jit(solution)/shard_map/all_to_all | solution.py:410
  151.7 8.9 %collective-permute-start.2 = (bf16[4,2,640,128]{3,2,1,0:T(8,128)(2,1)}, bf16[4,2,640,128]{3,2,1,0:T(8,128)(2,1)}, u32[]{:S(2)}, u32[]{:S(2)}) collective-permute-start(bf16[4,2,640,128]{3,2,1,0:T(8,128)(2,1)} %bitcast.27.own_ref), channel_id=1, source_target_pairs={{0,8},{8,0},{1,9},{9,1},{2,10},{10,2},{3,11},{11,3},{4,12},{12,4},... | collective-permute-start | bytes 3932168 | tf_op jit(solution)/shard_map/ppermute | solution.py:412
  160.7 2.2 %own_logits.1 = (f32[2,256,128]{2,1,0:T(8,128)S(1)}, f32[2,8,128]{2,1,0:T(8,128)S(1)}) custom-call(s32[2]{0:T(128)S(1)} %pad_add_fusion.2.at_ref, bf16[4,2,640,128]{3,2,1,0:T(8,128)(2,1)} %bitcast.27.own_ref, bf16[256,5120]{1,0:T(8,128)(2,1)S(1)} %weight.1.w_ref), custom_call_target="tpu_custom_call" | custom-call | tf_op jit(solution)/shard_map/own_logits/pallas_call | solution.py:414
  163.6 2.3 %logits.1 = f32[32,8,128]{2,1,0:T(8,128)S(1)} custom-call(s32[2]{0:T(128)S(1)} %pad_add_fusion.2.at_ref, s32[2,128]{1,0:T(2,128)S(1)} %reshape.131.ids_ref, f32[2,256,128]{2,1,0:T(8,128)S(1)} %get-tuple-element.32.sum_ref, f32[2,8,128]{2,1,0:T(8,128)S(1)} %get-tuple-element.33.square_ref, bf16[4,2,640,128]{3,2,1,0:T(8,128)(2,1)} %collective-permute-done.2.other_ref, ...), custom_call_target="tpu_custom_call" | custom-call | tf_op jit(solution)/shard_map/logits/pallas_call | solution.py:422
  165.8 10.9 %all_to_all.41.parts_ref = f32[32,8,128]{2,1,0:T(8,128)S(1)} all-to-all(f32[32,8,128]{2,1,0:T(8,128)S(1)} %logits.1), channel_id=1, replica_groups=mesh['x'=4,'zh'=2,'zl'=4,'c'=2,'h'=2,'y'=4] {'x','y','c'}, dimensions={0} | all-to-all | bytes 262144 | tf_op jit(solution)/shard_map/all_to_all | solution.py:426
  177.4 6.5 %all-to-all-start.7 = ((f32[16,8,128]{2,1,0:T(8,128)}), f32[16,8,128]{2,1,0:T(8,128)S(1)}, u32[]{:S(2)}, u32[]{:S(2)}) async-start(f32[16,8,128]{2,1,0:T(8,128)} %merge.1), calls=%async_computation.7 | async-start | bytes 131072 | tf_op jit(solution)/shard_map/all_to_all | solution.py:428
  184.8 10.8 %all-to-all-done.7.parts_ref = f32[16,8,128]{2,1,0:T(8,128)S(1)} async-done(((f32[16,8,128]{2,1,0:T(8,128)}), f32[16,8,128]{2,1,0:T(8,128)S(1)}, u32[]{:S(2)}, u32[]{:S(2)}) %all-to-all-start.7) | async-done | bytes 65568 | tf_op jit(solution)/shard_map/all_to_all | solution.py:428
  (83 shorter events, 22.8 us)
Async XLA Ops:
  0.6 1.0 copy-start.5
  1.6 0.8 copy-start.8
  5.1 17.1 %all-to-all-start = ((bf16[4,288,128]{2,1,0:T(8,128)(2,1)}), bf16[4,288,128]{2,1,0:T(8,128)(2,1)S(1)}, u32[]{:S(2)}, u32[]{:S(2)}) async-start(bf16[4,288,128]{2,1,0:T(8,128)(2,1)} %get-tuple-element.18), calls=%async_computation | async-start | bytes 589824 | tf_op jit(solution)/shard_map/all_to_all | solution.py:320
  11.5 10.7 %collective-permute-start = (bf16[288,128]{1,0:T(8,128)(2,1)S(1)}, bf16[288,128]{1,0:T(8,128)(2,1)S(1)}, u32[]{:S(2)}, u32[]{:S(2)}) collective-permute-start(bf16[288,128]{1,0:T(8,128)(2,1)S(1)} %get-tuple-element.19), channel_id=1, source_target_pairs={{0,64},{16,80},{32,96},{48,112},{64,0},{80,16},{96,32},{112,48},{1... | collective-permute-start | bytes 221192 | tf_op jit(solution)/shard_map/ppermute | solution.py:319
  22.9 15.5 %all-to-all-start.1 = ((bf16[4,288,128]{2,1,0:T(8,128)(2,1)}), bf16[4,288,128]{2,1,0:T(8,128)(2,1)S(1)}, u32[]{:S(2)}, u32[]{:S(2)}) async-start(bf16[4,288,128]{2,1,0:T(8,128)(2,1)} %broadcast_in_dim.87), calls=%async_computation.1 | async-start | bytes 589824 | tf_op jit(solution)/shard_map/all_to_all | solution.py:322
  39.9 5.1 %copy-start.11 = (s32[8192]{0:T(1024)S(1)}, s32[8192]{0:T(1024)}, u32[]{:S(2)}) copy-start(s32[8192]{0:T(1024)} %param.19) | copy-start | bytes 98308
  39.9 5.2 %copy-start.16 = (s32[8192]{0:T(1024)S(1)}, s32[8192]{0:T(1024)}, u32[]{:S(2)}) copy-start(s32[8192]{0:T(1024)} %param.18) | copy-start | bytes 98308
  39.9 6.9 %copy-start.15 = (bf16[80,256]{1,0:T(8,128)(2,1)S(1)}, bf16[80,256]{1,0:T(8,128)(2,1)}, u32[]{:S(2)}) copy-start(bf16[80,256]{1,0:T(8,128)(2,1)} %param.15) | copy-start | bytes 122884
  39.9 29.2 %all-to-all-start.2 = ((bf16[4,8,288,128]{3,2,1,0:T(8,128)(2,1)}), bf16[4,8,288,128]{3,2,1,0:T(8,128)(2,1)}, u32[]{:S(2)}, u32[]{:S(2)}) async-start(bf16[4,8,288,128]{3,2,1,0:T(8,128)(2,1)} %spread.1), calls=%async_computation.2 | async-start | bytes 4718592 | tf_op jit(solution)/shard_map/all_to_all | solution.py:366
  44.6 3.5 %copy-start.13 = (f32[5120]{0:T(1024)S(1)}, f32[5120]{0:T(1024)}, u32[]{:S(2)}) copy-start(f32[5120]{0:T(1024)} %param.16) | copy-start | bytes 61444
  44.6 3.5 %copy-start.14 = (s32[1,1280]{1,0:T(1,128)S(1)}, s32[1,1280]{1,0:T(1,128)}, u32[]{:S(2)}) copy-start(s32[1,1280]{1,0:T(1,128)} %constant.87.clone.source_ref) | copy-start | bytes 15364
  48.1 1.7 copy-start.12
  49.8 31.2 %copy-start.7 = (bf16[80,1024]{1,0:T(8,128)(2,1)S(1)}, bf16[80,1024]{1,0:T(8,128)(2,1)}, u32[]{:S(2)}) copy-start(bf16[80,1024]{1,0:T(8,128)(2,1)} %w_ref.3) | copy-start | bytes 491524
  69.1 11.8 %collective-permute-start.1 = (bf16[32,288,128]{2,1,0:T(8,128)(2,1)}, bf16[32,288,128]{2,1,0:T(8,128)(2,1)S(1)}, u32[]{:S(2)}, u32[]{:S(2)}) collective-permute-start(bf16[32,288,128]{2,1,0:T(8,128)(2,1)} %bitcast.8.own_ref), channel_id=1, source_target_pairs={{0,8},{8,0},{1,9},{9,1},{2,10},{10,2},{3,11},{11,3},{4,12},{12,4},... | collective-permute-start | bytes 7077896 | tf_op jit(solution)/shard_map/ppermute | solution.py:370
  81.0 17.8 %copy-start.2 = (bf16[32,288,128]{2,1,0:T(8,128)(2,1)}, bf16[32,288,128]{2,1,0:T(8,128)(2,1)S(1)}, u32[]{:S(2)}) copy-start(bf16[32,288,128]{2,1,0:T(8,128)(2,1)S(1)} %collective-permute-done.1.other_ref) | copy-start | bytes 7077892
  81.0 38.5 %copy-start.6 = (bf16[128,1024]{1,0:T(8,128)(2,1)S(1)}, bf16[128,1024]{1,0:T(8,128)(2,1)}, u32[]{:S(2)}) copy-start(bf16[128,1024]{1,0:T(8,128)(2,1)} %q_ref.5) | copy-start | bytes 786436
  108.2 23.2 %all-to-all-start.4 = ((bf16[16,40,128]{2,1,0:T(8,128)(2,1)}), bf16[16,40,128]{2,1,0:T(8,128)(2,1)S(1)}, u32[]{:S(2)}, u32[]{:S(2)}) async-start(bf16[16,40,128]{2,1,0:T(8,128)(2,1)} %add.73.refs_0_), calls=%async_computation.4 | async-start | bytes 327680 | tf_op jit(solution)/shard_map/all_to_all | solution.py:407
  119.5 1.7 copy-start.3
  131.5 1.1 copy-start
  132.6 19.0 %all-to-all-start.5 = ((bf16[16,320,128]{2,1,0:T(8,128)(2,1)}), bf16[16,320,128]{2,1,0:T(8,128)(2,1)}, u32[]{:S(2)}, u32[]{:S(2)}) async-start(bf16[16,320,128]{2,1,0:T(8,128)(2,1)} %copy-done), calls=%async_computation.5 | async-start | bytes 2621440 | tf_op jit(solution)/shard_map/all_to_all | solution.py:410
  137.0 1.3 copy-start.1
  138.4 1.7 copy-start.4
  151.7 11.9 %collective-permute-start.2 = (bf16[4,2,640,128]{3,2,1,0:T(8,128)(2,1)}, bf16[4,2,640,128]{3,2,1,0:T(8,128)(2,1)}, u32[]{:S(2)}, u32[]{:S(2)}) collective-permute-start(bf16[4,2,640,128]{3,2,1,0:T(8,128)(2,1)} %bitcast.27.own_ref), channel_id=1, source_target_pairs={{0,8},{8,0},{1,9},{9,1},{2,10},{10,2},{3,11},{11,3},{4,12},{12,4},... | collective-permute-start | bytes 3932168 | tf_op jit(solution)/shard_map/ppermute | solution.py:412
  177.4 18.2 %all-to-all-start.7 = ((f32[16,8,128]{2,1,0:T(8,128)}), f32[16,8,128]{2,1,0:T(8,128)S(1)}, u32[]{:S(2)}, u32[]{:S(2)}) async-start(f32[16,8,128]{2,1,0:T(8,128)} %merge.1), calls=%async_computation.7 | async-start | bytes 131072 | tf_op jit(solution)/shard_map/all_to_all | solution.py:428
  (2 other events, 1.5 us)

commit v4 on v3

--- a/solution.py
+++ b/solution.py
@@ -71,12 +71,32 @@
     single.wait()
 
 
-def spread_kernel(at_ref, near_ref, far_ref, out_ref, sems):
+def spread_kernel(near_ref, out_ref, sems):
+    send_copies(near_ref, out_ref, sems)
+
+
+def spread_far_kernel(at_ref, *refs):
+    out_ref, sems = refs[-2:]
     copies = []
     for i in range(4):
-        for j, (ref, half) in enumerate(((near_ref, at_ref[0]), (far_ref, 1 - at_ref[0]))):
-            target = out_ref.at[i, pl.ds(half * 4, 4)]
-            copies.append(pltpu.make_async_copy(ref, target, sems.at[2 * i + j]))
+        for k in range(4):
+            copies.append(
+                pltpu.make_async_copy(refs[k], out_ref.at[i, jnp.bitwise_xor(at_ref[0], k)], sems.at[i * 4 + k])
+            )
+    for copy in copies:
+        copy.start()
+    for copy in copies:
+        copy.wait()
+
+
+def collect(half, near_far, held, sems):
+    copies = []
+    for i, (near_ref, far_ref) in enumerate(near_far):
+        for x in range(4):
+            for j, ref in enumerate((near_ref, far_ref)):
+                at = x * 8 + (half * 4 if j == 0 else (1 - half) * 4)
+                target = held.at[i, pl.ds(pl.multiple_of(at, 4), 4)]
+                copies.append(pltpu.make_async_copy(ref.at[x], target, sems.at[i * 8 + x * 2 + j]))
     for copy in copies:
         copy.start()
     for copy in copies:
@@ -141,9 +161,11 @@
     return acc / total
 
 
-def scored_kernel(core_ref, first_ref, low_ref, high_ref, own_ref, other_ref, w_ref, *refs):
-    out_ref, rows, scored = refs[-5:-2]
+def scored_kernel(core_ref, first_ref, low_ref, high_ref, near, far, near_other, far_other, w_ref, *refs):
+    out_ref, rows, scored, held, sems = refs[-7:-2]
     core = core_ref[0]
+    collect(core_ref[1], ((near, far), (near_other, far_other)), held, sems)
+    own_ref, other_ref = held.at[0], held.at[1]
     for t in range(8):
         q = jnp.concatenate(
             (
@@ -177,8 +199,10 @@
             ]
 
 
-def context_kernel(start_head, at_ref, low_ref, high_ref, own_ref, other_ref, q_ref, *refs):
-    out_ref = refs[-3]
+def context_kernel(start_head, at_ref, low_ref, high_ref, near, far, near_other, far_other, q_ref, *refs):
+    out_ref, held, sems = refs[-5:-2]
+    collect(at_ref[3], ((near, far), (near_other, far_other)), held, sems)
+    own_ref, other_ref = held.at[0], held.at[1]
     heads = range(start_head, start_head + 4)
     q = jnp.concatenate([q_ref[:, h * 128 : (h + 1) * 128] for h in heads], axis=0)
     low, high = jnp.tile(low_ref[...], (1, 4)), jnp.tile(high_ref[...], (1, 4))
@@ -269,7 +293,7 @@
         in_specs=specs,
         out_specs=out if more is None else (out, out),
         scratch_shapes=list(scratch),
-        compiler_params=pltpu.CompilerParams(vmem_limit_bytes=vmem * 2**20),
+        compiler_params=pltpu.CompilerParams(vmem_limit_bytes=int(vmem * 2**20)),
         cost_estimate=pl.CostEstimate(flops=flops, bytes_accessed=size, transcendentals=0),
         name=name,
     )
@@ -314,12 +338,29 @@
         ],
         name="pack",
         out=ANY,
+        vmem=63.9,
         more=jax.ShapeDtypeStruct((4, BLOCK, 128), jnp.bfloat16),
     )(slab[None], slabs, queries, keys, values)
     block = lax.ppermute(block, ("zh", "zl"), [(i, i ^ 4) for i in range(8)])
     near = lax.all_to_all(packed, "zl", 0, 0)
-    near, block = lax.optimization_barrier((near, block))
-    far = lax.all_to_all(jnp.broadcast_to(block[None], (4, BLOCK, 128)), "zl", 0, 0)
+    spread = call(
+        spread_kernel, (4, 4, BLOCK, 128), jnp.bfloat16, [VMEM], [pltpu.SemaphoreType.DMA((4,))], name="spread", out=ANY
+    )(near)
+    spread, block = lax.optimization_barrier((spread, block))
+    near = lax.all_to_all(spread, "x", 0, 0)
+    blocks = [block] + [lax.ppermute(block, "zl", [(i, i ^ k) for i in range(4)]) for k in (1, 2, 3)]
+    spread = call(
+        spread_far_kernel,
+        (4, 4, BLOCK, 128),
+        jnp.bfloat16,
+        [SMEM] + [VMEM] * 4,
+        [pltpu.SemaphoreType.DMA((16,))],
+        name="spread_far",
+        out=ANY,
+    )(lax.axis_index("zl")[None], *blocks)
+    near, spread = lax.optimization_barrier((near, spread))
+    far = lax.all_to_all(spread, "x", 0, 0)
+    near_other = lax.ppermute(near, "c", [(0, 1), (1, 0)])
 
     bounds = jnp.cumsum(doc_lengths)
     position = jnp.arange(64 * SLAB, dtype=jnp.int32)
@@ -339,7 +380,8 @@
     low = columns(pick(begin))
     ids = pick(sampled_ids).reshape(CHIPS, 2, SCORED).transpose(1, 0, 2).reshape(2, 128)
     first = jnp.min(low, axis=1) // 256
-    core_at = core[None]
+    half = lax.axis_index("zh")
+    core_at = jnp.stack((core, half))
 
     source = jnp.asarray(source_columns())
     weight = call(weight_kernel, (256, D), jnp.bfloat16, [VMEM] * 3, flops=2 * 256 * D * 1280, name="weight", vmem=28)(
@@ -351,46 +393,38 @@
 
     own_begin = lax.dynamic_slice_in_dim(begin, slab * SLAB, SLAB, 0)
     own_position = slab * SLAB + jnp.arange(SLAB, dtype=jnp.int32)
-    at = jnp.stack((core, own_begin[0] // 256, chip))
+    at = jnp.stack((core, own_begin[0] // 256, chip, half))
     base = ((slab * 2 + h) * 4 + y) * 256
 
-    spread = call(
-        spread_kernel,
-        (4, 8, BLOCK, 128),
-        jnp.bfloat16,
-        [SMEM, VMEM, VMEM],
-        [pltpu.SemaphoreType.DMA((8,))],
-        name="spread",
-        out=ANY,
-    )(lax.axis_index("zh")[None], near, far)
-    own = lax.all_to_all(spread, "x", 0, 0).reshape(CHIPS, BLOCK, 128)
-    own, weight, mine, low, high, first, ids, own_begin = lax.optimization_barrier(
-        (own, weight, mine, low, high, first, ids, own_begin)
-    )
-    other = lax.ppermute(own, "c", [(0, 1), (1, 0)])
+    far, near_other, weight, mine, low, high, first, ids, own_begin = lax.optimization_barrier(
+        (far, near_other, weight, mine, low, high, first, ids, own_begin)
+    )
+    far_other = lax.ppermute(far, "c", [(0, 1), (1, 0)])
+    blocks = (near, far, near_other, far_other)
+    held = [pltpu.VMEM((2, CHIPS, BLOCK, 128), jnp.bfloat16), pltpu.SemaphoreType.DMA((16,))]
     scores = pltpu.VMEM((2 * GROUP * SLAB, 256), jnp.float32)
     parts = call(
         scored_kernel,
         (4, HALF, 128),
         jnp.float32,
-        [SMEM, SMEM] + [VMEM] * 5,
-        [pltpu.VMEM((256, 128), jnp.float32), pltpu.VMEM((256, 1024), jnp.bfloat16), scores, scores],
+        [SMEM, SMEM, VMEM, VMEM] + [ANY] * 4 + [VMEM],
+        [pltpu.VMEM((256, 128), jnp.float32), pltpu.VMEM((256, 1024), jnp.bfloat16)] + held + [scores, scores],
         name="scored",
         vmem=28,
-    )(core_at, first, low, high, own, other, out_weight)
+    )(core_at, first, low, high, *blocks, out_weight)
 
     def context_of(start_head, after):
         return call(
             functools.partial(context_kernel, start_head),
             (SLAB, 512),
             jnp.bfloat16,
-            [SMEM] + [VMEM] * 5 + [ANY],
-            [pltpu.VMEM((2 * GROUP * SLAB, 512), jnp.float32)] * 2,
+            [SMEM, VMEM, VMEM] + [ANY] * 4 + [VMEM, ANY],
+            held + [pltpu.VMEM((2 * GROUP * SLAB, 512), jnp.float32)] * 2,
             flops=4 * 1024 * 4224 * 128,
             size=6 * 2**20,
             name="context",
             vmem=28,
-        )(at, own_begin[None, :], own_position[None, :], own, other, queries, after)
+        )(at, own_begin[None, :], own_position[None, :], *blocks, queries, after)
 
     parts = lax.all_to_all(parts, "y", 0, 0)
     block = pltpu.VMEM((HALF, 128), jnp.bfloat16)

time: 198 us -> 195 us (0.985)
  waiting for transfers between devices: 53.7 us -> 41.1 us
  starting transfers between devices: 67.8 us -> 76.8 us
  Pallas kernels: 38 us -> 43.4 us
  local copies, waits for them, and re-layouts: 14.4 us -> 9.04 us
    ppermute x1 -> x5, starting transfers between devices: 7.49 us -> 21 us  [the longest x3 14.1 us: body(): lax.ppermute(block, 'zl', [(i, i ^ k) for i in range(4)])]
    all_to_all x2, waiting for transfers between devices: 20.7 us -> 8.99 us  [the longest x1 8.99 us: body(): far = lax.all_to_all(spread, 'x', 0, 0)]
    all_to_all x2, starting transfers between devices: 14.2 us -> 8.8 us  [the longest x1 4.52 us: body(): far = lax.all_to_all(spread, 'x', 0, 0)]
    unnamed x36 -> x30, local copies, waits for them, and re-layouts: 11 us -> 6.94 us
    pallas_call x2, Pallas kernels: 6.49 us -> 8.52 us  [context_of(): call(functools.partial(context_kernel, start_head), (SLAB, 512), jnp.bflo...]
    pallas_call x2 -> x3, Pallas kernels: 19.3 us -> 21.1 us  [the longest x1 18.9 us: body(): call(scored_kernel, (4, HALF, 128), jnp.float32, [SMEM, SMEM, VMEM, VMEM]...]
    ppermute x1 -> x5, waiting for transfers between devices: 4.35 us -> 5.64 us  [the longest x3 3.06 us: body(): lax.ppermute(block, 'zl', [(i, i ^ k) for i in range(4)])]
  transfers between devices with their start and end apart: 9 -> 13, of which waited for: 8 -> 9; matrix products, arithmetic and copies ran while one was open for 3% -> 2% of each run, Pallas kernels for 6% -> 9%
where the time goes in v4:
time: 195 us; the launch traced here: 193 us
  starting transfers between devices  76.8 us (39%)
  Pallas kernels  43.4 us (22%)
  waiting for transfers between devices  41.1 us (21%)
  blocking collectives  19.4 us (10%)
  local copies, waits for them, and re-layouts  9.04 us (5%)
  other arithmetic  2.16 us (1%)
    pallas_call x1, Pallas kernels, body(): call(scored_kernel, (4, HALF, 128), jnp.float32, [SMEM, SMEM, VMEM, VMEM]...  18.9 us
    ppermute x3, starting transfers between devices, body(): lax.ppermute(block, 'zl', [(i, i ^ k) for i in range(4)])  14.1 us
    all_to_all x1, blocking collectives, body(): tiles = lax.all_to_all(tiles, ('x', 'y', 'c'), 0, 0)  10.9 us
    all_to_all x1, waiting for transfers between devices, body(): tiles = lax.all_to_all(tiles, ('h', 'zh', 'zl'), 0, 0)  10.8 us
    all_to_all x1, starting transfers between devices, body(): sums = lax.all_to_all(sums, ('h', 'zh', 'zl'), 0, 0)  10.2 us
    all_to_all x1, waiting for transfers between devices, body(): far = lax.all_to_all(spread, 'x', 0, 0)  8.99 us
    ppermute x1, starting transfers between devices, body(): hidden_other = lax.ppermute(hidden, 'c', [(0, 1), (1, 0)])  8.9 us
    ppermute x1, starting transfers between devices, body(): block = lax.ppermute(block, ('zh', 'zl'), [(i, i ^ 4) for i in range(8)])  8.8 us
  transfers between devices with their start and end apart: 13, of which 9 were waited for; matrix products, arithmetic and copies ran while one was open for 2% of the time, Pallas kernels for 9%

profile of v4, /device:TPU:1, one launch (start us, length us, event | category | flops | bytes accessed | tf_op | source)
XLA Modules:
  0.0 193.4 jit_solution(11170730254979738025)
XLA Ops:
  0.7 2.7 %pack.1 = (bf16[288,128]{1,0:T(8,128)(2,1)}, bf16[4,288,128]{2,1,0:T(8,128)(2,1)}) custom-call(s32[1]{0:T(128)} %bitcast.6.at_ref, s32[64,128]{1,0:T(8,128)} %bitcast.72, bf16[128,1024]{1,0:T(8,128)(2,1)} %q_ref.5, bf16[128,128]{1,0:T(8,128)(2,1)} %k_ref.1, bf16[128,128]{1,0:T(8,128)(2,1)} %v_ref.1), custom_call_target="tpu_custom_call" | custom-call | tf_op jit(solution)/shard_map/pack/pallas_call | solution.py:328
  3.3 6.5 %all-to-all-start = ((bf16[4,288,128]{2,1,0:T(8,128)(2,1)}), bf16[4,288,128]{2,1,0:T(8,128)(2,1)S(1)}, u32[]{:S(2)}, u32[]{:S(2)}) async-start(bf16[4,288,128]{2,1,0:T(8,128)(2,1)} %get-tuple-element.21), calls=%async_computation | async-start | bytes 589824 | tf_op jit(solution)/shard_map/all_to_all | solution.py:345
  9.8 8.8 %collective-permute-start = (bf16[288,128]{1,0:T(8,128)(2,1)}, bf16[288,128]{1,0:T(8,128)(2,1)S(1)}, u32[]{:S(2)}, u32[]{:S(2)}) collective-permute-start(bf16[288,128]{1,0:T(8,128)(2,1)} %get-tuple-element.22), channel_id=1, source_target_pairs={{0,64},{16,80},{32,96},{48,112},{64,0},{80,16},{96,32},{112,48},{1... | collective-permute-start | bytes 221192 | tf_op jit(solution)/shard_map/ppermute | solution.py:344
  20.7 4.3 %all-to-all-start.1 = ((bf16[4,4,288,128]{3,2,1,0:T(8,128)(2,1)}), bf16[4,4,288,128]{3,2,1,0:T(8,128)(2,1)}, u32[]{:S(2)}, u32[]{:S(2)}) async-start(bf16[4,4,288,128]{3,2,1,0:T(8,128)(2,1)} %spread.1), calls=%async_computation.1 | async-start | bytes 2359296 | tf_op jit(solution)/shard_map/all_to_all | solution.py:350
  25.7 9.7 %collective-permute-start.3 = (bf16[288,128]{1,0:T(8,128)(2,1)S(1)}, bf16[288,128]{1,0:T(8,128)(2,1)S(1)}, u32[]{:S(2)}, u32[]{:S(2)}) collective-permute-start(bf16[288,128]{1,0:T(8,128)(2,1)S(1)} %collective-permute-done.refs_0_), channel_id=1, source_target_pairs={{0,48},{16,32},{32,16},{48,0},{1,49},{17,33},{33,17},{49,1},{2,50}... | collective-permute-start | bytes 221192 | tf_op jit(solution)/shard_map/ppermute | solution.py:351
  45.0 4.0 %collective-permute-start.4 = (bf16[4,4,288,128]{3,2,1,0:T(8,128)(2,1)}, bf16[4,4,288,128]{3,2,1,0:T(8,128)(2,1)}, u32[]{:S(2)}, u32[]{:S(2)}) collective-permute-start(bf16[4,4,288,128]{3,2,1,0:T(8,128)(2,1)} %all-to-all-done.1.near), channel_id=1, source_target_pairs={{0,8},{8,0},{1,9},{9,1},{2,10},{10,2},{3,11},{11,3},{4,12},{12,4},... | collective-permute-start | bytes 3538952 | tf_op jit(solution)/shard_map/ppermute | solution.py:363
  49.0 4.5 %all-to-all-start.2 = ((bf16[4,4,288,128]{3,2,1,0:T(8,128)(2,1)}), bf16[4,4,288,128]{3,2,1,0:T(8,128)(2,1)}, u32[]{:S(2)}, u32[]{:S(2)}) async-start(bf16[4,4,288,128]{3,2,1,0:T(8,128)(2,1)} %spread_far.1), calls=%async_computation.2 | async-start | bytes 2359296 | tf_op jit(solution)/shard_map/all_to_all | solution.py:362
  57.3 3.7 %weight.1.w_ref = bf16[256,5120]{1,0:T(8,128)(2,1)S(1)} custom-call(s32[1,1280]{1,0:T(1,128)S(1)} %copy-done.9, f32[1,5120]{1,0:T(1,128)S(1)} %bitcast.54, bf16[256,5120]{1,0:T(8,128)(2,1)S(1)} %copy-done.7), custom_call_target="tpu_custom_call" | custom-call | flops 3355443200 | tf_op jit(solution)/shard_map/weight/pallas_call | solution.py:387
  61.0 9.0 %all-to-all-done.2.far = bf16[4,4,288,128]{3,2,1,0:T(8,128)(2,1)} async-done(((bf16[4,4,288,128]{3,2,1,0:T(8,128)(2,1)}), bf16[4,4,288,128]{3,2,1,0:T(8,128)(2,1)}, u32[]{:S(2)}, u32[]{:S(2)}) %all-to-all-start.2) | async-done | bytes 1179680 | tf_op jit(solution)/shard_map/all_to_all | solution.py:362
  70.0 3.0 %collective-permute-start.5 = (bf16[4,4,288,128]{3,2,1,0:T(8,128)(2,1)}, bf16[4,4,288,128]{3,2,1,0:T(8,128)(2,1)S(1)}, u32[]{:S(2)}, u32[]{:S(2)}) collective-permute-start(bf16[4,4,288,128]{3,2,1,0:T(8,128)(2,1)} %all-to-all-done.2.far), channel_id=1, source_target_pairs={{0,8},{8,0},{1,9},{9,1},{2,10},{10,2},{3,11},{11,3},{4,12},{12,4},... | collective-permute-start | bytes 3538952 | tf_op jit(solution)/shard_map/ppermute | solution.py:402
  73.1 2.6 %collective-permute-done.5.far_other = bf16[4,4,288,128]{3,2,1,0:T(8,128)(2,1)S(1)} collective-permute-done((bf16[4,4,288,128]{3,2,1,0:T(8,128)(2,1)}, bf16[4,4,288,128]{3,2,1,0:T(8,128)(2,1)S(1)}, u32[]{:S(2)}, u32[]{:S(2)}) %collective-permute-start.5) | collective-permute-done | bytes 1179680 | tf_op jit(solution)/shard_map/ppermute | solution.py:402
  75.7 18.9 %scored.1 = f32[4,40,128]{2,1,0:T(8,128)S(1)} custom-call(s32[2]{0:T(128)S(1)} %pad_add_fusion.1.core_ref, s32[8]{0:T(128)S(1)} %and_select_fusion.first_ref, s32[8,256]{1,0:T(8,128)S(1)} %reshape.117.low_ref, s32[8,256]{1,0:T(8,128)S(1)} %reshape.124.high_ref, bf16[4,4,288,128]{3,2,1,0:T(8,128)(2,1)} %all-to-all-done.1.near, ...), custom_call_target="tpu_custom_call" | custom-call | tf_op jit(solution)/shard_map/scored/pallas_call | solution.py:406
  94.6 8.6 %all_to_all.40.parts_ref = f32[4,40,128]{2,1,0:T(8,128)S(1)} all-to-all(f32[4,40,128]{2,1,0:T(8,128)S(1)} %scored.1), channel_id=1, replica_groups=mesh['x'=4,'zh'=2,'zl'=4,'c'=2,'h'=2,'y'=4] {'y'}, dimensions={0} | all-to-all | bytes 163840 | tf_op jit(solution)/shard_map/all_to_all | solution.py:429
  104.0 10.2 %all-to-all-start.4 = ((bf16[16,40,128]{2,1,0:T(8,128)(2,1)}), bf16[16,40,128]{2,1,0:T(8,128)(2,1)S(1)}, u32[]{:S(2)}, u32[]{:S(2)}) async-start(bf16[16,40,128]{2,1,0:T(8,128)(2,1)} %add.77.refs_0_), calls=%async_computation.4 | async-start | bytes 327680 | tf_op jit(solution)/shard_map/all_to_all | solution.py:441
  115.7 4.3 %context.2.dep_ref = bf16[128,512]{1,0:T(8,128)(2,1)S(1)} custom-call(s32[4]{0:T(128)S(1)} %pad_add_fusion.at_ref, s32[1,128]{1,0:T(1,128)S(1)} %bitcast.52, s32[1,128]{1,0:T(1,128)S(1)} %iota_add_fusion.high_ref, bf16[4,4,288,128]{3,2,1,0:T(8,128)(2,1)} %all-to-all-done.1.near, bf16[4,4,288,128]{3,2,1,0:T(8,128)(2,1)} %all-to-all-done.2.far, ...), custom_call_target="tpu_custom_call" | custom-call | flops 2214592512 | bytes 6291456 | tf_op jit(solution)/shard_map/context/pallas_call | solution.py:417
  119.9 6.4 %all-to-all-done.4.parts_ref = bf16[16,40,128]{2,1,0:T(8,128)(2,1)S(1)} async-done(((bf16[16,40,128]{2,1,0:T(8,128)(2,1)}), bf16[16,40,128]{2,1,0:T(8,128)(2,1)S(1)}, u32[]{:S(2)}, u32[]{:S(2)}) %all-to-all-start.4) | async-done | bytes 163872 | tf_op jit(solution)/shard_map/all_to_all | solution.py:441
  127.5 4.4 %all-to-all-start.5 = ((bf16[16,320,128]{2,1,0:T(8,128)(2,1)}), bf16[16,320,128]{2,1,0:T(8,128)(2,1)}, u32[]{:S(2)}, u32[]{:S(2)}) async-start(bf16[16,320,128]{2,1,0:T(8,128)(2,1)} %copy-done), calls=%async_computation.5 | async-start | bytes 2621440 | tf_op jit(solution)/shard_map/all_to_all | solution.py:444
  134.6 4.3 %context.3.dep_ref = bf16[128,512]{1,0:T(8,128)(2,1)S(1)} custom-call(s32[4]{0:T(128)S(1)} %pad_add_fusion.at_ref, s32[1,128]{1,0:T(1,128)S(1)} %bitcast.53, s32[1,128]{1,0:T(1,128)S(1)} %iota_add_fusion.high_ref, bf16[4,4,288,128]{3,2,1,0:T(8,128)(2,1)} %all-to-all-done.1.near, bf16[4,4,288,128]{3,2,1,0:T(8,128)(2,1)} %all-to-all-done.2.far, ...), custom_call_target="tpu_custom_call" | custom-call | flops 2214592512 | bytes 6291456 | tf_op jit(solution)/shard_map/context/pallas_call | solution.py:417
  138.8 7.7 %all-to-all-done.5 = bf16[16,320,128]{2,1,0:T(8,128)(2,1)} async-done(((bf16[16,320,128]{2,1,0:T(8,128)(2,1)}), bf16[16,320,128]{2,1,0:T(8,128)(2,1)}, u32[]{:S(2)}, u32[]{:S(2)}) %all-to-all-start.5) | async-done | bytes 1310752 | tf_op jit(solution)/shard_map/all_to_all | solution.py:444
  146.6 8.9 %collective-permute-start.6 = (bf16[4,2,640,128]{3,2,1,0:T(8,128)(2,1)}, bf16[4,2,640,128]{3,2,1,0:T(8,128)(2,1)}, u32[]{:S(2)}, u32[]{:S(2)}) collective-permute-start(bf16[4,2,640,128]{3,2,1,0:T(8,128)(2,1)} %bitcast.27.own_ref), channel_id=1, source_target_pairs={{0,8},{8,0},{1,9},{9,1},{2,10},{10,2},{3,11},{11,3},{4,12},{12,4},... | collective-permute-start | bytes 3932168 | tf_op jit(solution)/shard_map/ppermute | solution.py:446
  158.5 2.3 %logits.1 = f32[32,8,128]{2,1,0:T(8,128)S(1)} custom-call(s32[2]{0:T(128)S(1)} %pad_add_fusion.3.at_ref, s32[2,128]{1,0:T(2,128)S(1)} %reshape.126.ids_ref, f32[2,256,128]{2,1,0:T(8,128)S(1)} %get-tuple-element.38.sum_ref, f32[2,8,128]{2,1,0:T(8,128)S(1)} %get-tuple-element.39.square_ref, bf16[4,2,640,128]{3,2,1,0:T(8,128)(2,1)} %collective-permute-done.6.other_ref, ...), custom_call_target="tpu_custom_call" | custom-call | tf_op jit(solution)/shard_map/logits/pallas_call | solution.py:456
  160.7 10.9 %all_to_all.41.parts_ref = f32[32,8,128]{2,1,0:T(8,128)S(1)} all-to-all(f32[32,8,128]{2,1,0:T(8,128)S(1)} %logits.1), channel_id=1, replica_groups=mesh['x'=4,'zh'=2,'zl'=4,'c'=2,'h'=2,'y'=4] {'x','y','c'}, dimensions={0} | all-to-all | bytes 262144 | tf_op jit(solution)/shard_map/all_to_all | solution.py:460
  172.3 8.3 %all-to-all-start.7 = ((f32[16,8,128]{2,1,0:T(8,128)}), f32[16,8,128]{2,1,0:T(8,128)S(1)}, u32[]{:S(2)}, u32[]{:S(2)}) async-start(f32[16,8,128]{2,1,0:T(8,128)} %merge.1), calls=%async_computation.7 | async-start | bytes 131072 | tf_op jit(solution)/shard_map/all_to_all | solution.py:462
  181.4 10.8 %all-to-all-done.7.parts_ref = f32[16,8,128]{2,1,0:T(8,128)S(1)} async-done(((f32[16,8,128]{2,1,0:T(8,128)}), f32[16,8,128]{2,1,0:T(8,128)S(1)}, u32[]{:S(2)}, u32[]{:S(2)}) %all-to-all-start.7) | async-done | bytes 65568 | tf_op jit(solution)/shard_map/all_to_all | solution.py:462
  (86 shorter events, 27.6 us)
Async XLA Ops:
  3.3 15.3 %all-to-all-start = ((bf16[4,288,128]{2,1,0:T(8,128)(2,1)}), bf16[4,288,128]{2,1,0:T(8,128)(2,1)S(1)}, u32[]{:S(2)}, u32[]{:S(2)}) async-start(bf16[4,288,128]{2,1,0:T(8,128)(2,1)} %get-tuple-element.21), calls=%async_computation | async-start | bytes 589824 | tf_op jit(solution)/shard_map/all_to_all | solution.py:345
  9.8 10.9 %collective-permute-start = (bf16[288,128]{1,0:T(8,128)(2,1)}, bf16[288,128]{1,0:T(8,128)(2,1)S(1)}, u32[]{:S(2)}, u32[]{:S(2)}) collective-permute-start(bf16[288,128]{1,0:T(8,128)(2,1)} %get-tuple-element.22), channel_id=1, source_target_pairs={{0,64},{16,80},{32,96},{48,112},{64,0},{80,16},{96,32},{112,48},{1... | collective-permute-start | bytes 221192 | tf_op jit(solution)/shard_map/ppermute | solution.py:344
  19.7 5.3 %copy-start.13 = (s32[32]{0:T(128)S(1)}, s32[32]{0:T(128)}, u32[]{:S(2)}) copy-start(s32[32]{0:T(128)} %param.20) | copy-start | bytes 388
  19.7 5.8 %copy-start.12 = (s32[8192]{0:T(1024)S(1)}, s32[8192]{0:T(1024)}, u32[]{:S(2)}) copy-start(s32[8192]{0:T(1024)} %param.19) | copy-start | bytes 98308
  19.7 20.1 %copy-start.11 = (s32[8192]{0:T(1024)S(1)}, s32[8192]{0:T(1024)}, u32[]{:S(2)}) copy-start(s32[8192]{0:T(1024)} %param.18) | copy-start | bytes 98308
  19.7 20.7 %copy-start.10 = (bf16[80,256]{1,0:T(8,128)(2,1)S(1)}, bf16[80,256]{1,0:T(8,128)(2,1)}, u32[]{:S(2)}) copy-start(bf16[80,256]{1,0:T(8,128)(2,1)} %param.15) | copy-start | bytes 122884
  20.7 24.3 %all-to-all-start.1 = ((bf16[4,4,288,128]{3,2,1,0:T(8,128)(2,1)}), bf16[4,4,288,128]{3,2,1,0:T(8,128)(2,1)}, u32[]{:S(2)}, u32[]{:S(2)}) async-start(bf16[4,4,288,128]{3,2,1,0:T(8,128)(2,1)} %spread.1), calls=%async_computation.1 | async-start | bytes 2359296 | tf_op jit(solution)/shard_map/all_to_all | solution.py:350
  25.7 15.0 %collective-permute-start.3 = (bf16[288,128]{1,0:T(8,128)(2,1)S(1)}, bf16[288,128]{1,0:T(8,128)(2,1)S(1)}, u32[]{:S(2)}, u32[]{:S(2)}) collective-permute-start(bf16[288,128]{1,0:T(8,128)(2,1)S(1)} %collective-permute-done.refs_0_), channel_id=1, source_target_pairs={{0,48},{16,32},{32,16},{48,0},{1,49},{17,33},{33,17},{49,1},{2,50}... | collective-permute-start | bytes 221192 | tf_op jit(solution)/shard_map/ppermute | solution.py:351
  35.4 7.2 %collective-permute-start.2 = (bf16[288,128]{1,0:T(8,128)(2,1)S(1)}, bf16[288,128]{1,0:T(8,128)(2,1)S(1)}, u32[]{:S(2)}, u32[]{:S(2)}) collective-permute-start(bf16[288,128]{1,0:T(8,128)(2,1)S(1)} %collective-permute-done.refs_0_), channel_id=1, source_target_pairs={{0,32},{16,48},{32,0},{48,16},{1,33},{17,49},{33,1},{49,17},{2,34}... | collective-permute-start | bytes 221192 | tf_op jit(solution)/shard_map/ppermute | solution.py:351
  37.6 6.2 %collective-permute-start.1 = (bf16[288,128]{1,0:T(8,128)(2,1)S(1)}, bf16[288,128]{1,0:T(8,128)(2,1)S(1)}, u32[]{:S(2)}, u32[]{:S(2)}) collective-permute-start(bf16[288,128]{1,0:T(8,128)(2,1)S(1)} %collective-permute-done.refs_0_), channel_id=1, source_target_pairs={{0,16},{16,0},{32,48},{48,32},{1,17},{17,1},{33,49},{49,33},{2,18}... | collective-permute-start | bytes 221192 | tf_op jit(solution)/shard_map/ppermute | solution.py:351
  45.0 25.0 %collective-permute-start.4 = (bf16[4,4,288,128]{3,2,1,0:T(8,128)(2,1)}, bf16[4,4,288,128]{3,2,1,0:T(8,128)(2,1)}, u32[]{:S(2)}, u32[]{:S(2)}) collective-permute-start(bf16[4,4,288,128]{3,2,1,0:T(8,128)(2,1)} %all-to-all-done.1.near), channel_id=1, source_target_pairs={{0,8},{8,0},{1,9},{9,1},{2,10},{10,2},{3,11},{11,3},{4,12},{12,4},... | collective-permute-start | bytes 3538952 | tf_op jit(solution)/shard_map/ppermute | solution.py:363
  49.0 6.5 %copy-start.8 = (f32[5120]{0:T(1024)S(1)}, f32[5120]{0:T(1024)}, u32[]{:S(2)}) copy-start(f32[5120]{0:T(1024)} %param.16) | copy-start | bytes 61444
  49.0 6.5 %copy-start.9 = (s32[1,1280]{1,0:T(1,128)S(1)}, s32[1,1280]{1,0:T(1,128)}, u32[]{:S(2)}) copy-start(s32[1,1280]{1,0:T(1,128)} %constant.87.clone.source_ref) | copy-start | bytes 15364
  49.0 21.0 %all-to-all-start.2 = ((bf16[4,4,288,128]{3,2,1,0:T(8,128)(2,1)}), bf16[4,4,288,128]{3,2,1,0:T(8,128)(2,1)}, u32[]{:S(2)}, u32[]{:S(2)}) async-start(bf16[4,4,288,128]{3,2,1,0:T(8,128)(2,1)} %spread_far.1), calls=%async_computation.2 | async-start | bytes 2359296 | tf_op jit(solution)/shard_map/all_to_all | solution.py:362
  55.5 1.7 copy-start.7
  57.3 18.4 %copy-start.6 = (bf16[80,1024]{1,0:T(8,128)(2,1)S(1)}, bf16[80,1024]{1,0:T(8,128)(2,1)}, u32[]{:S(2)}) copy-start(bf16[80,1024]{1,0:T(8,128)(2,1)} %w_ref.3) | copy-start | bytes 491524
  70.0 5.7 %collective-permute-start.5 = (bf16[4,4,288,128]{3,2,1,0:T(8,128)(2,1)}, bf16[4,4,288,128]{3,2,1,0:T(8,128)(2,1)S(1)}, u32[]{:S(2)}, u32[]{:S(2)}) collective-permute-start(bf16[4,4,288,128]{3,2,1,0:T(8,128)(2,1)} %all-to-all-done.2.far), channel_id=1, source_target_pairs={{0,8},{8,0},{1,9},{9,1},{2,10},{10,2},{3,11},{11,3},{4,12},{12,4},... | collective-permute-start | bytes 3538952 | tf_op jit(solution)/shard_map/ppermute | solution.py:402
  73.1 41.3 %copy-start.5 = (bf16[128,1024]{1,0:T(8,128)(2,1)S(1)}, bf16[128,1024]{1,0:T(8,128)(2,1)}, u32[]{:S(2)}) copy-start(bf16[128,1024]{1,0:T(8,128)(2,1)} %q_ref.5) | copy-start | bytes 786436
  75.7 18.9 %copy-start.2 = (bf16[4,4,288,128]{3,2,1,0:T(8,128)(2,1)}, bf16[4,4,288,128]{3,2,1,0:T(8,128)(2,1)S(1)}, u32[]{:S(2)}) copy-start(bf16[4,4,288,128]{3,2,1,0:T(8,128)(2,1)S(1)} %collective-permute-done.5.far_other) | copy-start | bytes 3538948
  104.0 22.4 %all-to-all-start.4 = ((bf16[16,40,128]{2,1,0:T(8,128)(2,1)}), bf16[16,40,128]{2,1,0:T(8,128)(2,1)S(1)}, u32[]{:S(2)}, u32[]{:S(2)}) async-start(bf16[16,40,128]{2,1,0:T(8,128)(2,1)} %add.77.refs_0_), calls=%async_computation.4 | async-start | bytes 327680 | tf_op jit(solution)/shard_map/all_to_all | solution.py:441
  127.5 19.0 %all-to-all-start.5 = ((bf16[16,320,128]{2,1,0:T(8,128)(2,1)}), bf16[16,320,128]{2,1,0:T(8,128)(2,1)}, u32[]{:S(2)}, u32[]{:S(2)}) async-start(bf16[16,320,128]{2,1,0:T(8,128)(2,1)} %copy-done), calls=%async_computation.5 | async-start | bytes 2621440 | tf_op jit(solution)/shard_map/all_to_all | solution.py:444
  131.9 1.3 copy-start.1
  146.6 11.9 %collective-permute-start.6 = (bf16[4,2,640,128]{3,2,1,0:T(8,128)(2,1)}, bf16[4,2,640,128]{3,2,1,0:T(8,128)(2,1)}, u32[]{:S(2)}, u32[]{:S(2)}) collective-permute-start(bf16[4,2,640,128]{3,2,1,0:T(8,128)(2,1)} %bitcast.27.own_ref), channel_id=1, source_target_pairs={{0,8},{8,0},{1,9},{9,1},{2,10},{10,2},{3,11},{11,3},{4,12},{12,4},... | collective-permute-start | bytes 3932168 | tf_op jit(solution)/shard_map/ppermute | solution.py:446
  172.3 19.9 %all-to-all-start.7 = ((f32[16,8,128]{2,1,0:T(8,128)}), f32[16,8,128]{2,1,0:T(8,128)S(1)}, u32[]{:S(2)}, u32[]{:S(2)}) async-start(f32[16,8,128]{2,1,0:T(8,128)} %merge.1), calls=%async_computation.7 | async-start | bytes 131072 | tf_op jit(solution)/shard_map/all_to_all | solution.py:462
  (3 other events, 3.6 us)

commit v5 on v4

--- a/solution.py
+++ b/solution.py
@@ -71,32 +71,36 @@
     single.wait()
 
 
-def spread_kernel(near_ref, out_ref, sems):
-    send_copies(near_ref, out_ref, sems)
-
-
-def spread_far_kernel(at_ref, *refs):
+def spread_kernel(*refs):
     out_ref, sems = refs[-2:]
     copies = []
     for i in range(4):
-        for k in range(4):
-            copies.append(
-                pltpu.make_async_copy(refs[k], out_ref.at[i, jnp.bitwise_xor(at_ref[0], k)], sems.at[i * 4 + k])
-            )
+        at = 0
+        for ref in refs[:-2]:
+            count = ref.shape[0] if len(ref.shape) == 3 else 1
+            target = out_ref.at[i, pl.ds(at, count)] if len(ref.shape) == 3 else out_ref.at[i, at]
+            copies.append(pltpu.make_async_copy(ref, target, sems.at[len(copies)]))
+            at += count
     for copy in copies:
         copy.start()
     for copy in copies:
         copy.wait()
 
 
-def collect(half, near_far, held, sems):
+def collect(half, place, near_far, held, sems):
     copies = []
+
+    def add(source, i, at, count=None):
+        target = held.at[i, at] if count is None else held.at[i, pl.ds(pl.multiple_of(at, 4), count)]
+        copies.append(pltpu.make_async_copy(source, target, sems.at[len(copies)]))
+
     for i, (near_ref, far_ref) in enumerate(near_far):
         for x in range(4):
-            for j, ref in enumerate((near_ref, far_ref)):
-                at = x * 8 + (half * 4 if j == 0 else (1 - half) * 4)
-                target = held.at[i, pl.ds(pl.multiple_of(at, 4), 4)]
-                copies.append(pltpu.make_async_copy(ref.at[x], target, sems.at[i * 8 + x * 2 + j]))
+            beyond = x * 8 + (1 - half) * 4
+            add(near_ref.at[x, pl.ds(0, 4)], i, x * 8 + half * 4, 4)
+            add(near_ref.at[x, 4], i, beyond + place)
+            for k in range(1, 4):
+                add(far_ref.at[x, k - 1], i, beyond + jnp.bitwise_xor(place, k))
     for copy in copies:
         copy.start()
     for copy in copies:
@@ -164,7 +168,7 @@
 def scored_kernel(core_ref, first_ref, low_ref, high_ref, near, far, near_other, far_other, w_ref, *refs):
     out_ref, rows, scored, held, sems = refs[-7:-2]
     core = core_ref[0]
-    collect(core_ref[1], ((near, far), (near_other, far_other)), held, sems)
+    collect(core_ref[1], core_ref[2], ((near, far), (near_other, far_other)), held, sems)
     own_ref, other_ref = held.at[0], held.at[1]
     for t in range(8):
         q = jnp.concatenate(
@@ -201,7 +205,7 @@
 
 def context_kernel(start_head, at_ref, low_ref, high_ref, near, far, near_other, far_other, q_ref, *refs):
     out_ref, held, sems = refs[-5:-2]
-    collect(at_ref[3], ((near, far), (near_other, far_other)), held, sems)
+    collect(at_ref[3], at_ref[4], ((near, far), (near_other, far_other)), held, sems)
     own_ref, other_ref = held.at[0], held.at[1]
     heads = range(start_head, start_head + 4)
     q = jnp.concatenate([q_ref[:, h * 128 : (h + 1) * 128] for h in heads], axis=0)
@@ -343,24 +347,18 @@
     )(slab[None], slabs, queries, keys, values)
     block = lax.ppermute(block, ("zh", "zl"), [(i, i ^ 4) for i in range(8)])
     near = lax.all_to_all(packed, "zl", 0, 0)
-    spread = call(
-        spread_kernel, (4, 4, BLOCK, 128), jnp.bfloat16, [VMEM], [pltpu.SemaphoreType.DMA((4,))], name="spread", out=ANY
-    )(near)
-    spread, block = lax.optimization_barrier((spread, block))
-    near = lax.all_to_all(spread, "x", 0, 0)
-    blocks = [block] + [lax.ppermute(block, "zl", [(i, i ^ k) for i in range(4)]) for k in (1, 2, 3)]
-    spread = call(
-        spread_far_kernel,
-        (4, 4, BLOCK, 128),
-        jnp.bfloat16,
-        [SMEM] + [VMEM] * 4,
-        [pltpu.SemaphoreType.DMA((16,))],
-        name="spread_far",
-        out=ANY,
-    )(lax.axis_index("zl")[None], *blocks)
-    near, spread = lax.optimization_barrier((near, spread))
-    far = lax.all_to_all(spread, "x", 0, 0)
-    near_other = lax.ppermute(near, "c", [(0, 1), (1, 0)])
+
+    def spread(name, *parts):
+        count = sum(part.shape[0] if part.ndim == 3 else 1 for part in parts)
+        return call(
+            spread_kernel,
+            (4, count, BLOCK, 128),
+            jnp.bfloat16,
+            [VMEM] * len(parts),
+            [pltpu.SemaphoreType.DMA((4 * len(parts),))],
+            name=name,
+            out=ANY,
+        )(*parts)
 
     bounds = jnp.cumsum(doc_lengths)
     position = jnp.arange(64 * SLAB, dtype=jnp.int32)
@@ -381,27 +379,33 @@
     ids = pick(sampled_ids).reshape(CHIPS, 2, SCORED).transpose(1, 0, 2).reshape(2, 128)
     first = jnp.min(low, axis=1) // 256
     half = lax.axis_index("zh")
-    core_at = jnp.stack((core, half))
-
-    source = jnp.asarray(source_columns())
-    weight = call(weight_kernel, (256, D), jnp.bfloat16, [VMEM] * 3, flops=2 * 256 * D * 1280, name="weight", vmem=28)(
-        source, norm_gain[None, :], head_weight
-    )
+    place = lax.axis_index("zl")
+    core_at = jnp.stack((core, half, place))
+
     mine = residual.reshape(2, HALF, CHIPS, 2, SCORED).transpose(3, 0, 1, 2, 4).reshape(4, HALF, 128)
     mine = lax.dynamic_index_in_dim(mine, y, 0, keepdims=False).astype(jnp.float32)
     mine = jnp.where(h == 0, mine, 0.0)
 
     own_begin = lax.dynamic_slice_in_dim(begin, slab * SLAB, SLAB, 0)
     own_position = slab * SLAB + jnp.arange(SLAB, dtype=jnp.int32)
-    at = jnp.stack((core, own_begin[0] // 256, chip, half))
+    at = jnp.stack((core, own_begin[0] // 256, chip, half, place))
     base = ((slab * 2 + h) * 4 + y) * 256
 
-    far, near_other, weight, mine, low, high, first, ids, own_begin = lax.optimization_barrier(
-        (far, near_other, weight, mine, low, high, first, ids, own_begin)
-    )
+    near, low, high, first, ids, own_begin = lax.optimization_barrier((near, low, high, first, ids, own_begin))
+    near = lax.all_to_all(spread("spread_near", near, block), "x", 0, 0)
+    blocks = [lax.ppermute(block, "zl", [(i, i ^ k) for i in range(4)]) for k in (1, 2, 3)]
+    near, far = lax.optimization_barrier((near, spread("spread_far", *blocks)))
+    far = lax.all_to_all(far, "x", 0, 0)
+    source = jnp.asarray(source_columns())
+    weight = call(
+        weight_kernel, (256, D), jnp.bfloat16, [VMEM] * 3, flops=2 * 256 * D * 1280, name="weight", vmem=28
+    )(source, norm_gain[None, :], head_weight)
+    near_other = lax.ppermute(near, "c", [(0, 1), (1, 0)])
+
+    far, weight, mine = lax.optimization_barrier((far, weight, mine))
     far_other = lax.ppermute(far, "c", [(0, 1), (1, 0)])
     blocks = (near, far, near_other, far_other)
-    held = [pltpu.VMEM((2, CHIPS, BLOCK, 128), jnp.bfloat16), pltpu.SemaphoreType.DMA((16,))]
+    held = [pltpu.VMEM((2, CHIPS, BLOCK, 128), jnp.bfloat16), pltpu.SemaphoreType.DMA((40,))]
     scores = pltpu.VMEM((2 * GROUP * SLAB, 256), jnp.float32)
     parts = call(
         scored_kernel,

time: 195 us -> 197 us (1.010)
  waiting for transfers between devices: 41.1 us -> 27.2 us
  local copies, waits for them, and re-layouts: 9.04 us -> 18.2 us
  Pallas kernels: 43.4 us -> 47.8 us
    unnamed x30 -> x42, local copies, waits for them, and re-layouts: 6.94 us -> 14.7 us
    all_to_all x2, waiting for transfers between devices: 8.99 us -> 2.48 us  [the longest x1 2.48 us: body(): near = lax.all_to_all(spread('spread_near', near, block), 'x', 0, 0)]
    all_to_all x1, waiting for transfers between devices: 6.38 us -> 2.73 us  [body(): sums = lax.all_to_all(sums, ('h', 'zh', 'zl'), 0, 0)]
    ppermute x3, starting transfers between devices: 14.1 us -> 10.5 us  [body(): lax.ppermute(block, 'zl', [(i, i ^ k) for i in range(4)])]
    all_to_all x1, waiting for transfers between devices: 7.74 us -> 4.93 us  [body(): hidden = lax.all_to_all(hidden, ('x', 'y'), 0, 0).reshape(4, 2, 640, 128)]
    pallas_call x2, Pallas kernels: 8.52 us -> 11.1 us  [context_of(): call(functools.partial(context_kernel, start_head), (SLAB, 512), jnp.bflo...]
    all_to_all x1, starting transfers between devices: 10.2 us -> 12.4 us  [body(): sums = lax.all_to_all(sums, ('h', 'zh', 'zl'), 0, 0)]
  transfers between devices with their start and end apart: 13 -> 13, of which waited for: 9 -> 8; matrix products, arithmetic and copies ran while one was open for 2% -> 4% of each run, Pallas kernels for 9% -> 9%
where the time goes in v5:
time: 197 us; the launch traced here: 196 us
  starting transfers between devices  77.8 us (39%)
  Pallas kernels  47.8 us (24%)
  waiting for transfers between devices  27.2 us (14%)
  blocking collectives  19.5 us (10%)
  local copies, waits for them, and re-layouts  18.2 us (9%)
  other arithmetic  2.89 us (1%)
    pallas_call x1, Pallas kernels, body(): call(scored_kernel, (4, HALF, 128), jnp.float32, [SMEM, SMEM, VMEM, VMEM]...  20.2 us
    unnamed x42, local copies, waits for them, and re-layouts  14.7 us
    all_to_all x1, starting transfers between devices, body(): sums = lax.all_to_all(sums, ('h', 'zh', 'zl'), 0, 0)  12.4 us
    pallas_call x2, Pallas kernels, context_of(): call(functools.partial(context_kernel, start_head), (SLAB, 512), jnp.bflo...  11.1 us
    all_to_all x1, blocking collectives, body(): tiles = lax.all_to_all(tiles, ('x', 'y', 'c'), 0, 0)  10.9 us
    ppermute x3, starting transfers between devices, body(): lax.ppermute(block, 'zl', [(i, i ^ k) for i in range(4)])  10.5 us
    all_to_all x1, waiting for transfers between devices, body(): tiles = lax.all_to_all(tiles, ('h', 'zh', 'zl'), 0, 0)  10.1 us
    all_to_all x1, starting transfers between devices, body(): tiles = lax.all_to_all(tiles, ('h', 'zh', 'zl'), 0, 0)  9.67 us
  transfers between devices with their start and end apart: 13, of which 8 were waited for; matrix products, arithmetic and copies ran while one was open for 4% of the time, Pallas kernels for 9%

profile of v5, /device:TPU:1, one launch (start us, length us, event | category | flops | bytes accessed | tf_op | source)
XLA Modules:
  0.0 195.6 jit_solution(4801842956496087269)
XLA Ops:
  0.7 2.7 %pack.1 = (bf16[288,128]{1,0:T(8,128)(2,1)}, bf16[4,288,128]{2,1,0:T(8,128)(2,1)}) custom-call(s32[1]{0:T(128)} %bitcast.7.at_ref, s32[64,128]{1,0:T(8,128)} %bitcast.72, bf16[128,1024]{1,0:T(8,128)(2,1)} %q_ref.5, bf16[128,128]{1,0:T(8,128)(2,1)} %k_ref.1, bf16[128,128]{1,0:T(8,128)(2,1)} %v_ref.1), custom_call_target="tpu_custom_call" | custom-call | tf_op jit(solution)/shard_map/pack/pallas_call | solution.py:332
  3.3 6.5 %all-to-all-start = ((bf16[4,288,128]{2,1,0:T(8,128)(2,1)}), bf16[4,288,128]{2,1,0:T(8,128)(2,1)S(1)}, u32[]{:S(2)}, u32[]{:S(2)}) async-start(bf16[4,288,128]{2,1,0:T(8,128)(2,1)} %get-tuple-element.19), calls=%async_computation | async-start | bytes 589824 | tf_op jit(solution)/shard_map/all_to_all | solution.py:349
  9.8 8.8 %collective-permute-start = (bf16[288,128]{1,0:T(8,128)(2,1)}, bf16[288,128]{1,0:T(8,128)(2,1)S(1)}, u32[]{:S(2)}, u32[]{:S(2)}) collective-permute-start(bf16[288,128]{1,0:T(8,128)(2,1)} %get-tuple-element.22), channel_id=1, source_target_pairs={{0,64},{16,80},{32,96},{48,112},{64,0},{80,16},{96,32},{112,48},{1... | collective-permute-start | bytes 221192 | tf_op jit(solution)/shard_map/ppermute | solution.py:348
  25.4 4.3 %all-to-all-start.1 = ((bf16[4,5,288,128]{3,2,1,0:T(8,128)(2,1)}), bf16[4,5,288,128]{3,2,1,0:T(8,128)(2,1)}, u32[]{:S(2)}, u32[]{:S(2)}) async-start(bf16[4,5,288,128]{3,2,1,0:T(8,128)(2,1)} %spread_near.1), calls=%async_computation.1 | async-start | bytes 2949120 | tf_op jit(solution)/shard_map/all_to_all | solution.py:395
  29.8 6.2 %collective-permute-start.3 = (bf16[288,128]{1,0:T(8,128)(2,1)S(1)}, bf16[288,128]{1,0:T(8,128)(2,1)S(1)}, u32[]{:S(2)}, u32[]{:S(2)}) collective-permute-start(bf16[288,128]{1,0:T(8,128)(2,1)S(1)} %collective-permute-done.refs_1_), channel_id=1, source_target_pairs={{0,48},{16,32},{32,16},{48,0},{1,49},{17,33},{33,17},{49,1},{2,50}... | collective-permute-start | bytes 221192 | tf_op jit(solution)/shard_map/ppermute | solution.py:396
  40.3 3.0 %collective-permute-done.2.refs_1_ = bf16[288,128]{1,0:T(8,128)(2,1)S(1)} collective-permute-done((bf16[288,128]{1,0:T(8,128)(2,1)S(1)}, bf16[288,128]{1,0:T(8,128)(2,1)S(1)}, u32[]{:S(2)}, u32[]{:S(2)}) %collective-permute-start.2) | collective-permute-done | bytes 73760 | tf_op jit(solution)/shard_map/ppermute | solution.py:396
  45.8 2.5 %all-to-all-done.1.near = bf16[4,5,288,128]{3,2,1,0:T(8,128)(2,1)} async-done(((bf16[4,5,288,128]{3,2,1,0:T(8,128)(2,1)}), bf16[4,5,288,128]{3,2,1,0:T(8,128)(2,1)}, u32[]{:S(2)}, u32[]{:S(2)}) %all-to-all-start.1) | async-done | bytes 1474592 | tf_op jit(solution)/shard_map/all_to_all | solution.py:395
  48.2 3.5 %all-to-all-start.2 = ((bf16[4,3,288,128]{3,2,1,0:T(8,128)(2,1)}), bf16[4,3,288,128]{3,2,1,0:T(8,128)(2,1)S(1)}, u32[]{:S(2)}, u32[]{:S(2)}) async-start(bf16[4,3,288,128]{3,2,1,0:T(8,128)(2,1)} %spread_far.1), calls=%async_computation.2 | async-start | bytes 1769472 | tf_op jit(solution)/shard_map/all_to_all | solution.py:398
  52.0 4.1 %collective-permute-start.4 = (bf16[4,5,288,128]{3,2,1,0:T(8,128)(2,1)}, bf16[4,5,288,128]{3,2,1,0:T(8,128)(2,1)}, u32[]{:S(2)}, u32[]{:S(2)}) collective-permute-start(bf16[4,5,288,128]{3,2,1,0:T(8,128)(2,1)} %all-to-all-done.1.near), channel_id=1, source_target_pairs={{0,8},{8,0},{1,9},{9,1},{2,10},{10,2},{3,11},{11,3},{4,12},{12,4},... | collective-permute-start | bytes 4423688 | tf_op jit(solution)/shard_map/ppermute | solution.py:403
  59.4 3.7 %weight.1.w_ref = bf16[256,5120]{1,0:T(8,128)(2,1)S(1)} custom-call(s32[1,1280]{1,0:T(1,128)S(1)} %copy-done.17, f32[1,5120]{1,0:T(1,128)S(1)} %bitcast.54, bf16[256,5120]{1,0:T(8,128)(2,1)S(1)} %copy-done.15), custom_call_target="tpu_custom_call" | custom-call | flops 3355443200 | tf_op jit(solution)/shard_map/weight/pallas_call | solution.py:400
  63.2 4.8 %collective-permute-start.5 = (bf16[4,3,288,128]{3,2,1,0:T(8,128)(2,1)S(1)}, bf16[4,3,288,128]{3,2,1,0:T(8,128)(2,1)S(1)}, u32[]{:S(2)}, u32[]{:S(2)}) collective-permute-start(bf16[4,3,288,128]{3,2,1,0:T(8,128)(2,1)S(1)} %all-to-all-done.2.far), channel_id=1, source_target_pairs={{0,8},{8,0},{1,9},{9,1},{2,10},{10,2},{3,11},{11,3},{4,12},{12,4},... | collective-permute-start | bytes 2654216 | tf_op jit(solution)/shard_map/ppermute | solution.py:406
  70.9 20.2 %scored.1 = f32[4,40,128]{2,1,0:T(8,128)S(1)} custom-call(s32[3]{0:T(128)S(1)} %pad_add_fusion.core_ref, s32[8]{0:T(128)S(1)} %and_select_fusion.first_ref, s32[8,256]{1,0:T(8,128)S(1)} %reshape.115.low_ref, s32[8,256]{1,0:T(8,128)S(1)} %reshape.122.high_ref, bf16[4,5,288,128]{3,2,1,0:T(8,128)(2,1)} %all-to-all-done.1.near, ...), custom_call_target="tpu_custom_call" | custom-call | tf_op jit(solution)/shard_map/scored/pallas_call | solution.py:410
  91.1 8.6 %all_to_all.40.parts_ref = f32[4,40,128]{2,1,0:T(8,128)S(1)} all-to-all(f32[4,40,128]{2,1,0:T(8,128)S(1)} %scored.1), channel_id=1, replica_groups=mesh['x'=4,'zh'=2,'zl'=4,'c'=2,'h'=2,'y'=4] {'y'}, dimensions={0} | all-to-all | bytes 163840 | tf_op jit(solution)/shard_map/all_to_all | solution.py:433
  100.7 12.4 %all-to-all-start.4 = ((bf16[16,40,128]{2,1,0:T(8,128)(2,1)}), bf16[16,40,128]{2,1,0:T(8,128)(2,1)}, u32[]{:S(2)}, u32[]{:S(2)}) async-start(bf16[16,40,128]{2,1,0:T(8,128)(2,1)} %copy-done.5), calls=%async_computation.4 | async-start | bytes 327680 | tf_op jit(solution)/shard_map/all_to_all | solution.py:445
  116.4 5.6 %context.2.dep_ref = bf16[128,512]{1,0:T(8,128)(2,1)S(1)} custom-call(s32[5]{0:T(128)S(1)} %stack.41.at_ref, s32[1,128]{1,0:T(1,128)S(1)} %bitcast.52, s32[1,128]{1,0:T(1,128)S(1)} %iota_add_fusion.high_ref, bf16[4,5,288,128]{3,2,1,0:T(8,128)(2,1)} %all-to-all-done.1.near, bf16[4,3,288,128]{3,2,1,0:T(8,128)(2,1)S(1)} %all-to-all-done.2.far, ...), custom_call_target="tpu_custom_call" | custom-call | flops 2214592512 | bytes 6291456 | tf_op jit(solution)/shard_map/context/pallas_call | solution.py:421
  122.6 2.7 %all-to-all-done.4.parts_ref = bf16[16,40,128]{2,1,0:T(8,128)(2,1)} async-done(((bf16[16,40,128]{2,1,0:T(8,128)(2,1)}), bf16[16,40,128]{2,1,0:T(8,128)(2,1)}, u32[]{:S(2)}, u32[]{:S(2)}) %all-to-all-start.4) | async-done | bytes 163872 | tf_op jit(solution)/shard_map/all_to_all | solution.py:445
  128.4 4.4 %all-to-all-start.5 = ((bf16[16,320,128]{2,1,0:T(8,128)(2,1)}), bf16[16,320,128]{2,1,0:T(8,128)(2,1)}, u32[]{:S(2)}, u32[]{:S(2)}) async-start(bf16[16,320,128]{2,1,0:T(8,128)(2,1)} %copy-done), calls=%async_computation.5 | async-start | bytes 2621440 | tf_op jit(solution)/shard_map/all_to_all | solution.py:448
  136.2 5.6 %context.3.dep_ref = bf16[128,512]{1,0:T(8,128)(2,1)S(1)} custom-call(s32[5]{0:T(128)S(1)} %stack.41.at_ref, s32[1,128]{1,0:T(1,128)S(1)} %bitcast.53, s32[1,128]{1,0:T(1,128)S(1)} %iota_add_fusion.high_ref, bf16[4,5,288,128]{3,2,1,0:T(8,128)(2,1)} %all-to-all-done.1.near, bf16[4,3,288,128]{3,2,1,0:T(8,128)(2,1)S(1)} %all-to-all-done.2.far, ...), custom_call_target="tpu_custom_call" | custom-call | flops 2214592512 | bytes 6291456 | tf_op jit(solution)/shard_map/context/pallas_call | solution.py:421
  142.4 4.9 %all-to-all-done.5 = bf16[16,320,128]{2,1,0:T(8,128)(2,1)} async-done(((bf16[16,320,128]{2,1,0:T(8,128)(2,1)}), bf16[16,320,128]{2,1,0:T(8,128)(2,1)}, u32[]{:S(2)}, u32[]{:S(2)}) %all-to-all-start.5) | async-done | bytes 1310752 | tf_op jit(solution)/shard_map/all_to_all | solution.py:448
  147.4 8.9 %collective-permute-start.6 = (bf16[4,2,640,128]{3,2,1,0:T(8,128)(2,1)}, bf16[4,2,640,128]{3,2,1,0:T(8,128)(2,1)}, u32[]{:S(2)}, u32[]{:S(2)}) collective-permute-start(bf16[4,2,640,128]{3,2,1,0:T(8,128)(2,1)} %bitcast.27.own_ref), channel_id=1, source_target_pairs={{0,8},{8,0},{1,9},{9,1},{2,10},{10,2},{3,11},{11,3},{4,12},{12,4},... | collective-permute-start | bytes 3932168 | tf_op jit(solution)/shard_map/ppermute | solution.py:450
  159.3 2.3 %logits.1 = f32[32,8,128]{2,1,0:T(8,128)S(1)} custom-call(s32[2]{0:T(128)S(1)} %pad_add_fusion.2.at_ref, s32[2,128]{1,0:T(2,128)S(1)} %reshape.124.ids_ref, f32[2,256,128]{2,1,0:T(8,128)S(1)} %get-tuple-element.34.sum_ref, f32[2,8,128]{2,1,0:T(8,128)S(1)} %get-tuple-element.35.square_ref, bf16[4,2,640,128]{3,2,1,0:T(8,128)(2,1)} %collective-permute-done.6.other_ref, ...), custom_call_target="tpu_custom_call" | custom-call | tf_op jit(solution)/shard_map/logits/pallas_call | solution.py:460
  161.6 10.9 %all_to_all.41.parts_ref = f32[32,8,128]{2,1,0:T(8,128)S(1)} all-to-all(f32[32,8,128]{2,1,0:T(8,128)S(1)} %logits.1), channel_id=1, replica_groups=mesh['x'=4,'zh'=2,'zl'=4,'c'=2,'h'=2,'y'=4] {'x','y','c'}, dimensions={0} | all-to-all | bytes 262144 | tf_op jit(solution)/shard_map/all_to_all | solution.py:464
  173.2 9.7 %all-to-all-start.7 = ((f32[16,8,128]{2,1,0:T(8,128)}), f32[16,8,128]{2,1,0:T(8,128)S(1)}, u32[]{:S(2)}, u32[]{:S(2)}) async-start(f32[16,8,128]{2,1,0:T(8,128)} %merge.1), calls=%async_computation.7 | async-start | bytes 131072 | tf_op jit(solution)/shard_map/all_to_all | solution.py:466
  184.3 10.1 %all-to-all-done.7.parts_ref = f32[16,8,128]{2,1,0:T(8,128)S(1)} async-done(((f32[16,8,128]{2,1,0:T(8,128)}), f32[16,8,128]{2,1,0:T(8,128)S(1)}, u32[]{:S(2)}, u32[]{:S(2)}) %all-to-all-start.7) | async-done | bytes 65568 | tf_op jit(solution)/shard_map/all_to_all | solution.py:466
  (98 shorter events, 38.2 us)
Async XLA Ops:
  3.3 20.8 %all-to-all-start = ((bf16[4,288,128]{2,1,0:T(8,128)(2,1)}), bf16[4,288,128]{2,1,0:T(8,128)(2,1)S(1)}, u32[]{:S(2)}, u32[]{:S(2)}) async-start(bf16[4,288,128]{2,1,0:T(8,128)(2,1)} %get-tuple-element.19), calls=%async_computation | async-start | bytes 589824 | tf_op jit(solution)/shard_map/all_to_all | solution.py:349
  9.8 14.4 %collective-permute-start = (bf16[288,128]{1,0:T(8,128)(2,1)}, bf16[288,128]{1,0:T(8,128)(2,1)S(1)}, u32[]{:S(2)}, u32[]{:S(2)}) collective-permute-start(bf16[288,128]{1,0:T(8,128)(2,1)} %get-tuple-element.22), channel_id=1, source_target_pairs={{0,64},{16,80},{32,96},{48,112},{64,0},{80,16},{96,32},{112,48},{1... | collective-permute-start | bytes 221192 | tf_op jit(solution)/shard_map/ppermute | solution.py:348
  20.8 1.3 copy-start.19
  25.4 22.9 %all-to-all-start.1 = ((bf16[4,5,288,128]{3,2,1,0:T(8,128)(2,1)}), bf16[4,5,288,128]{3,2,1,0:T(8,128)(2,1)}, u32[]{:S(2)}, u32[]{:S(2)}) async-start(bf16[4,5,288,128]{3,2,1,0:T(8,128)(2,1)} %spread_near.1), calls=%async_computation.1 | async-start | bytes 2949120 | tf_op jit(solution)/shard_map/all_to_all | solution.py:395
  29.7 22.0 %copy-start.18 = (bf16[80,256]{1,0:T(8,128)(2,1)S(1)}, bf16[80,256]{1,0:T(8,128)(2,1)}, u32[]{:S(2)}) copy-start(bf16[80,256]{1,0:T(8,128)(2,1)} %param.15) | copy-start | bytes 122884
  29.8 10.6 %collective-permute-start.3 = (bf16[288,128]{1,0:T(8,128)(2,1)S(1)}, bf16[288,128]{1,0:T(8,128)(2,1)S(1)}, u32[]{:S(2)}, u32[]{:S(2)}) collective-permute-start(bf16[288,128]{1,0:T(8,128)(2,1)S(1)} %collective-permute-done.refs_1_), channel_id=1, source_target_pairs={{0,48},{16,32},{32,16},{48,0},{1,49},{17,33},{33,17},{49,1},{2,50}... | collective-permute-start | bytes 221192 | tf_op jit(solution)/shard_map/ppermute | solution.py:396
  36.0 7.3 %collective-permute-start.2 = (bf16[288,128]{1,0:T(8,128)(2,1)S(1)}, bf16[288,128]{1,0:T(8,128)(2,1)S(1)}, u32[]{:S(2)}, u32[]{:S(2)}) collective-permute-start(bf16[288,128]{1,0:T(8,128)(2,1)S(1)} %collective-permute-done.refs_1_), channel_id=1, source_target_pairs={{0,32},{16,48},{32,0},{48,16},{1,33},{17,49},{33,1},{49,17},{2,34}... | collective-permute-start | bytes 221192 | tf_op jit(solution)/shard_map/ppermute | solution.py:396
  38.1 6.6 %collective-permute-start.1 = (bf16[288,128]{1,0:T(8,128)(2,1)S(1)}, bf16[288,128]{1,0:T(8,128)(2,1)S(1)}, u32[]{:S(2)}, u32[]{:S(2)}) collective-permute-start(bf16[288,128]{1,0:T(8,128)(2,1)S(1)} %collective-permute-done.refs_1_), channel_id=1, source_target_pairs={{0,16},{16,0},{32,48},{48,32},{1,17},{17,1},{33,49},{49,33},{2,18}... | collective-permute-start | bytes 221192 | tf_op jit(solution)/shard_map/ppermute | solution.py:396
  48.2 14.9 %all-to-all-start.2 = ((bf16[4,3,288,128]{3,2,1,0:T(8,128)(2,1)}), bf16[4,3,288,128]{3,2,1,0:T(8,128)(2,1)S(1)}, u32[]{:S(2)}, u32[]{:S(2)}) async-start(bf16[4,3,288,128]{3,2,1,0:T(8,128)(2,1)} %spread_far.1), calls=%async_computation.2 | async-start | bytes 1769472 | tf_op jit(solution)/shard_map/all_to_all | solution.py:398
  52.0 16.0 %collective-permute-start.4 = (bf16[4,5,288,128]{3,2,1,0:T(8,128)(2,1)}, bf16[4,5,288,128]{3,2,1,0:T(8,128)(2,1)}, u32[]{:S(2)}, u32[]{:S(2)}) collective-permute-start(bf16[4,5,288,128]{3,2,1,0:T(8,128)(2,1)} %all-to-all-done.1.near), channel_id=1, source_target_pairs={{0,8},{8,0},{1,9},{9,1},{2,10},{10,2},{3,11},{11,3},{4,12},{12,4},... | collective-permute-start | bytes 4423688 | tf_op jit(solution)/shard_map/ppermute | solution.py:403
  56.3 1.7 copy-start.15
  63.2 6.8 %collective-permute-start.5 = (bf16[4,3,288,128]{3,2,1,0:T(8,128)(2,1)S(1)}, bf16[4,3,288,128]{3,2,1,0:T(8,128)(2,1)S(1)}, u32[]{:S(2)}, u32[]{:S(2)}) collective-permute-start(bf16[4,3,288,128]{3,2,1,0:T(8,128)(2,1)S(1)} %all-to-all-done.2.far), channel_id=1, source_target_pairs={{0,8},{8,0},{1,9},{9,1},{2,10},{10,2},{3,11},{11,3},{4,12},{12,4},... | collective-permute-start | bytes 2654216 | tf_op jit(solution)/shard_map/ppermute | solution.py:406
  70.9 20.2 %copy-start.2 = (bf16[4,3,288,128]{3,2,1,0:T(8,128)(2,1)}, bf16[4,3,288,128]{3,2,1,0:T(8,128)(2,1)S(1)}, u32[]{:S(2)}) copy-start(bf16[4,3,288,128]{3,2,1,0:T(8,128)(2,1)S(1)} %collective-permute-done.5.far_other) | copy-start | bytes 2654212
  100.7 24.6 %all-to-all-start.4 = ((bf16[16,40,128]{2,1,0:T(8,128)(2,1)}), bf16[16,40,128]{2,1,0:T(8,128)(2,1)}, u32[]{:S(2)}, u32[]{:S(2)}) async-start(bf16[16,40,128]{2,1,0:T(8,128)(2,1)} %copy-done.5), calls=%async_computation.4 | async-start | bytes 327680 | tf_op jit(solution)/shard_map/all_to_all | solution.py:445
  113.3 1.2 copy-start.3
  115.4 0.9 copy-start.12
  127.3 1.1 copy-start
  128.4 19.0 %all-to-all-start.5 = ((bf16[16,320,128]{2,1,0:T(8,128)(2,1)}), bf16[16,320,128]{2,1,0:T(8,128)(2,1)}, u32[]{:S(2)}, u32[]{:S(2)}) async-start(bf16[16,320,128]{2,1,0:T(8,128)(2,1)} %copy-done), calls=%async_computation.5 | async-start | bytes 2621440 | tf_op jit(solution)/shard_map/all_to_all | solution.py:448
  132.8 1.3 copy-start.1
  134.1 1.2 copy-start.4
  147.4 11.9 %collective-permute-start.6 = (bf16[4,2,640,128]{3,2,1,0:T(8,128)(2,1)}, bf16[4,2,640,128]{3,2,1,0:T(8,128)(2,1)}, u32[]{:S(2)}, u32[]{:S(2)}) collective-permute-start(bf16[4,2,640,128]{3,2,1,0:T(8,128)(2,1)} %bitcast.27.own_ref), channel_id=1, source_target_pairs={{0,8},{8,0},{1,9},{9,1},{2,10},{10,2},{3,11},{11,3},{4,12},{12,4},... | collective-permute-start | bytes 3932168 | tf_op jit(solution)/shard_map/ppermute | solution.py:450
  156.4 2.9 %copy-start.11 = (bf16[128,512]{1,0:T(8,128)(2,1)S(1)}, bf16[128,512]{1,0:T(8,128)(2,1)}, u32[]{:S(2)}) copy-start(bf16[128,512]{1,0:T(8,128)(2,1)} %copy-done.10) | copy-start | bytes 393220
  159.3 24.3 %copy-start.9 = (bf16[128,512]{1,0:T(8,128)(2,1)S(1)}, bf16[128,512]{1,0:T(8,128)(2,1)}, u32[]{:S(2)}) copy-start(bf16[128,512]{1,0:T(8,128)(2,1)} %copy-done.7) | copy-start | bytes 393220
  173.2 21.3 %all-to-all-start.7 = ((f32[16,8,128]{2,1,0:T(8,128)}), f32[16,8,128]{2,1,0:T(8,128)S(1)}, u32[]{:S(2)}, u32[]{:S(2)}) async-start(f32[16,8,128]{2,1,0:T(8,128)} %merge.1), calls=%async_computation.7 | async-start | bytes 131072 | tf_op jit(solution)/shard_map/all_to_all | solution.py:466
  (9 other events, 7.1 us)

commit v6 on v5

--- a/solution.py
+++ b/solution.py
@@ -87,24 +87,22 @@
         copy.wait()
 
 
-def collect(half, place, near_far, held, sems):
+def collect(near_far, held, sems):
     copies = []
-
-    def add(source, i, at, count=None):
-        target = held.at[i, at] if count is None else held.at[i, pl.ds(pl.multiple_of(at, 4), count)]
-        copies.append(pltpu.make_async_copy(source, target, sems.at[len(copies)]))
-
     for i, (near_ref, far_ref) in enumerate(near_far):
         for x in range(4):
-            beyond = x * 8 + (1 - half) * 4
-            add(near_ref.at[x, pl.ds(0, 4)], i, x * 8 + half * 4, 4)
-            add(near_ref.at[x, 4], i, beyond + place)
-            for k in range(1, 4):
-                add(far_ref.at[x, k - 1], i, beyond + jnp.bitwise_xor(place, k))
+            for ref, at, count in ((near_ref, 8 * x, 5), (far_ref, 8 * x + 5, 3)):
+                target = held.at[i, pl.ds(at, count)]
+                copies.append(pltpu.make_async_copy(ref.at[x], target, sems.at[len(copies)]))
     for copy in copies:
         copy.start()
     for copy in copies:
         copy.wait()
+
+
+def held_at(half, place, t, j):
+    far = jnp.bitwise_xor(place, j) + 4
+    return t // 2 * 8 + jnp.where(half == t % 2, j, far)
 
 
 def weight_kernel(source_ref, gain_ref, w_ref, out_ref):
@@ -118,17 +116,23 @@
             out_ref[:, (c * 4 + x) * 640 : (c * 4 + x + 1) * 640] = moved[:, c * 640 : (c + 1) * 640]
 
 
-def attend(own_ref, other_ref, core, q, low, high, first, last, bufs):
+def attend(held, core, half, place, q, low, high, first, last, bufs):
     columns = q.shape[0]
-    half = GROUP * SLAB
-    row = iota((2 * half, 1), 0)
-    inside = jnp.where(row < half, row, row - half)
-    key0 = (inside // SLAB) * (2 * SLAB) + inside % SLAB + jnp.where(row < half, core, 1 - core) * SLAB
+    count = GROUP * SLAB
+    row = iota((2 * count, 1), 0)
+    inside = jnp.where(row < count, row, row - count)
+    key0 = (inside // SLAB) * (2 * SLAB) + inside % SLAB + jnp.where(row < count, core, 1 - core) * SLAB
+
     turned = q.T
 
+    def far(g):
+        return (g // 2) % 2 != half
+
     def rows(g, at):
-        chips = pl.ds(pl.multiple_of(jnp.minimum(g * GROUP, CHIPS - GROUP), GROUP), GROUP)
-        parts = [ref[chips, at : at + SLAB, :].reshape(half, HEAD_DIM) for ref in (own_ref, other_ref)]
+        g = jnp.minimum(g, CHIPS // GROUP - 1)
+        pair = jnp.where(far(g), 2 + jnp.bitwise_xor(g % 2, place // 2), g % 2)
+        chips = pl.ds(pl.multiple_of((g // 4 * 4 + pair) * GROUP, GROUP), GROUP)
+        parts = [held[i, chips, at : at + SLAB, :].reshape(count, HEAD_DIM) for i in range(2)]
         return jnp.concatenate(parts, axis=0)
 
     def scores(g):
@@ -136,8 +140,10 @@
 
     def soften(g, buf, carry):
         top, total, acc = carry
-        offset = g * (2 * half)
-        s = jnp.where((key0 >= low - offset) & (key0 <= high - offset), buf[...] * SCALE2, masked_fill)
+        offset = g * (2 * count)
+        turn = jnp.where(far(g) & (place % 2 == 1), 2 * SLAB, 0)
+        key = jnp.bitwise_xor(key0, turn)
+        s = jnp.where((key >= low - offset) & (key <= high - offset), buf[...] * SCALE2, masked_fill)
         new_top = jnp.maximum(top, jnp.max(s, axis=0, keepdims=True))
         p = jnp.exp2(s - new_top)
         keep = jnp.exp2(top - new_top)
@@ -168,20 +174,17 @@
 def scored_kernel(core_ref, first_ref, low_ref, high_ref, near, far, near_other, far_other, w_ref, *refs):
     out_ref, rows, scored, held, sems = refs[-7:-2]
     core = core_ref[0]
-    collect(core_ref[1], core_ref[2], ((near, far), (near_other, far_other)), held, sems)
-    own_ref, other_ref = held.at[0], held.at[1]
+    half, place = core_ref[1], core_ref[2]
+    collect(((near, far), (near_other, far_other)), held, sems)
     for t in range(8):
         q = jnp.concatenate(
-            (
-                own_ref[4 * t : 4 * t + 4, 2 * SLAB :, :].reshape(128, HEAD_DIM),
-                other_ref[4 * t : 4 * t + 4, 2 * SLAB :, :].reshape(128, HEAD_DIM),
-            ),
-            axis=0,
+            [held[i, held_at(half, place, t, j), 2 * SLAB :, :] for i in range(2) for j in range(4)], axis=0
         )
         mixed = attend(
-            own_ref,
-            other_ref,
+            held,
             core,
+            half,
+            place,
             q,
             low_ref[t : t + 1, :],
             high_ref[t : t + 1, :],
@@ -204,18 +207,19 @@
 
 
 def context_kernel(start_head, at_ref, low_ref, high_ref, near, far, near_other, far_other, q_ref, *refs):
-    out_ref, held, sems = refs[-5:-2]
-    collect(at_ref[3], at_ref[4], ((near, far), (near_other, far_other)), held, sems)
-    own_ref, other_ref = held.at[0], held.at[1]
+    out_ref, token_ref, held, sems = refs[-6:-2]
+    token_ref[...] = jnp.zeros_like(token_ref)
+    collect(((near, far), (near_other, far_other)), held, sems)
     heads = range(start_head, start_head + 4)
     q = jnp.concatenate([q_ref[:, h * 128 : (h + 1) * 128] for h in heads], axis=0)
     low, high = jnp.tile(low_ref[...], (1, 4)), jnp.tile(high_ref[...], (1, 4))
-    mixed = attend(own_ref, other_ref, at_ref[0], q, low, high, at_ref[1], at_ref[2], refs[-2:])
+    mixed = attend(held, at_ref[0], at_ref[3], at_ref[4], q, low, high, at_ref[1], at_ref[2], refs[-2:])
     for i in range(4):
         out_ref[:, i * 128 : (i + 1) * 128] = mixed[:, i * 128 : (i + 1) * 128].T.astype(jnp.bfloat16)
 
 
-def add_kernel(parts_ref, residual_ref, out_ref, block, sems):
+def add_kernel(parts_ref, residual_ref, out_ref, token_ref, block, sems):
+    token_ref[...] = jnp.zeros_like(token_ref)
     total = residual_ref[...]
     for i in range(parts_ref.shape[0]):
         total = total + parts_ref[i]
@@ -223,7 +227,8 @@
     send_copies(block, out_ref, sems)
 
 
-def hidden_kernel(parts_ref, dep_ref, out_ref):
+def hidden_kernel(parts_ref, dep_ref, out_ref, token_ref):
+    token_ref[...] = jnp.zeros_like(token_ref)
     total = parts_ref[:8].astype(jnp.float32) + parts_ref[8:].astype(jnp.float32)
     total = total.reshape(8 * HALF, 128).astype(jnp.bfloat16)
     for i in range(out_ref.shape[0]):
@@ -289,13 +294,13 @@
     out_ref[...] = result
 
 
-def call(kernel, shape, dtype, specs, scratch=(), flops=0, size=0, name=None, out=VMEM, more=None, vmem=16):
+def call(kernel, shape, dtype, specs, scratch=(), flops=0, size=0, name=None, out=VMEM, more=None, more_out=VMEM, vmem=16):
     shapes = jax.ShapeDtypeStruct(shape, dtype)
     return pl.pallas_call(
         kernel,
         out_shape=shapes if more is None else (shapes, more),
         in_specs=specs,
-        out_specs=out if more is None else (out, out),
+        out_specs=out if more is None else (out, more_out),
         scratch_shapes=list(scratch),
         compiler_params=pltpu.CompilerParams(vmem_limit_bytes=int(vmem * 2**20)),
         cost_estimate=pl.CostEstimate(flops=flops, bytes_accessed=size, transcendentals=0),
@@ -342,6 +347,7 @@
         ],
         name="pack",
         out=ANY,
+        more_out=ANY,
         vmem=63.9,
         more=jax.ShapeDtypeStruct((4, BLOCK, 128), jnp.bfloat16),
     )(slab[None], slabs, queries, keys, values)
@@ -405,7 +411,7 @@
     far, weight, mine = lax.optimization_barrier((far, weight, mine))
     far_other = lax.ppermute(far, "c", [(0, 1), (1, 0)])
     blocks = (near, far, near_other, far_other)
-    held = [pltpu.VMEM((2, CHIPS, BLOCK, 128), jnp.bfloat16), pltpu.SemaphoreType.DMA((40,))]
+    held = [pltpu.VMEM((2, CHIPS, BLOCK, 128), jnp.bfloat16), pltpu.SemaphoreType.DMA((16,))]
     scores = pltpu.VMEM((2 * GROUP * SLAB, 256), jnp.float32)
     parts = call(
         scored_kernel,
@@ -416,6 +422,8 @@
         name="scored",
         vmem=28,
     )(core_at, first, low, high, *blocks, out_weight)
+
+    token = jax.ShapeDtypeStruct((8, 128), jnp.float32)
 
     def context_of(start_head, after):
         return call(
@@ -428,11 +436,12 @@
             size=6 * 2**20,
             name="context",
             vmem=28,
+            more=token,
         )(at, own_begin[None, :], own_position[None, :], *blocks, queries, after)
 
     parts = lax.all_to_all(parts, "y", 0, 0)
     block = pltpu.VMEM((HALF, 128), jnp.bfloat16)
-    sums = call(
+    sums, after = call(
         add_kernel,
         (16, HALF, 128),
         jnp.bfloat16,
@@ -440,13 +449,16 @@
         [block, pltpu.SemaphoreType.DMA((16,))],
         name="add",
         out=HBM,
+        more=token,
     )(parts, mine)
-    context_a = context_of(0, sums)
+    context_a, done_a = context_of(0, after)
     sums = lax.all_to_all(sums, ("h", "zh", "zl"), 0, 0)
-    hidden = call(hidden_kernel, (16, 8 * HALF, 128), jnp.bfloat16, [VMEM, ANY], name="hidden")(sums, context_a)
-    context_b = context_of(4, hidden)
+    hidden, after = call(hidden_kernel, (16, 8 * HALF, 128), jnp.bfloat16, [VMEM, ANY], name="hidden", more=token)(
+        sums, done_a
+    )
+    context_b, done_b = context_of(4, after)
     hidden = lax.all_to_all(hidden, ("x", "y"), 0, 0).reshape(4, 2, 640, 128)
-    hidden, context_b = lax.optimization_barrier((hidden, context_b))
+    hidden, done_b = lax.optimization_barrier((hidden, done_b))
     hidden_other = lax.ppermute(hidden, "c", [(0, 1), (1, 0)])
     at_logits = jnp.stack((core, base))
     shares, squares = call(
@@ -458,7 +470,7 @@
         more=jax.ShapeDtypeStruct((2, 8, 128), jnp.float32),
     )(at_logits, hidden, weight)
     tiles = call(logits_kernel, (32, 8, 128), jnp.float32, [SMEM] + [VMEM] * 5 + [ANY], name="logits")(
-        at_logits, ids, shares, squares, hidden_other, weight, context_b
+        at_logits, ids, shares, squares, hidden_other, weight, done_b
     )
     context = jnp.concatenate((context_a, context_b), axis=1)
     tiles = lax.all_to_all(tiles, ("x", "y", "c"), 0, 0)

time: 197 us -> 197 us (level)
  local copies, waits for them, and re-layouts: 18.2 us -> 15 us
  waiting for transfers between devices: 27.2 us -> 29.9 us
    unnamed x42 -> x36, local copies, waits for them, and re-layouts: 14.7 us -> 11.5 us
where the time goes in v6:
time: 197 us; the launch traced here: 195 us
  starting transfers between devices  77.3 us (39%)
  Pallas kernels  48.3 us (25%)
  waiting for transfers between devices  29.9 us (15%)
  blocking collectives  19.4 us (10%)
  local copies, waits for them, and re-layouts  15 us (8%)
  other arithmetic  2.88 us (1%)
    pallas_call x1, Pallas kernels, body(): call(scored_kernel, (4, HALF, 128), jnp.float32, [SMEM, SMEM, VMEM, VMEM]...  21.1 us
    all_to_all x1, starting transfers between devices, body(): sums = lax.all_to_all(sums, ('h', 'zh', 'zl'), 0, 0)  12.4 us
    unnamed x36, local copies, waits for them, and re-layouts  11.5 us
    all_to_all x1, blocking collectives, body(): tiles = lax.all_to_all(tiles, ('x', 'y', 'c'), 0, 0)  10.9 us
    pallas_call x2, Pallas kernels, context_of(): call(functools.partial(context_kernel, start_head), (SLAB, 512), jnp.bflo...  10.7 us
    ppermute x3, starting transfers between devices, body(): lax.ppermute(block, 'zl', [(i, i ^ k) for i in range(4)])  10.5 us
    all_to_all x1, waiting for transfers between devices, body(): tiles = lax.all_to_all(tiles, ('h', 'zh', 'zl'), 0, 0)  10.1 us
    all_to_all x1, starting transfers between devices, body(): tiles = lax.all_to_all(tiles, ('h', 'zh', 'zl'), 0, 0)  9.21 us
  transfers between devices with their start and end apart: 13, of which 8 were waited for; matrix products, arithmetic and copies ran while one was open for 4% of the time, Pallas kernels for 9%

profile of v6, /device:TPU:1, one launch (start us, length us, event | category | flops | bytes accessed | tf_op | source)
XLA Modules:
  0.0 195.1 jit_solution(4276437012020426608)
XLA Ops:
  0.7 2.7 %pack.1 = (bf16[288,128]{1,0:T(8,128)(2,1)}, bf16[4,288,128]{2,1,0:T(8,128)(2,1)}) custom-call(s32[1]{0:T(128)} %bitcast.7.at_ref, s32[64,128]{1,0:T(8,128)} %bitcast.72, bf16[128,1024]{1,0:T(8,128)(2,1)} %q_ref.5, bf16[128,128]{1,0:T(8,128)(2,1)} %k_ref.1, bf16[128,128]{1,0:T(8,128)(2,1)} %v_ref.1), custom_call_target="tpu_custom_call" | custom-call | tf_op jit(solution)/shard_map/pack/pallas_call | solution.py:337
  3.3 6.5 %all-to-all-start = ((bf16[4,288,128]{2,1,0:T(8,128)(2,1)}), bf16[4,288,128]{2,1,0:T(8,128)(2,1)S(1)}, u32[]{:S(2)}, u32[]{:S(2)}) async-start(bf16[4,288,128]{2,1,0:T(8,128)(2,1)} %get-tuple-element.27), calls=%async_computation | async-start | bytes 589824 | tf_op jit(solution)/shard_map/all_to_all | solution.py:355
  9.8 8.8 %collective-permute-start = (bf16[288,128]{1,0:T(8,128)(2,1)}, bf16[288,128]{1,0:T(8,128)(2,1)S(1)}, u32[]{:S(2)}, u32[]{:S(2)}) collective-permute-start(bf16[288,128]{1,0:T(8,128)(2,1)} %get-tuple-element.30), channel_id=1, source_target_pairs={{0,64},{16,80},{32,96},{48,112},{64,0},{80,16},{96,32},{112,48},{1... | collective-permute-start | bytes 221192 | tf_op jit(solution)/shard_map/ppermute | solution.py:354
  25.4 4.3 %all-to-all-start.1 = ((bf16[4,5,288,128]{3,2,1,0:T(8,128)(2,1)}), bf16[4,5,288,128]{3,2,1,0:T(8,128)(2,1)}, u32[]{:S(2)}, u32[]{:S(2)}) async-start(bf16[4,5,288,128]{3,2,1,0:T(8,128)(2,1)} %spread_near.1), calls=%async_computation.1 | async-start | bytes 2949120 | tf_op jit(solution)/shard_map/all_to_all | solution.py:401
  29.7 6.2 %collective-permute-start.3 = (bf16[288,128]{1,0:T(8,128)(2,1)S(1)}, bf16[288,128]{1,0:T(8,128)(2,1)S(1)}, u32[]{:S(2)}, u32[]{:S(2)}) collective-permute-start(bf16[288,128]{1,0:T(8,128)(2,1)S(1)} %collective-permute-done.refs_1_), channel_id=1, source_target_pairs={{0,48},{16,32},{32,16},{48,0},{1,49},{17,33},{33,17},{49,1},{2,50}... | collective-permute-start | bytes 221192 | tf_op jit(solution)/shard_map/ppermute | solution.py:402
  40.3 3.0 %collective-permute-done.2.refs_1_ = bf16[288,128]{1,0:T(8,128)(2,1)S(1)} collective-permute-done((bf16[288,128]{1,0:T(8,128)(2,1)S(1)}, bf16[288,128]{1,0:T(8,128)(2,1)S(1)}, u32[]{:S(2)}, u32[]{:S(2)}) %collective-permute-start.2) | collective-permute-done | bytes 73760 | tf_op jit(solution)/shard_map/ppermute | solution.py:402
  45.7 2.5 %all-to-all-done.1.near = bf16[4,5,288,128]{3,2,1,0:T(8,128)(2,1)} async-done(((bf16[4,5,288,128]{3,2,1,0:T(8,128)(2,1)}), bf16[4,5,288,128]{3,2,1,0:T(8,128)(2,1)}, u32[]{:S(2)}, u32[]{:S(2)}) %all-to-all-start.1) | async-done | bytes 1474592 | tf_op jit(solution)/shard_map/all_to_all | solution.py:401
  48.2 3.5 %all-to-all-start.2 = ((bf16[4,3,288,128]{3,2,1,0:T(8,128)(2,1)}), bf16[4,3,288,128]{3,2,1,0:T(8,128)(2,1)S(1)}, u32[]{:S(2)}, u32[]{:S(2)}) async-start(bf16[4,3,288,128]{3,2,1,0:T(8,128)(2,1)} %spread_far.1), calls=%async_computation.2 | async-start | bytes 1769472 | tf_op jit(solution)/shard_map/all_to_all | solution.py:404
  52.0 4.1 %collective-permute-start.4 = (bf16[4,5,288,128]{3,2,1,0:T(8,128)(2,1)}, bf16[4,5,288,128]{3,2,1,0:T(8,128)(2,1)}, u32[]{:S(2)}, u32[]{:S(2)}) collective-permute-start(bf16[4,5,288,128]{3,2,1,0:T(8,128)(2,1)} %all-to-all-done.1.near), channel_id=1, source_target_pairs={{0,8},{8,0},{1,9},{9,1},{2,10},{10,2},{3,11},{11,3},{4,12},{12,4},... | collective-permute-start | bytes 4423688 | tf_op jit(solution)/shard_map/ppermute | solution.py:409
  59.4 3.7 %weight.1.w_ref = bf16[256,5120]{1,0:T(8,128)(2,1)S(1)} custom-call(s32[1,1280]{1,0:T(1,128)S(1)} %copy-done.14, f32[1,5120]{1,0:T(1,128)S(1)} %bitcast.54, bf16[256,5120]{1,0:T(8,128)(2,1)S(1)} %copy-done.12), custom_call_target="tpu_custom_call" | custom-call | flops 3355443200 | tf_op jit(solution)/shard_map/weight/pallas_call | solution.py:406
  63.2 4.7 %collective-permute-start.5 = (bf16[4,3,288,128]{3,2,1,0:T(8,128)(2,1)S(1)}, bf16[4,3,288,128]{3,2,1,0:T(8,128)(2,1)S(1)}, u32[]{:S(2)}, u32[]{:S(2)}) collective-permute-start(bf16[4,3,288,128]{3,2,1,0:T(8,128)(2,1)S(1)} %all-to-all-done.2.far), channel_id=1, source_target_pairs={{0,8},{8,0},{1,9},{9,1},{2,10},{10,2},{3,11},{11,3},{4,12},{12,4},... | collective-permute-start | bytes 2654216 | tf_op jit(solution)/shard_map/ppermute | solution.py:412
  70.8 21.1 %scored.1 = f32[4,40,128]{2,1,0:T(8,128)S(1)} custom-call(s32[3]{0:T(128)S(1)} %pad_add_fusion.core_ref, s32[8]{0:T(128)S(1)} %and_select_fusion.first_ref, s32[8,256]{1,0:T(8,128)S(1)} %reshape.115.low_ref, s32[8,256]{1,0:T(8,128)S(1)} %reshape.122.high_ref, bf16[4,5,288,128]{3,2,1,0:T(8,128)(2,1)} %all-to-all-done.1.near, ...), custom_call_target="tpu_custom_call" | custom-call | tf_op jit(solution)/shard_map/scored/pallas_call | solution.py:416
  92.0 8.6 %all_to_all.40.parts_ref = f32[4,40,128]{2,1,0:T(8,128)S(1)} all-to-all(f32[4,40,128]{2,1,0:T(8,128)S(1)} %scored.1), channel_id=1, replica_groups=mesh['x'=4,'zh'=2,'zl'=4,'c'=2,'h'=2,'y'=4] {'y'}, dimensions={0} | all-to-all | bytes 163840 | tf_op jit(solution)/shard_map/all_to_all | solution.py:442
  101.5 12.4 %all-to-all-start.4 = ((bf16[16,40,128]{2,1,0:T(8,128)(2,1)}), bf16[16,40,128]{2,1,0:T(8,128)(2,1)}, u32[]{:S(2)}, u32[]{:S(2)}) async-start(bf16[16,40,128]{2,1,0:T(8,128)(2,1)} %copy-done.7), calls=%async_computation.4 | async-start | bytes 327680 | tf_op jit(solution)/shard_map/all_to_all | solution.py:455
  116.3 5.4 %context.2 = (bf16[128,512]{1,0:T(8,128)(2,1)S(1)}, f32[8,128]{1,0:T(8,128)S(1)}) custom-call(s32[5]{0:T(128)S(1)} %stack.41.at_ref, s32[1,128]{1,0:T(1,128)S(1)} %bitcast.52, s32[1,128]{1,0:T(1,128)S(1)} %iota_add_fusion.high_ref, bf16[4,5,288,128]{3,2,1,0:T(8,128)(2,1)} %all-to-all-done.1.near, bf16[4,3,288,128]{3,2,1,0:T(8,128)(2,1)S(1)} %all-to-all-done.2.far, ...), custom_call_target="tpu_custom_call" | custom-call | flops 2214592512 | bytes 6291456 | tf_op jit(solution)/shard_map/context/pallas_call | solution.py:429
  122.3 3.8 %all-to-all-done.4.parts_ref = bf16[16,40,128]{2,1,0:T(8,128)(2,1)} async-done(((bf16[16,40,128]{2,1,0:T(8,128)(2,1)}), bf16[16,40,128]{2,1,0:T(8,128)(2,1)}, u32[]{:S(2)}, u32[]{:S(2)}) %all-to-all-start.4) | async-done | bytes 163872 | tf_op jit(solution)/shard_map/all_to_all | solution.py:455
  128.3 4.4 %all-to-all-start.5 = ((bf16[16,320,128]{2,1,0:T(8,128)(2,1)}), bf16[16,320,128]{2,1,0:T(8,128)(2,1)}, u32[]{:S(2)}, u32[]{:S(2)}) async-start(bf16[16,320,128]{2,1,0:T(8,128)(2,1)} %copy-done), calls=%async_computation.5 | async-start | bytes 2621440 | tf_op jit(solution)/shard_map/all_to_all | solution.py:460
  134.8 5.4 %context.3 = (bf16[128,512]{1,0:T(8,128)(2,1)S(1)}, f32[8,128]{1,0:T(8,128)S(1)}) custom-call(s32[5]{0:T(128)S(1)} %stack.41.at_ref, s32[1,128]{1,0:T(1,128)S(1)} %bitcast.53, s32[1,128]{1,0:T(1,128)S(1)} %iota_add_fusion.high_ref, bf16[4,5,288,128]{3,2,1,0:T(8,128)(2,1)} %all-to-all-done.1.near, bf16[4,3,288,128]{3,2,1,0:T(8,128)(2,1)S(1)} %all-to-all-done.2.far, ...), custom_call_target="tpu_custom_call" | custom-call | flops 2214592512 | bytes 6291456 | tf_op jit(solution)/shard_map/context/pallas_call | solution.py:429
  140.9 6.5 %all-to-all-done.5 = bf16[16,320,128]{2,1,0:T(8,128)(2,1)} async-done(((bf16[16,320,128]{2,1,0:T(8,128)(2,1)}), bf16[16,320,128]{2,1,0:T(8,128)(2,1)}, u32[]{:S(2)}, u32[]{:S(2)}) %all-to-all-start.5) | async-done | bytes 1310752 | tf_op jit(solution)/shard_map/all_to_all | solution.py:460
  147.3 8.9 %collective-permute-start.6 = (bf16[4,2,640,128]{3,2,1,0:T(8,128)(2,1)}, bf16[4,2,640,128]{3,2,1,0:T(8,128)(2,1)}, u32[]{:S(2)}, u32[]{:S(2)}) collective-permute-start(bf16[4,2,640,128]{3,2,1,0:T(8,128)(2,1)} %bitcast.28.own_ref), channel_id=1, source_target_pairs={{0,8},{8,0},{1,9},{9,1},{2,10},{10,2},{3,11},{11,3},{4,12},{12,4},... | collective-permute-start | bytes 3932168 | tf_op jit(solution)/shard_map/ppermute | solution.py:462
  159.2 2.3 %logits.1 = f32[32,8,128]{2,1,0:T(8,128)S(1)} custom-call(s32[2]{0:T(128)S(1)} %pad_add_fusion.2.at_ref, s32[2,128]{1,0:T(2,128)S(1)} %reshape.124.ids_ref, f32[2,256,128]{2,1,0:T(8,128)S(1)} %get-tuple-element.49.sum_ref, f32[2,8,128]{2,1,0:T(8,128)S(1)} %get-tuple-element.50.square_ref, bf16[4,2,640,128]{3,2,1,0:T(8,128)(2,1)} %collective-permute-done.6.other_ref, ...), custom_call_target="tpu_custom_call" | custom-call | tf_op jit(solution)/shard_map/logits/pallas_call | solution.py:472
  161.5 10.9 %all_to_all.41.parts_ref = f32[32,8,128]{2,1,0:T(8,128)S(1)} all-to-all(f32[32,8,128]{2,1,0:T(8,128)S(1)} %logits.1), channel_id=1, replica_groups=mesh['x'=4,'zh'=2,'zl'=4,'c'=2,'h'=2,'y'=4] {'x','y','c'}, dimensions={0} | all-to-all | bytes 262144 | tf_op jit(solution)/shard_map/all_to_all | solution.py:476
  173.1 9.2 %all-to-all-start.7 = ((f32[16,8,128]{2,1,0:T(8,128)}), f32[16,8,128]{2,1,0:T(8,128)S(1)}, u32[]{:S(2)}, u32[]{:S(2)}) async-start(f32[16,8,128]{2,1,0:T(8,128)} %merge.1), calls=%async_computation.7 | async-start | bytes 131072 | tf_op jit(solution)/shard_map/all_to_all | solution.py:478
  183.8 10.1 %all-to-all-done.7.parts_ref = f32[16,8,128]{2,1,0:T(8,128)S(1)} async-done(((f32[16,8,128]{2,1,0:T(8,128)}), f32[16,8,128]{2,1,0:T(8,128)S(1)}, u32[]{:S(2)}, u32[]{:S(2)}) %all-to-all-start.7) | async-done | bytes 65568 | tf_op jit(solution)/shard_map/all_to_all | solution.py:478
  (92 shorter events, 35.0 us)
Async XLA Ops:
  3.3 20.8 %all-to-all-start = ((bf16[4,288,128]{2,1,0:T(8,128)(2,1)}), bf16[4,288,128]{2,1,0:T(8,128)(2,1)S(1)}, u32[]{:S(2)}, u32[]{:S(2)}) async-start(bf16[4,288,128]{2,1,0:T(8,128)(2,1)} %get-tuple-element.27), calls=%async_computation | async-start | bytes 589824 | tf_op jit(solution)/shard_map/all_to_all | solution.py:355
  9.8 14.4 %collective-permute-start = (bf16[288,128]{1,0:T(8,128)(2,1)}, bf16[288,128]{1,0:T(8,128)(2,1)S(1)}, u32[]{:S(2)}, u32[]{:S(2)}) collective-permute-start(bf16[288,128]{1,0:T(8,128)(2,1)} %get-tuple-element.30), channel_id=1, source_target_pairs={{0,64},{16,80},{32,96},{48,112},{64,0},{80,16},{96,32},{112,48},{1... | collective-permute-start | bytes 221192 | tf_op jit(solution)/shard_map/ppermute | solution.py:354
  20.8 1.3 copy-start.16
  25.4 22.8 %all-to-all-start.1 = ((bf16[4,5,288,128]{3,2,1,0:T(8,128)(2,1)}), bf16[4,5,288,128]{3,2,1,0:T(8,128)(2,1)}, u32[]{:S(2)}, u32[]{:S(2)}) async-start(bf16[4,5,288,128]{3,2,1,0:T(8,128)(2,1)} %spread_near.1), calls=%async_computation.1 | async-start | bytes 2949120 | tf_op jit(solution)/shard_map/all_to_all | solution.py:401
  29.7 22.0 %copy-start.15 = (bf16[80,256]{1,0:T(8,128)(2,1)S(1)}, bf16[80,256]{1,0:T(8,128)(2,1)}, u32[]{:S(2)}) copy-start(bf16[80,256]{1,0:T(8,128)(2,1)} %param.15) | copy-start | bytes 122884
  29.7 10.6 %collective-permute-start.3 = (bf16[288,128]{1,0:T(8,128)(2,1)S(1)}, bf16[288,128]{1,0:T(8,128)(2,1)S(1)}, u32[]{:S(2)}, u32[]{:S(2)}) collective-permute-start(bf16[288,128]{1,0:T(8,128)(2,1)S(1)} %collective-permute-done.refs_1_), channel_id=1, source_target_pairs={{0,48},{16,32},{32,16},{48,0},{1,49},{17,33},{33,17},{49,1},{2,50}... | collective-permute-start | bytes 221192 | tf_op jit(solution)/shard_map/ppermute | solution.py:402
  35.9 7.3 %collective-permute-start.2 = (bf16[288,128]{1,0:T(8,128)(2,1)S(1)}, bf16[288,128]{1,0:T(8,128)(2,1)S(1)}, u32[]{:S(2)}, u32[]{:S(2)}) collective-permute-start(bf16[288,128]{1,0:T(8,128)(2,1)S(1)} %collective-permute-done.refs_1_), channel_id=1, source_target_pairs={{0,32},{16,48},{32,0},{48,16},{1,33},{17,49},{33,1},{49,17},{2,34}... | collective-permute-start | bytes 221192 | tf_op jit(solution)/shard_map/ppermute | solution.py:402
  38.1 6.6 %collective-permute-start.1 = (bf16[288,128]{1,0:T(8,128)(2,1)S(1)}, bf16[288,128]{1,0:T(8,128)(2,1)S(1)}, u32[]{:S(2)}, u32[]{:S(2)}) collective-permute-start(bf16[288,128]{1,0:T(8,128)(2,1)S(1)} %collective-permute-done.refs_1_), channel_id=1, source_target_pairs={{0,16},{16,0},{32,48},{48,32},{1,17},{17,1},{33,49},{49,33},{2,18}... | collective-permute-start | bytes 221192 | tf_op jit(solution)/shard_map/ppermute | solution.py:402
  48.2 14.9 %all-to-all-start.2 = ((bf16[4,3,288,128]{3,2,1,0:T(8,128)(2,1)}), bf16[4,3,288,128]{3,2,1,0:T(8,128)(2,1)S(1)}, u32[]{:S(2)}, u32[]{:S(2)}) async-start(bf16[4,3,288,128]{3,2,1,0:T(8,128)(2,1)} %spread_far.1), calls=%async_computation.2 | async-start | bytes 1769472 | tf_op jit(solution)/shard_map/all_to_all | solution.py:404
  52.0 16.0 %collective-permute-start.4 = (bf16[4,5,288,128]{3,2,1,0:T(8,128)(2,1)}, bf16[4,5,288,128]{3,2,1,0:T(8,128)(2,1)}, u32[]{:S(2)}, u32[]{:S(2)}) collective-permute-start(bf16[4,5,288,128]{3,2,1,0:T(8,128)(2,1)} %all-to-all-done.1.near), channel_id=1, source_target_pairs={{0,8},{8,0},{1,9},{9,1},{2,10},{10,2},{3,11},{11,3},{4,12},{12,4},... | collective-permute-start | bytes 4423688 | tf_op jit(solution)/shard_map/ppermute | solution.py:409
  56.2 1.7 copy-start.12
  63.2 6.8 %collective-permute-start.5 = (bf16[4,3,288,128]{3,2,1,0:T(8,128)(2,1)S(1)}, bf16[4,3,288,128]{3,2,1,0:T(8,128)(2,1)S(1)}, u32[]{:S(2)}, u32[]{:S(2)}) collective-permute-start(bf16[4,3,288,128]{3,2,1,0:T(8,128)(2,1)S(1)} %all-to-all-done.2.far), channel_id=1, source_target_pairs={{0,8},{8,0},{1,9},{9,1},{2,10},{10,2},{3,11},{11,3},{4,12},{12,4},... | collective-permute-start | bytes 2654216 | tf_op jit(solution)/shard_map/ppermute | solution.py:412
  70.8 21.1 %copy-start.1 = (bf16[4,3,288,128]{3,2,1,0:T(8,128)(2,1)}, bf16[4,3,288,128]{3,2,1,0:T(8,128)(2,1)S(1)}, u32[]{:S(2)}) copy-start(bf16[4,3,288,128]{3,2,1,0:T(8,128)(2,1)S(1)} %collective-permute-done.5.far_other) | copy-start | bytes 2654212
  101.5 24.6 %all-to-all-start.4 = ((bf16[16,40,128]{2,1,0:T(8,128)(2,1)}), bf16[16,40,128]{2,1,0:T(8,128)(2,1)}, u32[]{:S(2)}, u32[]{:S(2)}) async-start(bf16[16,40,128]{2,1,0:T(8,128)(2,1)} %copy-done.7), calls=%async_computation.4 | async-start | bytes 327680 | tf_op jit(solution)/shard_map/all_to_all | solution.py:455
  114.2 1.2 copy-start.2
  115.4 0.9 copy-start.4
  127.2 1.1 copy-start
  128.3 19.0 %all-to-all-start.5 = ((bf16[16,320,128]{2,1,0:T(8,128)(2,1)}), bf16[16,320,128]{2,1,0:T(8,128)(2,1)}, u32[]{:S(2)}, u32[]{:S(2)}) async-start(bf16[16,320,128]{2,1,0:T(8,128)(2,1)} %copy-done), calls=%async_computation.5 | async-start | bytes 2621440 | tf_op jit(solution)/shard_map/all_to_all | solution.py:460
  132.7 1.2 copy-start.3
  133.9 0.9 copy-start.5
  147.3 11.9 %collective-permute-start.6 = (bf16[4,2,640,128]{3,2,1,0:T(8,128)(2,1)}, bf16[4,2,640,128]{3,2,1,0:T(8,128)(2,1)}, u32[]{:S(2)}, u32[]{:S(2)}) collective-permute-start(bf16[4,2,640,128]{3,2,1,0:T(8,128)(2,1)} %bitcast.28.own_ref), channel_id=1, source_target_pairs={{0,8},{8,0},{1,9},{9,1},{2,10},{10,2},{3,11},{11,3},{4,12},{12,4},... | collective-permute-start | bytes 3932168 | tf_op jit(solution)/shard_map/ppermute | solution.py:462
  159.2 23.9 %copy-start.9 = (bf16[128,512]{1,0:T(8,128)(2,1)S(1)}, bf16[128,512]{1,0:T(8,128)(2,1)}, u32[]{:S(2)}) copy-start(bf16[128,512]{1,0:T(8,128)(2,1)} %copy-done.8) | copy-start | bytes 393220
  159.2 23.9 %copy-start.11 = (bf16[128,512]{1,0:T(8,128)(2,1)S(1)}, bf16[128,512]{1,0:T(8,128)(2,1)}, u32[]{:S(2)}) copy-start(bf16[128,512]{1,0:T(8,128)(2,1)} %copy-done.10) | copy-start | bytes 393220
  173.1 20.8 %all-to-all-start.7 = ((f32[16,8,128]{2,1,0:T(8,128)}), f32[16,8,128]{2,1,0:T(8,128)S(1)}, u32[]{:S(2)}, u32[]{:S(2)}) async-start(f32[16,8,128]{2,1,0:T(8,128)} %merge.1), calls=%async_computation.7 | async-start | bytes 131072 | tf_op jit(solution)/shard_map/all_to_all | solution.py:478
  (6 other events, 4.3 us)

commit v7 on v4

--- a/solution.py
+++ b/solution.py
@@ -200,7 +200,8 @@
 
 
 def context_kernel(start_head, at_ref, low_ref, high_ref, near, far, near_other, far_other, q_ref, *refs):
-    out_ref, held, sems = refs[-5:-2]
+    out_ref, token_ref, held, sems = refs[-6:-2]
+    token_ref[...] = jnp.zeros_like(token_ref)
     collect(at_ref[3], ((near, far), (near_other, far_other)), held, sems)
     own_ref, other_ref = held.at[0], held.at[1]
     heads = range(start_head, start_head + 4)
@@ -211,7 +212,8 @@
         out_ref[:, i * 128 : (i + 1) * 128] = mixed[:, i * 128 : (i + 1) * 128].T.astype(jnp.bfloat16)
 
 
-def add_kernel(parts_ref, residual_ref, out_ref, block, sems):
+def add_kernel(parts_ref, residual_ref, out_ref, token_ref, block, sems):
+    token_ref[...] = jnp.zeros_like(token_ref)
     total = residual_ref[...]
     for i in range(parts_ref.shape[0]):
         total = total + parts_ref[i]
@@ -219,7 +221,8 @@
     send_copies(block, out_ref, sems)
 
 
-def hidden_kernel(parts_ref, dep_ref, out_ref):
+def hidden_kernel(parts_ref, dep_ref, out_ref, token_ref):
+    token_ref[...] = jnp.zeros_like(token_ref)
     total = parts_ref[:8].astype(jnp.float32) + parts_ref[8:].astype(jnp.float32)
     total = total.reshape(8 * HALF, 128).astype(jnp.bfloat16)
     for i in range(out_ref.shape[0]):
@@ -285,13 +288,13 @@
     out_ref[...] = result
 
 
-def call(kernel, shape, dtype, specs, scratch=(), flops=0, size=0, name=None, out=VMEM, more=None, vmem=16):
+def call(kernel, shape, dtype, specs, scratch=(), flops=0, size=0, name=None, out=VMEM, more=None, more_out=VMEM, vmem=16):
     shapes = jax.ShapeDtypeStruct(shape, dtype)
     return pl.pallas_call(
         kernel,
         out_shape=shapes if more is None else (shapes, more),
         in_specs=specs,
-        out_specs=out if more is None else (out, out),
+        out_specs=out if more is None else (out, more_out),
         scratch_shapes=list(scratch),
         compiler_params=pltpu.CompilerParams(vmem_limit_bytes=int(vmem * 2**20)),
         cost_estimate=pl.CostEstimate(flops=flops, bytes_accessed=size, transcendentals=0),
@@ -338,18 +341,50 @@
         ],
         name="pack",
         out=ANY,
+        more_out=ANY,
         vmem=63.9,
         more=jax.ShapeDtypeStruct((4, BLOCK, 128), jnp.bfloat16),
     )(slab[None], slabs, queries, keys, values)
     block = lax.ppermute(block, ("zh", "zl"), [(i, i ^ 4) for i in range(8)])
     near = lax.all_to_all(packed, "zl", 0, 0)
-    spread = call(
+    bounds = jnp.cumsum(doc_lengths)
+    position = jnp.arange(64 * SLAB, dtype=jnp.int32)
+    begin = jnp.max(jnp.where(bounds[None, :] <= position[:, None], bounds[None, :], 0), axis=1)
+    chosen = rank[:, None, :] == jnp.arange(SCORED, dtype=jnp.int32)[None, :, None]
+
+    def pick(values_of):
+        return jnp.sum(jnp.where(chosen, values_of.reshape(64, 1, SLAB), 0), axis=2)
+
+    def columns(of_scored):
+        pairs = of_scored.reshape(CHIPS, 2, SCORED)
+        pairs = jnp.where(core == 0, pairs, pairs[:, ::-1])
+        tiles = pairs.reshape(8, 4, 2, SCORED).transpose(0, 2, 1, 3)
+        return jnp.repeat(tiles.reshape(8, 32), HEADS_DEV, axis=1)
+
+    high = columns(pick(position))
+    low = columns(pick(begin))
+    ids = pick(sampled_ids).reshape(CHIPS, 2, SCORED).transpose(1, 0, 2).reshape(2, 128)
+    first = jnp.min(low, axis=1) // 256
+    half = lax.axis_index("zh")
+    core_at = jnp.stack((core, half))
+
+    mine = residual.reshape(2, HALF, CHIPS, 2, SCORED).transpose(3, 0, 1, 2, 4).reshape(4, HALF, 128)
+    mine = lax.dynamic_index_in_dim(mine, y, 0, keepdims=False).astype(jnp.float32)
+    mine = jnp.where(h == 0, mine, 0.0)
+
+    own_begin = lax.dynamic_slice_in_dim(begin, slab * SLAB, SLAB, 0)
+    own_position = slab * SLAB + jnp.arange(SLAB, dtype=jnp.int32)
+    at = jnp.stack((core, own_begin[0] // 256, chip, half))
+    base = ((slab * 2 + h) * 4 + y) * 256
+
+    near, low, high, first, ids, own_begin = lax.optimization_barrier((near, low, high, first, ids, own_begin))
+    near = call(
         spread_kernel, (4, 4, BLOCK, 128), jnp.bfloat16, [VMEM], [pltpu.SemaphoreType.DMA((4,))], name="spread", out=ANY
     )(near)
-    spread, block = lax.optimization_barrier((spread, block))
-    near = lax.all_to_all(spread, "x", 0, 0)
+    near, block = lax.optimization_barrier((near, block))
+    near = lax.all_to_all(near, "x", 0, 0)
     blocks = [block] + [lax.ppermute(block, "zl", [(i, i ^ k) for i in range(4)]) for k in (1, 2, 3)]
-    spread = call(
+    far = call(
         spread_far_kernel,
         (4, 4, BLOCK, 128),
         jnp.bfloat16,
@@ -358,47 +393,15 @@
         name="spread_far",
         out=ANY,
     )(lax.axis_index("zl")[None], *blocks)
-    near, spread = lax.optimization_barrier((near, spread))
-    far = lax.all_to_all(spread, "x", 0, 0)
+    near, far = lax.optimization_barrier((near, far))
+    far = lax.all_to_all(far, "x", 0, 0)
+    source = jnp.asarray(source_columns())
+    weight = call(
+        weight_kernel, (256, D), jnp.bfloat16, [VMEM] * 3, flops=2 * 256 * D * 1280, name="weight", vmem=28
+    )(source, norm_gain[None, :], head_weight)
     near_other = lax.ppermute(near, "c", [(0, 1), (1, 0)])
 
-    bounds = jnp.cumsum(doc_lengths)
-    position = jnp.arange(64 * SLAB, dtype=jnp.int32)
-    begin = jnp.max(jnp.where(bounds[None, :] <= position[:, None], bounds[None, :], 0), axis=1)
-    chosen = rank[:, None, :] == jnp.arange(SCORED, dtype=jnp.int32)[None, :, None]
-
-    def pick(values_of):
-        return jnp.sum(jnp.where(chosen, values_of.reshape(64, 1, SLAB), 0), axis=2)
-
-    def columns(of_scored):
-        pairs = of_scored.reshape(CHIPS, 2, SCORED)
-        pairs = jnp.where(core == 0, pairs, pairs[:, ::-1])
-        tiles = pairs.reshape(8, 4, 2, SCORED).transpose(0, 2, 1, 3)
-        return jnp.repeat(tiles.reshape(8, 32), HEADS_DEV, axis=1)
-
-    high = columns(pick(position))
-    low = columns(pick(begin))
-    ids = pick(sampled_ids).reshape(CHIPS, 2, SCORED).transpose(1, 0, 2).reshape(2, 128)
-    first = jnp.min(low, axis=1) // 256
-    half = lax.axis_index("zh")
-    core_at = jnp.stack((core, half))
-
-    source = jnp.asarray(source_columns())
-    weight = call(weight_kernel, (256, D), jnp.bfloat16, [VMEM] * 3, flops=2 * 256 * D * 1280, name="weight", vmem=28)(
-        source, norm_gain[None, :], head_weight
-    )
-    mine = residual.reshape(2, HALF, CHIPS, 2, SCORED).transpose(3, 0, 1, 2, 4).reshape(4, HALF, 128)
-    mine = lax.dynamic_index_in_dim(mine, y, 0, keepdims=False).astype(jnp.float32)
-    mine = jnp.where(h == 0, mine, 0.0)
-
-    own_begin = lax.dynamic_slice_in_dim(begin, slab * SLAB, SLAB, 0)
-    own_position = slab * SLAB + jnp.arange(SLAB, dtype=jnp.int32)
-    at = jnp.stack((core, own_begin[0] // 256, chip, half))
-    base = ((slab * 2 + h) * 4 + y) * 256
-
-    far, near_other, weight, mine, low, high, first, ids, own_begin = lax.optimization_barrier(
-        (far, near_other, weight, mine, low, high, first, ids, own_begin)
-    )
+    far, weight, mine = lax.optimization_barrier((far, weight, mine))
     far_other = lax.ppermute(far, "c", [(0, 1), (1, 0)])
     blocks = (near, far, near_other, far_other)
     held = [pltpu.VMEM((2, CHIPS, BLOCK, 128), jnp.bfloat16), pltpu.SemaphoreType.DMA((16,))]
@@ -413,6 +416,8 @@
         vmem=28,
     )(core_at, first, low, high, *blocks, out_weight)
 
+    token = jax.ShapeDtypeStruct((8, 128), jnp.float32)
+
     def context_of(start_head, after):
         return call(
             functools.partial(context_kernel, start_head),
@@ -424,11 +429,12 @@
             size=6 * 2**20,
             name="context",
             vmem=28,
+            more=token,
         )(at, own_begin[None, :], own_position[None, :], *blocks, queries, after)
 
     parts = lax.all_to_all(parts, "y", 0, 0)
     block = pltpu.VMEM((HALF, 128), jnp.bfloat16)
-    sums = call(
+    sums, after = call(
         add_kernel,
         (16, HALF, 128),
         jnp.bfloat16,
@@ -436,13 +442,16 @@
         [block, pltpu.SemaphoreType.DMA((16,))],
         name="add",
         out=HBM,
+        more=token,
     )(parts, mine)
-    context_a = context_of(0, sums)
+    context_a, done_a = context_of(0, after)
     sums = lax.all_to_all(sums, ("h", "zh", "zl"), 0, 0)
-    hidden = call(hidden_kernel, (16, 8 * HALF, 128), jnp.bfloat16, [VMEM, ANY], name="hidden")(sums, context_a)
-    context_b = context_of(4, hidden)
+    hidden, after = call(hidden_kernel, (16, 8 * HALF, 128), jnp.bfloat16, [VMEM, ANY], name="hidden", more=token)(
+        sums, done_a
+    )
+    context_b, done_b = context_of(4, after)
     hidden = lax.all_to_all(hidden, ("x", "y"), 0, 0).reshape(4, 2, 640, 128)
-    hidden, context_b = lax.optimization_barrier((hidden, context_b))
+    hidden, done_b = lax.optimization_barrier((hidden, done_b))
     hidden_other = lax.ppermute(hidden, "c", [(0, 1), (1, 0)])
     at_logits = jnp.stack((core, base))
     shares, squares = call(
@@ -454,7 +463,7 @@
         more=jax.ShapeDtypeStruct((2, 8, 128), jnp.float32),
     )(at_logits, hidden, weight)
     tiles = call(logits_kernel, (32, 8, 128), jnp.float32, [SMEM] + [VMEM] * 5 + [ANY], name="logits")(
-        at_logits, ids, shares, squares, hidden_other, weight, context_b
+        at_logits, ids, shares, squares, hidden_other, weight, done_b
     )
     context = jnp.concatenate((context_a, context_b), axis=1)
     tiles = lax.all_to_all(tiles, ("x", "y", "c"), 0, 0)

time: 195 us -> 190 us (0.974)
  waiting for transfers between devices: 41.1 us -> 38.3 us
    all_to_all x2, waiting for transfers between devices: 8.99 us -> 4.39 us  [the longest x1 4.39 us: body(): far = lax.all_to_all(far, 'x', 0, 0)]
    ppermute x3, starting transfers between devices: 14.1 us -> 10.2 us  [body(): lax.ppermute(block, 'zl', [(i, i ^ k) for i in range(4)])]
    ppermute x1, starting transfers between devices: 2.99 us -> 5.03 us  [body(): far_other = lax.ppermute(far, 'c', [(0, 1), (1, 0)])]
    unnamed x30 -> x24, local copies, waits for them, and re-layouts: 6.94 us -> 5.57 us
  transfers between devices with their start and end apart: 13 -> 13, of which waited for: 9 -> 8; matrix products, arithmetic and copies ran while one was open for 2% -> 3% of each run, Pallas kernels for 9% -> 9%
where the time goes in v7:
time: 190 us; the launch traced here: 188 us
  starting transfers between devices  75.6 us (40%)
  Pallas kernels  42.3 us (22%)
  waiting for transfers between devices  38.3 us (20%)
  blocking collectives  19.4 us (10%)
  local copies, waits for them, and re-layouts  8.31 us (4%)
  other arithmetic  2.2 us (1%)
    pallas_call x1, Pallas kernels, body(): call(scored_kernel, (4, HALF, 128), jnp.float32, [SMEM, SMEM, VMEM, VMEM]...  17.9 us
    all_to_all x1, starting transfers between devices, body(): sums = lax.all_to_all(sums, ('h', 'zh', 'zl'), 0, 0)  11.4 us
    all_to_all x1, blocking collectives, body(): tiles = lax.all_to_all(tiles, ('x', 'y', 'c'), 0, 0)  10.9 us
    all_to_all x1, waiting for transfers between devices, body(): tiles = lax.all_to_all(tiles, ('h', 'zh', 'zl'), 0, 0)  10.8 us
    ppermute x3, starting transfers between devices, body(): lax.ppermute(block, 'zl', [(i, i ^ k) for i in range(4)])  10.2 us
    all_to_all x1, waiting for transfers between devices, body(): hidden = lax.all_to_all(hidden, ('x', 'y'), 0, 0).reshape(4, 2, 640, 128)  9.08 us
    ppermute x1, starting transfers between devices, body(): hidden_other = lax.ppermute(hidden, 'c', [(0, 1), (1, 0)])  8.9 us
    ppermute x1, starting transfers between devices, body(): block = lax.ppermute(block, ('zh', 'zl'), [(i, i ^ 4) for i in range(8)])  8.8 us
  transfers between devices with their start and end apart: 13, of which 8 were waited for; matrix products, arithmetic and copies ran while one was open for 3% of the time, Pallas kernels for 9%

profile of v7, /device:TPU:1, one launch (start us, length us, event | category | flops | bytes accessed | tf_op | source)
XLA Modules:
  0.0 188.4 jit_solution(1024709651762537877)
XLA Ops:
  0.7 2.7 %pack.1 = (bf16[288,128]{1,0:T(8,128)(2,1)}, bf16[4,288,128]{2,1,0:T(8,128)(2,1)}) custom-call(s32[1]{0:T(128)} %bitcast.6.at_ref, s32[64,128]{1,0:T(8,128)} %bitcast.72, bf16[128,1024]{1,0:T(8,128)(2,1)} %q_ref.5, bf16[128,128]{1,0:T(8,128)(2,1)} %k_ref.1, bf16[128,128]{1,0:T(8,128)(2,1)} %v_ref.1), custom_call_target="tpu_custom_call" | custom-call | tf_op jit(solution)/shard_map/pack/pallas_call | solution.py:331
  3.3 6.5 %all-to-all-start = ((bf16[4,288,128]{2,1,0:T(8,128)(2,1)}), bf16[4,288,128]{2,1,0:T(8,128)(2,1)S(1)}, u32[]{:S(2)}, u32[]{:S(2)}) async-start(bf16[4,288,128]{2,1,0:T(8,128)(2,1)} %get-tuple-element.29), calls=%async_computation | async-start | bytes 589824 | tf_op jit(solution)/shard_map/all_to_all | solution.py:349
  9.8 8.8 %collective-permute-start = (bf16[288,128]{1,0:T(8,128)(2,1)}, bf16[288,128]{1,0:T(8,128)(2,1)S(1)}, u32[]{:S(2)}, u32[]{:S(2)}) collective-permute-start(bf16[288,128]{1,0:T(8,128)(2,1)} %get-tuple-element.32), channel_id=1, source_target_pairs={{0,64},{16,80},{32,96},{48,112},{64,0},{80,16},{96,32},{112,48},{1... | collective-permute-start | bytes 221192 | tf_op jit(solution)/shard_map/ppermute | solution.py:348
  24.5 4.3 %all-to-all-start.1 = ((bf16[4,4,288,128]{3,2,1,0:T(8,128)(2,1)}), bf16[4,4,288,128]{3,2,1,0:T(8,128)(2,1)}, u32[]{:S(2)}, u32[]{:S(2)}) async-start(bf16[4,4,288,128]{3,2,1,0:T(8,128)(2,1)} %spread.1), calls=%async_computation.1 | async-start | bytes 2359296 | tf_op jit(solution)/shard_map/all_to_all | solution.py:385
  28.8 5.9 %collective-permute-start.3 = (bf16[288,128]{1,0:T(8,128)(2,1)S(1)}, bf16[288,128]{1,0:T(8,128)(2,1)S(1)}, u32[]{:S(2)}, u32[]{:S(2)}) collective-permute-start(bf16[288,128]{1,0:T(8,128)(2,1)S(1)} %collective-permute-done.refs_0_), channel_id=1, source_target_pairs={{0,48},{16,32},{32,16},{48,0},{1,49},{17,33},{33,17},{49,1},{2,50}... | collective-permute-start | bytes 221192 | tf_op jit(solution)/shard_map/ppermute | solution.py:386
  39.1 2.8 %collective-permute-done.2.refs_2_ = bf16[288,128]{1,0:T(8,128)(2,1)S(1)} collective-permute-done((bf16[288,128]{1,0:T(8,128)(2,1)S(1)}, bf16[288,128]{1,0:T(8,128)(2,1)S(1)}, u32[]{:S(2)}, u32[]{:S(2)}) %collective-permute-start.2) | collective-permute-done | bytes 73760 | tf_op jit(solution)/shard_map/ppermute | solution.py:386
  44.7 4.3 %all-to-all-start.2 = ((bf16[4,4,288,128]{3,2,1,0:T(8,128)(2,1)}), bf16[4,4,288,128]{3,2,1,0:T(8,128)(2,1)}, u32[]{:S(2)}, u32[]{:S(2)}) async-start(bf16[4,4,288,128]{3,2,1,0:T(8,128)(2,1)} %spread_far.1), calls=%async_computation.2 | async-start | bytes 2359296 | tf_op jit(solution)/shard_map/all_to_all | solution.py:397
  51.2 3.7 %weight.1.w_ref = bf16[256,5120]{1,0:T(8,128)(2,1)S(1)} custom-call(s32[1,1280]{1,0:T(1,128)S(1)} %copy-done.8, f32[1,5120]{1,0:T(1,128)S(1)} %bitcast.54, bf16[256,5120]{1,0:T(8,128)(2,1)S(1)} %copy-done.6), custom_call_target="tpu_custom_call" | custom-call | flops 3355443200 | tf_op jit(solution)/shard_map/weight/pallas_call | solution.py:399
  54.9 4.1 %collective-permute-start.4 = (bf16[4,4,288,128]{3,2,1,0:T(8,128)(2,1)}, bf16[4,4,288,128]{3,2,1,0:T(8,128)(2,1)}, u32[]{:S(2)}, u32[]{:S(2)}) collective-permute-start(bf16[4,4,288,128]{3,2,1,0:T(8,128)(2,1)} %all-to-all-done.1.near), channel_id=1, source_target_pairs={{0,8},{8,0},{1,9},{9,1},{2,10},{10,2},{3,11},{11,3},{4,12},{12,4},... | collective-permute-start | bytes 3538952 | tf_op jit(solution)/shard_map/ppermute | solution.py:402
  59.0 4.4 %all-to-all-done.2.far = bf16[4,4,288,128]{3,2,1,0:T(8,128)(2,1)} async-done(((bf16[4,4,288,128]{3,2,1,0:T(8,128)(2,1)}), bf16[4,4,288,128]{3,2,1,0:T(8,128)(2,1)}, u32[]{:S(2)}, u32[]{:S(2)}) %all-to-all-start.2) | async-done | bytes 1179680 | tf_op jit(solution)/shard_map/all_to_all | solution.py:397
  63.4 5.0 %collective-permute-start.5 = (bf16[4,4,288,128]{3,2,1,0:T(8,128)(2,1)}, bf16[4,4,288,128]{3,2,1,0:T(8,128)(2,1)S(1)}, u32[]{:S(2)}, u32[]{:S(2)}) collective-permute-start(bf16[4,4,288,128]{3,2,1,0:T(8,128)(2,1)} %all-to-all-done.2.far), channel_id=1, source_target_pairs={{0,8},{8,0},{1,9},{9,1},{2,10},{10,2},{3,11},{11,3},{4,12},{12,4},... | collective-permute-start | bytes 3538952 | tf_op jit(solution)/shard_map/ppermute | solution.py:405
  68.5 2.6 %collective-permute-done.5.far_other = bf16[4,4,288,128]{3,2,1,0:T(8,128)(2,1)S(1)} collective-permute-done((bf16[4,4,288,128]{3,2,1,0:T(8,128)(2,1)}, bf16[4,4,288,128]{3,2,1,0:T(8,128)(2,1)S(1)}, u32[]{:S(2)}, u32[]{:S(2)}) %collective-permute-start.5) | collective-permute-done | bytes 1179680 | tf_op jit(solution)/shard_map/ppermute | solution.py:405
  71.1 17.9 %scored.1 = f32[4,40,128]{2,1,0:T(8,128)S(1)} custom-call(s32[2]{0:T(128)S(1)} %pad_add_fusion.1.core_ref, s32[8]{0:T(128)S(1)} %and_select_fusion.first_ref, s32[8,256]{1,0:T(8,128)S(1)} %reshape.115.low_ref, s32[8,256]{1,0:T(8,128)S(1)} %reshape.122.high_ref, bf16[4,4,288,128]{3,2,1,0:T(8,128)(2,1)} %all-to-all-done.1.near, ...), custom_call_target="tpu_custom_call" | custom-call | tf_op jit(solution)/shard_map/scored/pallas_call | solution.py:409
  89.0 8.6 %all_to_all.40.parts_ref = f32[4,40,128]{2,1,0:T(8,128)S(1)} all-to-all(f32[4,40,128]{2,1,0:T(8,128)S(1)} %scored.1), channel_id=1, replica_groups=mesh['x'=4,'zh'=2,'zl'=4,'c'=2,'h'=2,'y'=4] {'y'}, dimensions={0} | all-to-all | bytes 163840 | tf_op jit(solution)/shard_map/all_to_all | solution.py:435
  98.3 11.4 %all-to-all-start.4 = ((bf16[16,40,128]{2,1,0:T(8,128)(2,1)}), bf16[16,40,128]{2,1,0:T(8,128)(2,1)S(1)}, u32[]{:S(2)}, u32[]{:S(2)}) async-start(bf16[16,40,128]{2,1,0:T(8,128)(2,1)} %get-tuple-element.44), calls=%async_computation.4 | async-start | bytes 327680 | tf_op jit(solution)/shard_map/all_to_all | solution.py:448
  111.3 4.3 %context.2 = (bf16[128,512]{1,0:T(8,128)(2,1)S(1)}, f32[8,128]{1,0:T(8,128)S(1)}) custom-call(s32[4]{0:T(128)S(1)} %pad_add_fusion.at_ref, s32[1,128]{1,0:T(1,128)S(1)} %bitcast.52, s32[1,128]{1,0:T(1,128)S(1)} %iota_add_fusion.high_ref, bf16[4,4,288,128]{3,2,1,0:T(8,128)(2,1)} %all-to-all-done.1.near, bf16[4,4,288,128]{3,2,1,0:T(8,128)(2,1)} %all-to-all-done.2.far, ...), custom_call_target="tpu_custom_call" | custom-call | flops 2214592512 | bytes 6291456 | tf_op jit(solution)/shard_map/context/pallas_call | solution.py:422
  115.6 6.4 %all-to-all-done.4.parts_ref = bf16[16,40,128]{2,1,0:T(8,128)(2,1)S(1)} async-done(((bf16[16,40,128]{2,1,0:T(8,128)(2,1)}), bf16[16,40,128]{2,1,0:T(8,128)(2,1)S(1)}, u32[]{:S(2)}, u32[]{:S(2)}) %all-to-all-start.4) | async-done | bytes 163872 | tf_op jit(solution)/shard_map/all_to_all | solution.py:448
  123.2 4.4 %all-to-all-start.5 = ((bf16[16,320,128]{2,1,0:T(8,128)(2,1)}), bf16[16,320,128]{2,1,0:T(8,128)(2,1)}, u32[]{:S(2)}, u32[]{:S(2)}) async-start(bf16[16,320,128]{2,1,0:T(8,128)(2,1)} %copy-done), calls=%async_computation.5 | async-start | bytes 2621440 | tf_op jit(solution)/shard_map/all_to_all | solution.py:453
  128.8 4.3 %context.3 = (bf16[128,512]{1,0:T(8,128)(2,1)S(1)}, f32[8,128]{1,0:T(8,128)S(1)}) custom-call(s32[4]{0:T(128)S(1)} %pad_add_fusion.at_ref, s32[1,128]{1,0:T(1,128)S(1)} %bitcast.53, s32[1,128]{1,0:T(1,128)S(1)} %iota_add_fusion.high_ref, bf16[4,4,288,128]{3,2,1,0:T(8,128)(2,1)} %all-to-all-done.1.near, bf16[4,4,288,128]{3,2,1,0:T(8,128)(2,1)} %all-to-all-done.2.far, ...), custom_call_target="tpu_custom_call" | custom-call | flops 2214592512 | bytes 6291456 | tf_op jit(solution)/shard_map/context/pallas_call | solution.py:422
  133.1 9.1 %all-to-all-done.5 = bf16[16,320,128]{2,1,0:T(8,128)(2,1)} async-done(((bf16[16,320,128]{2,1,0:T(8,128)(2,1)}), bf16[16,320,128]{2,1,0:T(8,128)(2,1)}, u32[]{:S(2)}, u32[]{:S(2)}) %all-to-all-start.5) | async-done | bytes 1310752 | tf_op jit(solution)/shard_map/all_to_all | solution.py:453
  142.2 8.9 %collective-permute-start.6 = (bf16[4,2,640,128]{3,2,1,0:T(8,128)(2,1)}, bf16[4,2,640,128]{3,2,1,0:T(8,128)(2,1)}, u32[]{:S(2)}, u32[]{:S(2)}) collective-permute-start(bf16[4,2,640,128]{3,2,1,0:T(8,128)(2,1)} %bitcast.28.own_ref), channel_id=1, source_target_pairs={{0,8},{8,0},{1,9},{9,1},{2,10},{10,2},{3,11},{11,3},{4,12},{12,4},... | collective-permute-start | bytes 3932168 | tf_op jit(solution)/shard_map/ppermute | solution.py:455
  156.4 10.9 %all_to_all.41.parts_ref = f32[32,8,128]{2,1,0:T(8,128)S(1)} all-to-all(f32[32,8,128]{2,1,0:T(8,128)S(1)} %logits.1), channel_id=1, replica_groups=mesh['x'=4,'zh'=2,'zl'=4,'c'=2,'h'=2,'y'=4] {'x','y','c'}, dimensions={0} | all-to-all | bytes 262144 | tf_op jit(solution)/shard_map/all_to_all | solution.py:469
  167.9 7.7 %all-to-all-start.7 = ((f32[16,8,128]{2,1,0:T(8,128)}), f32[16,8,128]{2,1,0:T(8,128)S(1)}, u32[]{:S(2)}, u32[]{:S(2)}) async-start(f32[16,8,128]{2,1,0:T(8,128)} %merge.1), calls=%async_computation.7 | async-start | bytes 131072 | tf_op jit(solution)/shard_map/all_to_all | solution.py:471
  176.4 10.8 %all-to-all-done.7.parts_ref = f32[16,8,128]{2,1,0:T(8,128)S(1)} async-done(((f32[16,8,128]{2,1,0:T(8,128)}), f32[16,8,128]{2,1,0:T(8,128)S(1)}, u32[]{:S(2)}, u32[]{:S(2)}) %all-to-all-start.7) | async-done | bytes 65568 | tf_op jit(solution)/shard_map/all_to_all | solution.py:471
  (80 shorter events, 27.6 us)
Async XLA Ops:
  0.6 20.2 %copy-start.10 = (s32[8192]{0:T(1024)S(1)}, s32[8192]{0:T(1024)}, u32[]{:S(2)}) copy-start(s32[8192]{0:T(1024)} %param.18) | copy-start | bytes 98308
  3.3 20.0 %all-to-all-start = ((bf16[4,288,128]{2,1,0:T(8,128)(2,1)}), bf16[4,288,128]{2,1,0:T(8,128)(2,1)S(1)}, u32[]{:S(2)}, u32[]{:S(2)}) async-start(bf16[4,288,128]{2,1,0:T(8,128)(2,1)} %get-tuple-element.29), calls=%async_computation | async-start | bytes 589824 | tf_op jit(solution)/shard_map/all_to_all | solution.py:349
  9.8 14.7 %collective-permute-start = (bf16[288,128]{1,0:T(8,128)(2,1)}, bf16[288,128]{1,0:T(8,128)(2,1)S(1)}, u32[]{:S(2)}, u32[]{:S(2)}) collective-permute-start(bf16[288,128]{1,0:T(8,128)(2,1)} %get-tuple-element.32), channel_id=1, source_target_pairs={{0,64},{16,80},{32,96},{48,112},{64,0},{80,16},{96,32},{112,48},{1... | collective-permute-start | bytes 221192 | tf_op jit(solution)/shard_map/ppermute | solution.py:348
  24.5 20.2 %all-to-all-start.1 = ((bf16[4,4,288,128]{3,2,1,0:T(8,128)(2,1)}), bf16[4,4,288,128]{3,2,1,0:T(8,128)(2,1)}, u32[]{:S(2)}, u32[]{:S(2)}) async-start(bf16[4,4,288,128]{3,2,1,0:T(8,128)(2,1)} %spread.1), calls=%async_computation.1 | async-start | bytes 2359296 | tf_op jit(solution)/shard_map/all_to_all | solution.py:385
  28.8 10.3 %collective-permute-start.3 = (bf16[288,128]{1,0:T(8,128)(2,1)S(1)}, bf16[288,128]{1,0:T(8,128)(2,1)S(1)}, u32[]{:S(2)}, u32[]{:S(2)}) collective-permute-start(bf16[288,128]{1,0:T(8,128)(2,1)S(1)} %collective-permute-done.refs_0_), channel_id=1, source_target_pairs={{0,48},{16,32},{32,16},{48,0},{1,49},{17,33},{33,17},{49,1},{2,50}... | collective-permute-start | bytes 221192 | tf_op jit(solution)/shard_map/ppermute | solution.py:386
  34.7 7.2 %collective-permute-start.2 = (bf16[288,128]{1,0:T(8,128)(2,1)S(1)}, bf16[288,128]{1,0:T(8,128)(2,1)S(1)}, u32[]{:S(2)}, u32[]{:S(2)}) collective-permute-start(bf16[288,128]{1,0:T(8,128)(2,1)S(1)} %collective-permute-done.refs_0_), channel_id=1, source_target_pairs={{0,32},{16,48},{32,0},{48,16},{1,33},{17,49},{33,1},{49,17},{2,34}... | collective-permute-start | bytes 221192 | tf_op jit(solution)/shard_map/ppermute | solution.py:386
  36.8 6.6 %collective-permute-start.1 = (bf16[288,128]{1,0:T(8,128)(2,1)S(1)}, bf16[288,128]{1,0:T(8,128)(2,1)S(1)}, u32[]{:S(2)}, u32[]{:S(2)}) collective-permute-start(bf16[288,128]{1,0:T(8,128)(2,1)S(1)} %collective-permute-done.refs_0_), channel_id=1, source_target_pairs={{0,16},{16,0},{32,48},{48,32},{1,17},{17,1},{33,49},{49,33},{2,18}... | collective-permute-start | bytes 221192 | tf_op jit(solution)/shard_map/ppermute | solution.py:386
  44.7 4.3 %copy-start.9 = (bf16[80,256]{1,0:T(8,128)(2,1)S(1)}, bf16[80,256]{1,0:T(8,128)(2,1)}, u32[]{:S(2)}) copy-start(bf16[80,256]{1,0:T(8,128)(2,1)} %param.15) | copy-start | bytes 122884
  44.7 4.7 %copy-start.7 = (f32[5120]{0:T(1024)S(1)}, f32[5120]{0:T(1024)}, u32[]{:S(2)}) copy-start(f32[5120]{0:T(1024)} %param.16) | copy-start | bytes 61444
  44.7 4.7 %copy-start.8 = (s32[1,1280]{1,0:T(1,128)S(1)}, s32[1,1280]{1,0:T(1,128)}, u32[]{:S(2)}) copy-start(s32[1,1280]{1,0:T(1,128)} %constant.87.clone.source_ref) | copy-start | bytes 15364
  44.7 18.7 %all-to-all-start.2 = ((bf16[4,4,288,128]{3,2,1,0:T(8,128)(2,1)}), bf16[4,4,288,128]{3,2,1,0:T(8,128)(2,1)}, u32[]{:S(2)}, u32[]{:S(2)}) async-start(bf16[4,4,288,128]{3,2,1,0:T(8,128)(2,1)} %spread_far.1), calls=%async_computation.2 | async-start | bytes 2359296 | tf_op jit(solution)/shard_map/all_to_all | solution.py:397
  49.4 1.7 copy-start.6
  51.2 19.9 %copy-start.5 = (bf16[80,1024]{1,0:T(8,128)(2,1)S(1)}, bf16[80,1024]{1,0:T(8,128)(2,1)}, u32[]{:S(2)}) copy-start(bf16[80,1024]{1,0:T(8,128)(2,1)} %w_ref.3) | copy-start | bytes 491524
  54.9 13.6 %collective-permute-start.4 = (bf16[4,4,288,128]{3,2,1,0:T(8,128)(2,1)}, bf16[4,4,288,128]{3,2,1,0:T(8,128)(2,1)}, u32[]{:S(2)}, u32[]{:S(2)}) collective-permute-start(bf16[4,4,288,128]{3,2,1,0:T(8,128)(2,1)} %all-to-all-done.1.near), channel_id=1, source_target_pairs={{0,8},{8,0},{1,9},{9,1},{2,10},{10,2},{3,11},{11,3},{4,12},{12,4},... | collective-permute-start | bytes 3538952 | tf_op jit(solution)/shard_map/ppermute | solution.py:402
  63.4 7.7 %collective-permute-start.5 = (bf16[4,4,288,128]{3,2,1,0:T(8,128)(2,1)}, bf16[4,4,288,128]{3,2,1,0:T(8,128)(2,1)S(1)}, u32[]{:S(2)}, u32[]{:S(2)}) collective-permute-start(bf16[4,4,288,128]{3,2,1,0:T(8,128)(2,1)} %all-to-all-done.2.far), channel_id=1, source_target_pairs={{0,8},{8,0},{1,9},{9,1},{2,10},{10,2},{3,11},{11,3},{4,12},{12,4},... | collective-permute-start | bytes 3538952 | tf_op jit(solution)/shard_map/ppermute | solution.py:405
  68.5 41.6 %copy-start.4 = (bf16[128,1024]{1,0:T(8,128)(2,1)S(1)}, bf16[128,1024]{1,0:T(8,128)(2,1)}, u32[]{:S(2)}) copy-start(bf16[128,1024]{1,0:T(8,128)(2,1)} %q_ref.5) | copy-start | bytes 786436
  71.1 17.9 %copy-start.1 = (bf16[4,4,288,128]{3,2,1,0:T(8,128)(2,1)}, bf16[4,4,288,128]{3,2,1,0:T(8,128)(2,1)S(1)}, u32[]{:S(2)}) copy-start(bf16[4,4,288,128]{3,2,1,0:T(8,128)(2,1)S(1)} %collective-permute-done.5.far_other) | copy-start | bytes 3538948
  98.3 23.6 %all-to-all-start.4 = ((bf16[16,40,128]{2,1,0:T(8,128)(2,1)}), bf16[16,40,128]{2,1,0:T(8,128)(2,1)S(1)}, u32[]{:S(2)}, u32[]{:S(2)}) async-start(bf16[16,40,128]{2,1,0:T(8,128)(2,1)} %get-tuple-element.44), calls=%async_computation.4 | async-start | bytes 327680 | tf_op jit(solution)/shard_map/all_to_all | solution.py:448
  110.0 1.3 copy-start.2
  122.1 1.1 copy-start
  123.2 19.0 %all-to-all-start.5 = ((bf16[16,320,128]{2,1,0:T(8,128)(2,1)}), bf16[16,320,128]{2,1,0:T(8,128)(2,1)}, u32[]{:S(2)}, u32[]{:S(2)}) async-start(bf16[16,320,128]{2,1,0:T(8,128)(2,1)} %copy-done), calls=%async_computation.5 | async-start | bytes 2621440 | tf_op jit(solution)/shard_map/all_to_all | solution.py:453
  127.6 1.3 copy-start.3
  142.2 11.9 %collective-permute-start.6 = (bf16[4,2,640,128]{3,2,1,0:T(8,128)(2,1)}, bf16[4,2,640,128]{3,2,1,0:T(8,128)(2,1)}, u32[]{:S(2)}, u32[]{:S(2)}) collective-permute-start(bf16[4,2,640,128]{3,2,1,0:T(8,128)(2,1)} %bitcast.28.own_ref), channel_id=1, source_target_pairs={{0,8},{8,0},{1,9},{9,1},{2,10},{10,2},{3,11},{11,3},{4,12},{12,4},... | collective-permute-start | bytes 3932168 | tf_op jit(solution)/shard_map/ppermute | solution.py:455
  167.9 19.3 %all-to-all-start.7 = ((f32[16,8,128]{2,1,0:T(8,128)}), f32[16,8,128]{2,1,0:T(8,128)S(1)}, u32[]{:S(2)}, u32[]{:S(2)}) async-start(f32[16,8,128]{2,1,0:T(8,128)} %merge.1), calls=%async_computation.7 | async-start | bytes 131072 | tf_op jit(solution)/shard_map/all_to_all | solution.py:471

commit v8 on v7

--- a/solution.py
+++ b/solution.py
@@ -324,10 +324,6 @@
     chip = x * 8 + z
     slab = chip * 2 + core
     slabs = loss_mask.reshape(64, SLAB)
-    upto = jnp.tril(jnp.ones((SLAB, SLAB), jnp.float32)).T
-    rank = jnp.dot(slabs.astype(jnp.float32), upto, preferred_element_type=jnp.float32).astype(jnp.int32)
-    rank = jnp.where(slabs == 1, rank - 1, -1)
-    own_rank = lax.dynamic_slice_in_dim(rank, slab, 1, 0)
     block, packed = call(
         pack_kernel,
         (BLOCK, 128),
@@ -347,37 +343,6 @@
     )(slab[None], slabs, queries, keys, values)
     block = lax.ppermute(block, ("zh", "zl"), [(i, i ^ 4) for i in range(8)])
     near = lax.all_to_all(packed, "zl", 0, 0)
-    bounds = jnp.cumsum(doc_lengths)
-    position = jnp.arange(64 * SLAB, dtype=jnp.int32)
-    begin = jnp.max(jnp.where(bounds[None, :] <= position[:, None], bounds[None, :], 0), axis=1)
-    chosen = rank[:, None, :] == jnp.arange(SCORED, dtype=jnp.int32)[None, :, None]
-
-    def pick(values_of):
-        return jnp.sum(jnp.where(chosen, values_of.reshape(64, 1, SLAB), 0), axis=2)
-
-    def columns(of_scored):
-        pairs = of_scored.reshape(CHIPS, 2, SCORED)
-        pairs = jnp.where(core == 0, pairs, pairs[:, ::-1])
-        tiles = pairs.reshape(8, 4, 2, SCORED).transpose(0, 2, 1, 3)
-        return jnp.repeat(tiles.reshape(8, 32), HEADS_DEV, axis=1)
-
-    high = columns(pick(position))
-    low = columns(pick(begin))
-    ids = pick(sampled_ids).reshape(CHIPS, 2, SCORED).transpose(1, 0, 2).reshape(2, 128)
-    first = jnp.min(low, axis=1) // 256
-    half = lax.axis_index("zh")
-    core_at = jnp.stack((core, half))
-
-    mine = residual.reshape(2, HALF, CHIPS, 2, SCORED).transpose(3, 0, 1, 2, 4).reshape(4, HALF, 128)
-    mine = lax.dynamic_index_in_dim(mine, y, 0, keepdims=False).astype(jnp.float32)
-    mine = jnp.where(h == 0, mine, 0.0)
-
-    own_begin = lax.dynamic_slice_in_dim(begin, slab * SLAB, SLAB, 0)
-    own_position = slab * SLAB + jnp.arange(SLAB, dtype=jnp.int32)
-    at = jnp.stack((core, own_begin[0] // 256, chip, half))
-    base = ((slab * 2 + h) * 4 + y) * 256
-
-    near, low, high, first, ids, own_begin = lax.optimization_barrier((near, low, high, first, ids, own_begin))
     near = call(
         spread_kernel, (4, 4, BLOCK, 128), jnp.bfloat16, [VMEM], [pltpu.SemaphoreType.DMA((4,))], name="spread", out=ANY
     )(near)
@@ -395,10 +360,49 @@
     )(lax.axis_index("zl")[None], *blocks)
     near, far = lax.optimization_barrier((near, far))
     far = lax.all_to_all(far, "x", 0, 0)
+    near, loss_mask, sampled_ids, doc_lengths, norm_gain, residual = lax.optimization_barrier(
+        (near, loss_mask, sampled_ids, doc_lengths, norm_gain, residual)
+    )
     source = jnp.asarray(source_columns())
     weight = call(
         weight_kernel, (256, D), jnp.bfloat16, [VMEM] * 3, flops=2 * 256 * D * 1280, name="weight", vmem=28
     )(source, norm_gain[None, :], head_weight)
+    slabs = loss_mask.reshape(64, SLAB)
+    upto = jnp.tril(jnp.ones((SLAB, SLAB), jnp.float32)).T
+    rank = jnp.dot(slabs.astype(jnp.float32), upto, preferred_element_type=jnp.float32).astype(jnp.int32)
+    rank = jnp.where(slabs == 1, rank - 1, -1)
+    own_rank = lax.dynamic_slice_in_dim(rank, slab, 1, 0)
+    bounds = jnp.cumsum(doc_lengths)
+    position = jnp.arange(64 * SLAB, dtype=jnp.int32)
+    begin = jnp.max(jnp.where(bounds[None, :] <= position[:, None], bounds[None, :], 0), axis=1)
+    chosen = rank[:, None, :] == jnp.arange(SCORED, dtype=jnp.int32)[None, :, None]
+
+    def pick(values_of):
+        return jnp.sum(jnp.where(chosen, values_of.reshape(64, 1, SLAB), 0), axis=2)
+
+    def columns(of_scored):
+        pairs = of_scored.reshape(CHIPS, 2, SCORED)
+        pairs = jnp.where(core == 0, pairs, pairs[:, ::-1])
+        tiles = pairs.reshape(8, 4, 2, SCORED).transpose(0, 2, 1, 3)
+        return jnp.repeat(tiles.reshape(8, 32), HEADS_DEV, axis=1)
+
+    high = columns(pick(position))
+    low = columns(pick(begin))
+    ids = pick(sampled_ids).reshape(CHIPS, 2, SCORED).transpose(1, 0, 2).reshape(2, 128)
+    first = jnp.min(low, axis=1) // 256
+    half = lax.axis_index("zh")
+    core_at = jnp.stack((core, half))
+
+    mine = residual.reshape(2, HALF, CHIPS, 2, SCORED).transpose(3, 0, 1, 2, 4).reshape(4, HALF, 128)
+    mine = lax.dynamic_index_in_dim(mine, y, 0, keepdims=False).astype(jnp.float32)
+    mine = jnp.where(h == 0, mine, 0.0)
+
+    own_begin = lax.dynamic_slice_in_dim(begin, slab * SLAB, SLAB, 0)
+    own_position = slab * SLAB + jnp.arange(SLAB, dtype=jnp.int32)
+    at = jnp.stack((core, own_begin[0] // 256, chip, half))
+    base = ((slab * 2 + h) * 4 + y) * 256
+
+    near, low, high, first, ids, own_begin = lax.optimization_barrier((near, low, high, first, ids, own_begin))
     near_other = lax.ppermute(near, "c", [(0, 1), (1, 0)])
 
     far, weight, mine = lax.optimization_barrier((far, weight, mine))

time: 190 us -> 190 us (level)
  starting transfers between devices: 75.6 us -> 81.1 us
  waiting for transfers between devices: 38.3 us -> 34.8 us
    all_to_all x1, waiting for transfers between devices: 4.39 us -> 0.26 us  [body(): far = lax.all_to_all(far, 'x', 0, 0)]
    ppermute x3, starting transfers between devices: 10.2 us -> 14.1 us  [body(): lax.ppermute(block, 'zl', [(i, i ^ k) for i in range(4)])]
    unnamed x24 -> x27, local copies, waits for them, and re-layouts: 5.57 us -> 5.47 us
  transfers between devices with their start and end apart: 13 -> 13, of which waited for: 8 -> 9; matrix products, arithmetic and copies ran while one was open for 3% -> 2% of each run, Pallas kernels for 9% -> 9%
where the time goes in v8:
time: 190 us; the launch traced here: 189 us
  starting transfers between devices  81.1 us (43%)
  Pallas kernels  42.7 us (22%)
  waiting for transfers between devices  34.8 us (18%)
  blocking collectives  19.4 us (10%)
  local copies, waits for them, and re-layouts  7.69 us (4%)
  other arithmetic  2.18 us (1%)
    pallas_call x1, Pallas kernels, body(): call(scored_kernel, (4, HALF, 128), jnp.float32, [SMEM, SMEM, VMEM, VMEM]...  18.3 us
    ppermute x3, starting transfers between devices, body(): lax.ppermute(block, 'zl', [(i, i ^ k) for i in range(4)])  14.1 us
    all_to_all x1, starting transfers between devices, body(): sums = lax.all_to_all(sums, ('h', 'zh', 'zl'), 0, 0)  11.8 us
    all_to_all x1, blocking collectives, body(): tiles = lax.all_to_all(tiles, ('x', 'y', 'c'), 0, 0)  10.9 us
    all_to_all x1, waiting for transfers between devices, body(): tiles = lax.all_to_all(tiles, ('h', 'zh', 'zl'), 0, 0)  10.8 us
    all_to_all x1, waiting for transfers between devices, body(): hidden = lax.all_to_all(hidden, ('x', 'y'), 0, 0).reshape(4, 2, 640, 128)  9.1 us
    ppermute x1, starting transfers between devices, body(): hidden_other = lax.ppermute(hidden, 'c', [(0, 1), (1, 0)])  8.9 us
    ppermute x1, starting transfers between devices, body(): block = lax.ppermute(block, ('zh', 'zl'), [(i, i ^ 4) for i in range(8)])  8.8 us
  transfers between devices with their start and end apart: 13, of which 9 were waited for; matrix products, arithmetic and copies ran while one was open for 2% of the time, Pallas kernels for 9%

profile of v8, /device:TPU:1, one launch (start us, length us, event | category | flops | bytes accessed | tf_op | source)
XLA Modules:
  0.0 189.3 jit_solution(8223948145683223156)
XLA Ops:
  0.7 2.7 %pack.1 = (bf16[288,128]{1,0:T(8,128)(2,1)}, bf16[4,288,128]{2,1,0:T(8,128)(2,1)}) custom-call(s32[1]{0:T(128)} %bitcast.1.at_ref, s32[64,128]{1,0:T(8,128)} %bitcast.69, bf16[128,1024]{1,0:T(8,128)(2,1)} %q_ref.5, bf16[128,128]{1,0:T(8,128)(2,1)} %k_ref.1, bf16[128,128]{1,0:T(8,128)(2,1)} %v_ref.1), custom_call_target="tpu_custom_call" | custom-call | tf_op jit(solution)/shard_map/pack/pallas_call | solution.py:327
  3.3 6.5 %all-to-all-start = ((bf16[4,288,128]{2,1,0:T(8,128)(2,1)}), bf16[4,288,128]{2,1,0:T(8,128)(2,1)S(1)}, u32[]{:S(2)}, u32[]{:S(2)}) async-start(bf16[4,288,128]{2,1,0:T(8,128)(2,1)} %get-tuple-element.35), calls=%async_computation | async-start | bytes 589824 | tf_op jit(solution)/shard_map/all_to_all | solution.py:345
  9.8 8.8 %collective-permute-start = (bf16[288,128]{1,0:T(8,128)(2,1)}, bf16[288,128]{1,0:T(8,128)(2,1)S(1)}, u32[]{:S(2)}, u32[]{:S(2)}) collective-permute-start(bf16[288,128]{1,0:T(8,128)(2,1)} %get-tuple-element.36), channel_id=1, source_target_pairs={{0,64},{16,80},{32,96},{48,112},{64,0},{80,16},{96,32},{112,48},{1... | collective-permute-start | bytes 221192 | tf_op jit(solution)/shard_map/ppermute | solution.py:344
  20.7 4.3 %all-to-all-start.1 = ((bf16[4,4,288,128]{3,2,1,0:T(8,128)(2,1)}), bf16[4,4,288,128]{3,2,1,0:T(8,128)(2,1)}, u32[]{:S(2)}, u32[]{:S(2)}) async-start(bf16[4,4,288,128]{3,2,1,0:T(8,128)(2,1)} %spread.1), calls=%async_computation.1 | async-start | bytes 2359296 | tf_op jit(solution)/shard_map/all_to_all | solution.py:350
  25.0 9.7 %collective-permute-start.3 = (bf16[288,128]{1,0:T(8,128)(2,1)S(1)}, bf16[288,128]{1,0:T(8,128)(2,1)S(1)}, u32[]{:S(2)}, u32[]{:S(2)}) collective-permute-start(bf16[288,128]{1,0:T(8,128)(2,1)S(1)} %collective-permute-done.refs_0_), channel_id=1, source_target_pairs={{0,48},{16,32},{32,16},{48,0},{1,49},{17,33},{33,17},{49,1},{2,50}... | collective-permute-start | bytes 221192 | tf_op jit(solution)/shard_map/ppermute | solution.py:351
  39.1 3.0 %collective-permute-done.2.refs_2_ = bf16[288,128]{1,0:T(8,128)(2,1)S(1)} collective-permute-done((bf16[288,128]{1,0:T(8,128)(2,1)S(1)}, bf16[288,128]{1,0:T(8,128)(2,1)S(1)}, u32[]{:S(2)}, u32[]{:S(2)}) %collective-permute-start.2) | collective-permute-done | bytes 73760 | tf_op jit(solution)/shard_map/ppermute | solution.py:351
  44.3 4.3 %all-to-all-start.2 = ((bf16[4,4,288,128]{3,2,1,0:T(8,128)(2,1)}), bf16[4,4,288,128]{3,2,1,0:T(8,128)(2,1)}, u32[]{:S(2)}, u32[]{:S(2)}) async-start(bf16[4,4,288,128]{3,2,1,0:T(8,128)(2,1)} %spread_far.1), calls=%async_computation.2 | async-start | bytes 2359296 | tf_op jit(solution)/shard_map/all_to_all | solution.py:362
  52.3 4.5 %collective-permute-start.4 = (bf16[4,4,288,128]{3,2,1,0:T(8,128)(2,1)}, bf16[4,4,288,128]{3,2,1,0:T(8,128)(2,1)}, u32[]{:S(2)}, u32[]{:S(2)}) collective-permute-start(bf16[4,4,288,128]{3,2,1,0:T(8,128)(2,1)} %all-to-all-done.1.near), channel_id=1, source_target_pairs={{0,8},{8,0},{1,9},{9,1},{2,10},{10,2},{3,11},{11,3},{4,12},{12,4},... | collective-permute-start | bytes 3538952 | tf_op jit(solution)/shard_map/ppermute | solution.py:406
  58.6 3.7 %weight.1.w_ref = bf16[256,5120]{1,0:T(8,128)(2,1)S(1)} custom-call(s32[1,1280]{1,0:T(1,128)S(1)} %copy-done.8, f32[1,5120]{1,0:T(1,128)S(1)} %bitcast.51, bf16[256,5120]{1,0:T(8,128)(2,1)S(1)} %copy-done.6), custom_call_target="tpu_custom_call" | custom-call | flops 3355443200 | tf_op jit(solution)/shard_map/weight/pallas_call | solution.py:367
  62.5 5.4 %collective-permute-start.5 = (bf16[4,4,288,128]{3,2,1,0:T(8,128)(2,1)}, bf16[4,4,288,128]{3,2,1,0:T(8,128)(2,1)S(1)}, u32[]{:S(2)}, u32[]{:S(2)}) collective-permute-start(bf16[4,4,288,128]{3,2,1,0:T(8,128)(2,1)} %all-to-all-done.2.far), channel_id=1, source_target_pairs={{0,8},{8,0},{1,9},{9,1},{2,10},{10,2},{3,11},{11,3},{4,12},{12,4},... | collective-permute-start | bytes 3538952 | tf_op jit(solution)/shard_map/ppermute | solution.py:409
  68.1 2.6 %collective-permute-done.5.far_other = bf16[4,4,288,128]{3,2,1,0:T(8,128)(2,1)S(1)} collective-permute-done((bf16[4,4,288,128]{3,2,1,0:T(8,128)(2,1)}, bf16[4,4,288,128]{3,2,1,0:T(8,128)(2,1)S(1)}, u32[]{:S(2)}, u32[]{:S(2)}) %collective-permute-start.5) | collective-permute-done | bytes 1179680 | tf_op jit(solution)/shard_map/ppermute | solution.py:409
  70.7 18.3 %scored.1 = f32[4,40,128]{2,1,0:T(8,128)S(1)} custom-call(s32[2]{0:T(128)S(1)} %pad_add_fusion.1.core_ref, s32[8]{0:T(128)S(1)} %and_select_fusion.first_ref, s32[8,256]{1,0:T(8,128)S(1)} %reshape.119.low_ref, s32[8,256]{1,0:T(8,128)S(1)} %reshape.126.high_ref, bf16[4,4,288,128]{3,2,1,0:T(8,128)(2,1)} %all-to-all-done.1.near, ...), custom_call_target="tpu_custom_call" | custom-call | tf_op jit(solution)/shard_map/scored/pallas_call | solution.py:413
  89.0 8.5 %all_to_all.40.parts_ref = f32[4,40,128]{2,1,0:T(8,128)S(1)} all-to-all(f32[4,40,128]{2,1,0:T(8,128)S(1)} %scored.1), channel_id=1, replica_groups=mesh['x'=4,'zh'=2,'zl'=4,'c'=2,'h'=2,'y'=4] {'y'}, dimensions={0} | all-to-all | bytes 163840 | tf_op jit(solution)/shard_map/all_to_all | solution.py:439
  98.3 11.8 %all-to-all-start.4 = ((bf16[16,40,128]{2,1,0:T(8,128)(2,1)}), bf16[16,40,128]{2,1,0:T(8,128)(2,1)S(1)}, u32[]{:S(2)}, u32[]{:S(2)}) async-start(bf16[16,40,128]{2,1,0:T(8,128)(2,1)} %get-tuple-element.56), calls=%async_computation.4 | async-start | bytes 327680 | tf_op jit(solution)/shard_map/all_to_all | solution.py:452
  111.7 4.2 %context.2 = (bf16[128,512]{1,0:T(8,128)(2,1)S(1)}, f32[8,128]{1,0:T(8,128)S(1)}) custom-call(s32[4]{0:T(128)S(1)} %pad_add_fusion.at_ref, s32[1,128]{1,0:T(1,128)S(1)} %bitcast.49, s32[1,128]{1,0:T(1,128)S(1)} %iota_add_fusion.high_ref, bf16[4,4,288,128]{3,2,1,0:T(8,128)(2,1)} %all-to-all-done.1.near, bf16[4,4,288,128]{3,2,1,0:T(8,128)(2,1)} %all-to-all-done.2.far, ...), custom_call_target="tpu_custom_call" | custom-call | flops 2214592512 | bytes 6291456 | tf_op jit(solution)/shard_map/context/pallas_call | solution.py:426
  115.9 6.4 %all-to-all-done.4.parts_ref = bf16[16,40,128]{2,1,0:T(8,128)(2,1)S(1)} async-done(((bf16[16,40,128]{2,1,0:T(8,128)(2,1)}), bf16[16,40,128]{2,1,0:T(8,128)(2,1)S(1)}, u32[]{:S(2)}, u32[]{:S(2)}) %all-to-all-start.4) | async-done | bytes 163872 | tf_op jit(solution)/shard_map/all_to_all | solution.py:452
  123.5 4.4 %all-to-all-start.5 = ((bf16[16,320,128]{2,1,0:T(8,128)(2,1)}), bf16[16,320,128]{2,1,0:T(8,128)(2,1)}, u32[]{:S(2)}, u32[]{:S(2)}) async-start(bf16[16,320,128]{2,1,0:T(8,128)(2,1)} %copy-done), calls=%async_computation.5 | async-start | bytes 2621440 | tf_op jit(solution)/shard_map/all_to_all | solution.py:457
  129.2 4.3 %context.3 = (bf16[128,512]{1,0:T(8,128)(2,1)S(1)}, f32[8,128]{1,0:T(8,128)S(1)}) custom-call(s32[4]{0:T(128)S(1)} %pad_add_fusion.at_ref, s32[1,128]{1,0:T(1,128)S(1)} %bitcast.50, s32[1,128]{1,0:T(1,128)S(1)} %iota_add_fusion.high_ref, bf16[4,4,288,128]{3,2,1,0:T(8,128)(2,1)} %all-to-all-done.1.near, bf16[4,4,288,128]{3,2,1,0:T(8,128)(2,1)} %all-to-all-done.2.far, ...), custom_call_target="tpu_custom_call" | custom-call | flops 2214592512 | bytes 6291456 | tf_op jit(solution)/shard_map/context/pallas_call | solution.py:426
  133.4 9.1 %all-to-all-done.5 = bf16[16,320,128]{2,1,0:T(8,128)(2,1)} async-done(((bf16[16,320,128]{2,1,0:T(8,128)(2,1)}), bf16[16,320,128]{2,1,0:T(8,128)(2,1)}, u32[]{:S(2)}, u32[]{:S(2)}) %all-to-all-start.5) | async-done | bytes 1310752 | tf_op jit(solution)/shard_map/all_to_all | solution.py:457
  142.5 8.9 %collective-permute-start.6 = (bf16[4,2,640,128]{3,2,1,0:T(8,128)(2,1)}, bf16[4,2,640,128]{3,2,1,0:T(8,128)(2,1)}, u32[]{:S(2)}, u32[]{:S(2)}) collective-permute-start(bf16[4,2,640,128]{3,2,1,0:T(8,128)(2,1)} %bitcast.29.own_ref), channel_id=1, source_target_pairs={{0,8},{8,0},{1,9},{9,1},{2,10},{10,2},{3,11},{11,3},{4,12},{12,4},... | collective-permute-start | bytes 3932168 | tf_op jit(solution)/shard_map/ppermute | solution.py:459
  154.4 2.3 %logits.1 = f32[32,8,128]{2,1,0:T(8,128)S(1)} custom-call(s32[2]{0:T(128)S(1)} %pad_add_fusion.3.at_ref, s32[2,128]{1,0:T(2,128)S(1)} %reshape.128.ids_ref, f32[2,256,128]{2,1,0:T(8,128)S(1)} %get-tuple-element.65.sum_ref, f32[2,8,128]{2,1,0:T(8,128)S(1)} %get-tuple-element.66.square_ref, bf16[4,2,640,128]{3,2,1,0:T(8,128)(2,1)} %collective-permute-done.6.other_ref, ...), custom_call_target="tpu_custom_call" | custom-call | tf_op jit(solution)/shard_map/logits/pallas_call | solution.py:469
  156.7 10.9 %all_to_all.41.parts_ref = f32[32,8,128]{2,1,0:T(8,128)S(1)} all-to-all(f32[32,8,128]{2,1,0:T(8,128)S(1)} %logits.1), channel_id=1, replica_groups=mesh['x'=4,'zh'=2,'zl'=4,'c'=2,'h'=2,'y'=4] {'x','y','c'}, dimensions={0} | all-to-all | bytes 262144 | tf_op jit(solution)/shard_map/all_to_all | solution.py:473
  168.3 8.2 %all-to-all-start.7 = ((f32[16,8,128]{2,1,0:T(8,128)}), f32[16,8,128]{2,1,0:T(8,128)S(1)}, u32[]{:S(2)}, u32[]{:S(2)}) async-start(f32[16,8,128]{2,1,0:T(8,128)} %merge.1), calls=%async_computation.7 | async-start | bytes 131072 | tf_op jit(solution)/shard_map/all_to_all | solution.py:475
  177.3 10.8 %all-to-all-done.7.parts_ref = f32[16,8,128]{2,1,0:T(8,128)S(1)} async-done(((f32[16,8,128]{2,1,0:T(8,128)}), f32[16,8,128]{2,1,0:T(8,128)S(1)}, u32[]{:S(2)}, u32[]{:S(2)}) %all-to-all-start.7) | async-done | bytes 65568 | tf_op jit(solution)/shard_map/all_to_all | solution.py:475
  (84 shorter events, 24.6 us)
Async XLA Ops:
  3.3 15.3 %all-to-all-start = ((bf16[4,288,128]{2,1,0:T(8,128)(2,1)}), bf16[4,288,128]{2,1,0:T(8,128)(2,1)S(1)}, u32[]{:S(2)}, u32[]{:S(2)}) async-start(bf16[4,288,128]{2,1,0:T(8,128)(2,1)} %get-tuple-element.35), calls=%async_computation | async-start | bytes 589824 | tf_op jit(solution)/shard_map/all_to_all | solution.py:345
  9.8 10.9 %collective-permute-start = (bf16[288,128]{1,0:T(8,128)(2,1)}, bf16[288,128]{1,0:T(8,128)(2,1)S(1)}, u32[]{:S(2)}, u32[]{:S(2)}) collective-permute-start(bf16[288,128]{1,0:T(8,128)(2,1)} %get-tuple-element.36), channel_id=1, source_target_pairs={{0,64},{16,80},{32,96},{48,112},{64,0},{80,16},{96,32},{112,48},{1... | collective-permute-start | bytes 221192 | tf_op jit(solution)/shard_map/ppermute | solution.py:344
  20.7 23.6 %all-to-all-start.1 = ((bf16[4,4,288,128]{3,2,1,0:T(8,128)(2,1)}), bf16[4,4,288,128]{3,2,1,0:T(8,128)(2,1)}, u32[]{:S(2)}, u32[]{:S(2)}) async-start(bf16[4,4,288,128]{3,2,1,0:T(8,128)(2,1)} %spread.1), calls=%async_computation.1 | async-start | bytes 2359296 | tf_op jit(solution)/shard_map/all_to_all | solution.py:350
  25.0 14.1 %collective-permute-start.3 = (bf16[288,128]{1,0:T(8,128)(2,1)S(1)}, bf16[288,128]{1,0:T(8,128)(2,1)S(1)}, u32[]{:S(2)}, u32[]{:S(2)}) collective-permute-start(bf16[288,128]{1,0:T(8,128)(2,1)S(1)} %collective-permute-done.refs_0_), channel_id=1, source_target_pairs={{0,48},{16,32},{32,16},{48,0},{1,49},{17,33},{33,17},{49,1},{2,50}... | collective-permute-start | bytes 221192 | tf_op jit(solution)/shard_map/ppermute | solution.py:351
  34.7 7.3 %collective-permute-start.2 = (bf16[288,128]{1,0:T(8,128)(2,1)S(1)}, bf16[288,128]{1,0:T(8,128)(2,1)S(1)}, u32[]{:S(2)}, u32[]{:S(2)}) collective-permute-start(bf16[288,128]{1,0:T(8,128)(2,1)S(1)} %collective-permute-done.refs_0_), channel_id=1, source_target_pairs={{0,32},{16,48},{32,0},{48,16},{1,33},{17,49},{33,1},{49,17},{2,34}... | collective-permute-start | bytes 221192 | tf_op jit(solution)/shard_map/ppermute | solution.py:351
  36.8 6.2 %collective-permute-start.1 = (bf16[288,128]{1,0:T(8,128)(2,1)S(1)}, bf16[288,128]{1,0:T(8,128)(2,1)S(1)}, u32[]{:S(2)}, u32[]{:S(2)}) collective-permute-start(bf16[288,128]{1,0:T(8,128)(2,1)S(1)} %collective-permute-done.refs_0_), channel_id=1, source_target_pairs={{0,16},{16,0},{32,48},{48,32},{1,17},{17,1},{33,49},{49,33},{2,18}... | collective-permute-start | bytes 221192 | tf_op jit(solution)/shard_map/ppermute | solution.py:351
  44.3 4.3 %copy-start.12 = (s32[32]{0:T(128)S(1)}, s32[32]{0:T(128)}, u32[]{:S(2)}) copy-start(s32[32]{0:T(128)} %param.20) | copy-start | bytes 388
  44.3 4.9 %copy-start.11 = (s32[8192]{0:T(1024)S(1)}, s32[8192]{0:T(1024)}, u32[]{:S(2)}) copy-start(s32[8192]{0:T(1024)} %param.19) | copy-start | bytes 98308
  44.3 5.0 %copy-start.10 = (s32[8192]{0:T(1024)S(1)}, s32[8192]{0:T(1024)}, u32[]{:S(2)}) copy-start(s32[8192]{0:T(1024)} %param.18) | copy-start | bytes 98308
  44.3 5.7 %copy-start.9 = (bf16[80,256]{1,0:T(8,128)(2,1)S(1)}, bf16[80,256]{1,0:T(8,128)(2,1)}, u32[]{:S(2)}) copy-start(bf16[80,256]{1,0:T(8,128)(2,1)} %param.15) | copy-start | bytes 122884
  44.3 18.2 %all-to-all-start.2 = ((bf16[4,4,288,128]{3,2,1,0:T(8,128)(2,1)}), bf16[4,4,288,128]{3,2,1,0:T(8,128)(2,1)}, u32[]{:S(2)}, u32[]{:S(2)}) async-start(bf16[4,4,288,128]{3,2,1,0:T(8,128)(2,1)} %spread_far.1), calls=%async_computation.2 | async-start | bytes 2359296 | tf_op jit(solution)/shard_map/all_to_all | solution.py:362
  48.9 7.9 %copy-start.7 = (f32[5120]{0:T(1024)S(1)}, f32[5120]{0:T(1024)}, u32[]{:S(2)}) copy-start(f32[5120]{0:T(1024)} %param.16) | copy-start | bytes 61444
  48.9 7.9 %copy-start.8 = (s32[1,1280]{1,0:T(1,128)S(1)}, s32[1,1280]{1,0:T(1,128)}, u32[]{:S(2)}) copy-start(s32[1,1280]{1,0:T(1,128)} %constant.87.clone.source_ref) | copy-start | bytes 15364
  52.3 15.8 %collective-permute-start.4 = (bf16[4,4,288,128]{3,2,1,0:T(8,128)(2,1)}, bf16[4,4,288,128]{3,2,1,0:T(8,128)(2,1)}, u32[]{:S(2)}, u32[]{:S(2)}) collective-permute-start(bf16[4,4,288,128]{3,2,1,0:T(8,128)(2,1)} %all-to-all-done.1.near), channel_id=1, source_target_pairs={{0,8},{8,0},{1,9},{9,1},{2,10},{10,2},{3,11},{11,3},{4,12},{12,4},... | collective-permute-start | bytes 3538952 | tf_op jit(solution)/shard_map/ppermute | solution.py:406
  56.8 1.7 copy-start.6
  58.6 12.1 %copy-start.5 = (bf16[80,1024]{1,0:T(8,128)(2,1)S(1)}, bf16[80,1024]{1,0:T(8,128)(2,1)}, u32[]{:S(2)}) copy-start(bf16[80,1024]{1,0:T(8,128)(2,1)} %w_ref.3) | copy-start | bytes 491524
  62.5 8.1 %collective-permute-start.5 = (bf16[4,4,288,128]{3,2,1,0:T(8,128)(2,1)}, bf16[4,4,288,128]{3,2,1,0:T(8,128)(2,1)S(1)}, u32[]{:S(2)}, u32[]{:S(2)}) collective-permute-start(bf16[4,4,288,128]{3,2,1,0:T(8,128)(2,1)} %all-to-all-done.2.far), channel_id=1, source_target_pairs={{0,8},{8,0},{1,9},{9,1},{2,10},{10,2},{3,11},{11,3},{4,12},{12,4},... | collective-permute-start | bytes 3538952 | tf_op jit(solution)/shard_map/ppermute | solution.py:409
  68.1 42.3 %copy-start.4 = (bf16[128,1024]{1,0:T(8,128)(2,1)S(1)}, bf16[128,1024]{1,0:T(8,128)(2,1)}, u32[]{:S(2)}) copy-start(bf16[128,1024]{1,0:T(8,128)(2,1)} %q_ref.5) | copy-start | bytes 786436
  70.7 18.3 %copy-start.1 = (bf16[4,4,288,128]{3,2,1,0:T(8,128)(2,1)}, bf16[4,4,288,128]{3,2,1,0:T(8,128)(2,1)S(1)}, u32[]{:S(2)}) copy-start(bf16[4,4,288,128]{3,2,1,0:T(8,128)(2,1)S(1)} %collective-permute-done.5.far_other) | copy-start | bytes 3538948
  98.3 24.0 %all-to-all-start.4 = ((bf16[16,40,128]{2,1,0:T(8,128)(2,1)}), bf16[16,40,128]{2,1,0:T(8,128)(2,1)S(1)}, u32[]{:S(2)}, u32[]{:S(2)}) async-start(bf16[16,40,128]{2,1,0:T(8,128)(2,1)} %get-tuple-element.56), calls=%async_computation.4 | async-start | bytes 327680 | tf_op jit(solution)/shard_map/all_to_all | solution.py:452
  110.4 1.3 copy-start.2
  123.5 19.0 %all-to-all-start.5 = ((bf16[16,320,128]{2,1,0:T(8,128)(2,1)}), bf16[16,320,128]{2,1,0:T(8,128)(2,1)}, u32[]{:S(2)}, u32[]{:S(2)}) async-start(bf16[16,320,128]{2,1,0:T(8,128)(2,1)} %copy-done), calls=%async_computation.5 | async-start | bytes 2621440 | tf_op jit(solution)/shard_map/all_to_all | solution.py:457
  142.5 11.9 %collective-permute-start.6 = (bf16[4,2,640,128]{3,2,1,0:T(8,128)(2,1)}, bf16[4,2,640,128]{3,2,1,0:T(8,128)(2,1)}, u32[]{:S(2)}, u32[]{:S(2)}) collective-permute-start(bf16[4,2,640,128]{3,2,1,0:T(8,128)(2,1)} %bitcast.29.own_ref), channel_id=1, source_target_pairs={{0,8},{8,0},{1,9},{9,1},{2,10},{10,2},{3,11},{11,3},{4,12},{12,4},... | collective-permute-start | bytes 3932168 | tf_op jit(solution)/shard_map/ppermute | solution.py:459
  168.3 19.8 %all-to-all-start.7 = ((f32[16,8,128]{2,1,0:T(8,128)}), f32[16,8,128]{2,1,0:T(8,128)S(1)}, u32[]{:S(2)}, u32[]{:S(2)}) async-start(f32[16,8,128]{2,1,0:T(8,128)} %merge.1), calls=%async_computation.7 | async-start | bytes 131072 | tf_op jit(solution)/shard_map/all_to_all | solution.py:475
  (2 other events, 2.3 us)

commit v9 on v8

--- a/solution.py
+++ b/solution.py
@@ -103,7 +103,7 @@
         copy.wait()
 
 
-def weight_kernel(source_ref, gain_ref, w_ref, out_ref):
+def weight_kernel(source_ref, gain_ref, w_ref, early_ref, out_ref):
     width = 1280
     move = (iota((width, width), 0) == source_ref[...]).astype(jnp.bfloat16)
     for x in range(4):
@@ -365,8 +365,8 @@
     )
     source = jnp.asarray(source_columns())
     weight = call(
-        weight_kernel, (256, D), jnp.bfloat16, [VMEM] * 3, flops=2 * 256 * D * 1280, name="weight", vmem=28
-    )(source, norm_gain[None, :], head_weight)
+        weight_kernel, (256, D), jnp.bfloat16, [VMEM] * 4, flops=2 * 256 * D * 1280, name="weight", vmem=28
+    )(source, norm_gain[None, :], head_weight, out_weight)
     slabs = loss_mask.reshape(64, SLAB)
     upto = jnp.tril(jnp.ones((SLAB, SLAB), jnp.float32)).T
     rank = jnp.dot(slabs.astype(jnp.float32), upto, preferred_element_type=jnp.float32).astype(jnp.int32)

time: 190 us -> 191 us (level)
  no operation moved by 1% of the time
where the time goes in v9:
time: 191 us; the launch traced here: 189 us
  starting transfers between devices  80.5 us (42%)
  Pallas kernels  42.7 us (22%)
  waiting for transfers between devices  34.8 us (18%)
  blocking collectives  19.4 us (10%)
  local copies, waits for them, and re-layouts  7.69 us (4%)
  other arithmetic  2.18 us (1%)
    pallas_call x1, Pallas kernels, body(): call(scored_kernel, (4, HALF, 128), jnp.float32, [SMEM, SMEM, VMEM, VMEM]...  18.3 us
    ppermute x3, starting transfers between devices, body(): lax.ppermute(block, 'zl', [(i, i ^ k) for i in range(4)])  14.1 us
    all_to_all x1, starting transfers between devices, body(): sums = lax.all_to_all(sums, ('h', 'zh', 'zl'), 0, 0)  11.8 us
    all_to_all x1, blocking collectives, body(): tiles = lax.all_to_all(tiles, ('x', 'y', 'c'), 0, 0)  10.9 us
    all_to_all x1, waiting for transfers between devices, body(): tiles = lax.all_to_all(tiles, ('h', 'zh', 'zl'), 0, 0)  10.8 us
    all_to_all x1, waiting for transfers between devices, body(): hidden = lax.all_to_all(hidden, ('x', 'y'), 0, 0).reshape(4, 2, 640, 128)  9.1 us
    ppermute x1, starting transfers between devices, body(): hidden_other = lax.ppermute(hidden, 'c', [(0, 1), (1, 0)])  8.9 us
    ppermute x1, starting transfers between devices, body(): block = lax.ppermute(block, ('zh', 'zl'), [(i, i ^ 4) for i in range(8)])  8.8 us
  transfers between devices with their start and end apart: 13, of which 9 were waited for; matrix products, arithmetic and copies ran while one was open for 2% of the time, Pallas kernels for 9%

profile of v9, /device:TPU:1, one launch (start us, length us, event | category | flops | bytes accessed | tf_op | source)
XLA Modules:
  0.0 188.7 jit_solution(14711674680639822002)
XLA Ops:
  0.7 2.7 %pack.1 = (bf16[288,128]{1,0:T(8,128)(2,1)}, bf16[4,288,128]{2,1,0:T(8,128)(2,1)}) custom-call(s32[1]{0:T(128)} %bitcast.1.at_ref, s32[64,128]{1,0:T(8,128)} %bitcast.69, bf16[128,1024]{1,0:T(8,128)(2,1)} %q_ref.5, bf16[128,128]{1,0:T(8,128)(2,1)} %k_ref.1, bf16[128,128]{1,0:T(8,128)(2,1)} %v_ref.1), custom_call_target="tpu_custom_call" | custom-call | tf_op jit(solution)/shard_map/pack/pallas_call | solution.py:327
  3.3 6.5 %all-to-all-start = ((bf16[4,288,128]{2,1,0:T(8,128)(2,1)}), bf16[4,288,128]{2,1,0:T(8,128)(2,1)S(1)}, u32[]{:S(2)}, u32[]{:S(2)}) async-start(bf16[4,288,128]{2,1,0:T(8,128)(2,1)} %get-tuple-element.35), calls=%async_computation | async-start | bytes 589824 | tf_op jit(solution)/shard_map/all_to_all | solution.py:345
  9.8 8.8 %collective-permute-start = (bf16[288,128]{1,0:T(8,128)(2,1)}, bf16[288,128]{1,0:T(8,128)(2,1)S(1)}, u32[]{:S(2)}, u32[]{:S(2)}) collective-permute-start(bf16[288,128]{1,0:T(8,128)(2,1)} %get-tuple-element.36), channel_id=1, source_target_pairs={{0,64},{16,80},{32,96},{48,112},{64,0},{80,16},{96,32},{112,48},{1... | collective-permute-start | bytes 221192 | tf_op jit(solution)/shard_map/ppermute | solution.py:344
  20.7 4.3 %all-to-all-start.1 = ((bf16[4,4,288,128]{3,2,1,0:T(8,128)(2,1)}), bf16[4,4,288,128]{3,2,1,0:T(8,128)(2,1)}, u32[]{:S(2)}, u32[]{:S(2)}) async-start(bf16[4,4,288,128]{3,2,1,0:T(8,128)(2,1)} %spread.1), calls=%async_computation.1 | async-start | bytes 2359296 | tf_op jit(solution)/shard_map/all_to_all | solution.py:350
  25.0 9.7 %collective-permute-start.3 = (bf16[288,128]{1,0:T(8,128)(2,1)S(1)}, bf16[288,128]{1,0:T(8,128)(2,1)S(1)}, u32[]{:S(2)}, u32[]{:S(2)}) collective-permute-start(bf16[288,128]{1,0:T(8,128)(2,1)S(1)} %collective-permute-done.refs_0_), channel_id=1, source_target_pairs={{0,48},{16,32},{32,16},{48,0},{1,49},{17,33},{33,17},{49,1},{2,50}... | collective-permute-start | bytes 221192 | tf_op jit(solution)/shard_map/ppermute | solution.py:351
  39.1 3.0 %collective-permute-done.2.refs_2_ = bf16[288,128]{1,0:T(8,128)(2,1)S(1)} collective-permute-done((bf16[288,128]{1,0:T(8,128)(2,1)S(1)}, bf16[288,128]{1,0:T(8,128)(2,1)S(1)}, u32[]{:S(2)}, u32[]{:S(2)}) %collective-permute-start.2) | collective-permute-done | bytes 73760 | tf_op jit(solution)/shard_map/ppermute | solution.py:351
  44.3 4.3 %all-to-all-start.2 = ((bf16[4,4,288,128]{3,2,1,0:T(8,128)(2,1)}), bf16[4,4,288,128]{3,2,1,0:T(8,128)(2,1)}, u32[]{:S(2)}, u32[]{:S(2)}) async-start(bf16[4,4,288,128]{3,2,1,0:T(8,128)(2,1)} %spread_far.1), calls=%async_computation.2 | async-start | bytes 2359296 | tf_op jit(solution)/shard_map/all_to_all | solution.py:362
  52.3 4.5 %collective-permute-start.4 = (bf16[4,4,288,128]{3,2,1,0:T(8,128)(2,1)}, bf16[4,4,288,128]{3,2,1,0:T(8,128)(2,1)}, u32[]{:S(2)}, u32[]{:S(2)}) collective-permute-start(bf16[4,4,288,128]{3,2,1,0:T(8,128)(2,1)} %all-to-all-done.1.near), channel_id=1, source_target_pairs={{0,8},{8,0},{1,9},{9,1},{2,10},{10,2},{3,11},{11,3},{4,12},{12,4},... | collective-permute-start | bytes 3538952 | tf_op jit(solution)/shard_map/ppermute | solution.py:406
  58.6 3.7 %weight.1.w_ref = bf16[256,5120]{1,0:T(8,128)(2,1)S(1)} custom-call(s32[1,1280]{1,0:T(1,128)S(1)} %copy-done.8, f32[1,5120]{1,0:T(1,128)S(1)} %bitcast.51, bf16[256,5120]{1,0:T(8,128)(2,1)S(1)} %copy-done.6, bf16[80,1024]{1,0:T(8,128)(2,1)S(1)} %copy-done.5), custom_call_target="tpu_custom_call" | custom-call | flops 3355443200 | tf_op jit(solution)/shard_map/weight/pallas_call | solution.py:367
  62.5 5.4 %collective-permute-start.5 = (bf16[4,4,288,128]{3,2,1,0:T(8,128)(2,1)}, bf16[4,4,288,128]{3,2,1,0:T(8,128)(2,1)S(1)}, u32[]{:S(2)}, u32[]{:S(2)}) collective-permute-start(bf16[4,4,288,128]{3,2,1,0:T(8,128)(2,1)} %all-to-all-done.2.far), channel_id=1, source_target_pairs={{0,8},{8,0},{1,9},{9,1},{2,10},{10,2},{3,11},{11,3},{4,12},{12,4},... | collective-permute-start | bytes 3538952 | tf_op jit(solution)/shard_map/ppermute | solution.py:409
  68.1 2.6 %collective-permute-done.5.far_other = bf16[4,4,288,128]{3,2,1,0:T(8,128)(2,1)S(1)} collective-permute-done((bf16[4,4,288,128]{3,2,1,0:T(8,128)(2,1)}, bf16[4,4,288,128]{3,2,1,0:T(8,128)(2,1)S(1)}, u32[]{:S(2)}, u32[]{:S(2)}) %collective-permute-start.5) | collective-permute-done | bytes 1179680 | tf_op jit(solution)/shard_map/ppermute | solution.py:409
  70.7 18.3 %scored.1 = f32[4,40,128]{2,1,0:T(8,128)S(1)} custom-call(s32[2]{0:T(128)S(1)} %pad_add_fusion.1.core_ref, s32[8]{0:T(128)S(1)} %and_select_fusion.first_ref, s32[8,256]{1,0:T(8,128)S(1)} %reshape.119.low_ref, s32[8,256]{1,0:T(8,128)S(1)} %reshape.126.high_ref, bf16[4,4,288,128]{3,2,1,0:T(8,128)(2,1)} %all-to-all-done.1.near, ...), custom_call_target="tpu_custom_call" | custom-call | tf_op jit(solution)/shard_map/scored/pallas_call | solution.py:413
  88.9 8.5 %all_to_all.40.parts_ref = f32[4,40,128]{2,1,0:T(8,128)S(1)} all-to-all(f32[4,40,128]{2,1,0:T(8,128)S(1)} %scored.1), channel_id=1, replica_groups=mesh['x'=4,'zh'=2,'zl'=4,'c'=2,'h'=2,'y'=4] {'y'}, dimensions={0} | all-to-all | bytes 163840 | tf_op jit(solution)/shard_map/all_to_all | solution.py:439
  98.3 11.8 %all-to-all-start.4 = ((bf16[16,40,128]{2,1,0:T(8,128)(2,1)}), bf16[16,40,128]{2,1,0:T(8,128)(2,1)S(1)}, u32[]{:S(2)}, u32[]{:S(2)}) async-start(bf16[16,40,128]{2,1,0:T(8,128)(2,1)} %get-tuple-element.56), calls=%async_computation.4 | async-start | bytes 327680 | tf_op jit(solution)/shard_map/all_to_all | solution.py:452
  111.6 4.2 %context.2 = (bf16[128,512]{1,0:T(8,128)(2,1)S(1)}, f32[8,128]{1,0:T(8,128)S(1)}) custom-call(s32[4]{0:T(128)S(1)} %pad_add_fusion.at_ref, s32[1,128]{1,0:T(1,128)S(1)} %bitcast.49, s32[1,128]{1,0:T(1,128)S(1)} %iota_add_fusion.high_ref, bf16[4,4,288,128]{3,2,1,0:T(8,128)(2,1)} %all-to-all-done.1.near, bf16[4,4,288,128]{3,2,1,0:T(8,128)(2,1)} %all-to-all-done.2.far, ...), custom_call_target="tpu_custom_call" | custom-call | flops 2214592512 | bytes 6291456 | tf_op jit(solution)/shard_map/context/pallas_call | solution.py:426
  115.9 6.4 %all-to-all-done.4.parts_ref = bf16[16,40,128]{2,1,0:T(8,128)(2,1)S(1)} async-done(((bf16[16,40,128]{2,1,0:T(8,128)(2,1)}), bf16[16,40,128]{2,1,0:T(8,128)(2,1)S(1)}, u32[]{:S(2)}, u32[]{:S(2)}) %all-to-all-start.4) | async-done | bytes 163872 | tf_op jit(solution)/shard_map/all_to_all | solution.py:452
  123.5 4.4 %all-to-all-start.5 = ((bf16[16,320,128]{2,1,0:T(8,128)(2,1)}), bf16[16,320,128]{2,1,0:T(8,128)(2,1)}, u32[]{:S(2)}, u32[]{:S(2)}) async-start(bf16[16,320,128]{2,1,0:T(8,128)(2,1)} %copy-done), calls=%async_computation.5 | async-start | bytes 2621440 | tf_op jit(solution)/shard_map/all_to_all | solution.py:457
  129.2 4.2 %context.3 = (bf16[128,512]{1,0:T(8,128)(2,1)S(1)}, f32[8,128]{1,0:T(8,128)S(1)}) custom-call(s32[4]{0:T(128)S(1)} %pad_add_fusion.at_ref, s32[1,128]{1,0:T(1,128)S(1)} %bitcast.50, s32[1,128]{1,0:T(1,128)S(1)} %iota_add_fusion.high_ref, bf16[4,4,288,128]{3,2,1,0:T(8,128)(2,1)} %all-to-all-done.1.near, bf16[4,4,288,128]{3,2,1,0:T(8,128)(2,1)} %all-to-all-done.2.far, ...), custom_call_target="tpu_custom_call" | custom-call | flops 2214592512 | bytes 6291456 | tf_op jit(solution)/shard_map/context/pallas_call | solution.py:426
  133.4 9.1 %all-to-all-done.5 = bf16[16,320,128]{2,1,0:T(8,128)(2,1)} async-done(((bf16[16,320,128]{2,1,0:T(8,128)(2,1)}), bf16[16,320,128]{2,1,0:T(8,128)(2,1)}, u32[]{:S(2)}, u32[]{:S(2)}) %all-to-all-start.5) | async-done | bytes 1310752 | tf_op jit(solution)/shard_map/all_to_all | solution.py:457
  142.5 8.9 %collective-permute-start.6 = (bf16[4,2,640,128]{3,2,1,0:T(8,128)(2,1)}, bf16[4,2,640,128]{3,2,1,0:T(8,128)(2,1)}, u32[]{:S(2)}, u32[]{:S(2)}) collective-permute-start(bf16[4,2,640,128]{3,2,1,0:T(8,128)(2,1)} %bitcast.29.own_ref), channel_id=1, source_target_pairs={{0,8},{8,0},{1,9},{9,1},{2,10},{10,2},{3,11},{11,3},{4,12},{12,4},... | collective-permute-start | bytes 3932168 | tf_op jit(solution)/shard_map/ppermute | solution.py:459
  154.4 2.3 %logits.1 = f32[32,8,128]{2,1,0:T(8,128)S(1)} custom-call(s32[2]{0:T(128)S(1)} %pad_add_fusion.3.at_ref, s32[2,128]{1,0:T(2,128)S(1)} %reshape.128.ids_ref, f32[2,256,128]{2,1,0:T(8,128)S(1)} %get-tuple-element.65.sum_ref, f32[2,8,128]{2,1,0:T(8,128)S(1)} %get-tuple-element.66.square_ref, bf16[4,2,640,128]{3,2,1,0:T(8,128)(2,1)} %collective-permute-done.6.other_ref, ...), custom_call_target="tpu_custom_call" | custom-call | tf_op jit(solution)/shard_map/logits/pallas_call | solution.py:469
  156.7 10.9 %all_to_all.41.parts_ref = f32[32,8,128]{2,1,0:T(8,128)S(1)} all-to-all(f32[32,8,128]{2,1,0:T(8,128)S(1)} %logits.1), channel_id=1, replica_groups=mesh['x'=4,'zh'=2,'zl'=4,'c'=2,'h'=2,'y'=4] {'x','y','c'}, dimensions={0} | all-to-all | bytes 262144 | tf_op jit(solution)/shard_map/all_to_all | solution.py:473
  168.3 7.6 %all-to-all-start.7 = ((f32[16,8,128]{2,1,0:T(8,128)}), f32[16,8,128]{2,1,0:T(8,128)S(1)}, u32[]{:S(2)}, u32[]{:S(2)}) async-start(f32[16,8,128]{2,1,0:T(8,128)} %merge.1), calls=%async_computation.7 | async-start | bytes 131072 | tf_op jit(solution)/shard_map/all_to_all | solution.py:475
  176.7 10.8 %all-to-all-done.7.parts_ref = f32[16,8,128]{2,1,0:T(8,128)S(1)} async-done(((f32[16,8,128]{2,1,0:T(8,128)}), f32[16,8,128]{2,1,0:T(8,128)S(1)}, u32[]{:S(2)}, u32[]{:S(2)}) %all-to-all-start.7) | async-done | bytes 65568 | tf_op jit(solution)/shard_map/all_to_all | solution.py:475
  (84 shorter events, 24.5 us)
Async XLA Ops:
  3.3 15.3 %all-to-all-start = ((bf16[4,288,128]{2,1,0:T(8,128)(2,1)}), bf16[4,288,128]{2,1,0:T(8,128)(2,1)S(1)}, u32[]{:S(2)}, u32[]{:S(2)}) async-start(bf16[4,288,128]{2,1,0:T(8,128)(2,1)} %get-tuple-element.35), calls=%async_computation | async-start | bytes 589824 | tf_op jit(solution)/shard_map/all_to_all | solution.py:345
  9.8 10.9 %collective-permute-start = (bf16[288,128]{1,0:T(8,128)(2,1)}, bf16[288,128]{1,0:T(8,128)(2,1)S(1)}, u32[]{:S(2)}, u32[]{:S(2)}) collective-permute-start(bf16[288,128]{1,0:T(8,128)(2,1)} %get-tuple-element.36), channel_id=1, source_target_pairs={{0,64},{16,80},{32,96},{48,112},{64,0},{80,16},{96,32},{112,48},{1... | collective-permute-start | bytes 221192 | tf_op jit(solution)/shard_map/ppermute | solution.py:344
  20.7 23.6 %all-to-all-start.1 = ((bf16[4,4,288,128]{3,2,1,0:T(8,128)(2,1)}), bf16[4,4,288,128]{3,2,1,0:T(8,128)(2,1)}, u32[]{:S(2)}, u32[]{:S(2)}) async-start(bf16[4,4,288,128]{3,2,1,0:T(8,128)(2,1)} %spread.1), calls=%async_computation.1 | async-start | bytes 2359296 | tf_op jit(solution)/shard_map/all_to_all | solution.py:350
  25.0 14.1 %collective-permute-start.3 = (bf16[288,128]{1,0:T(8,128)(2,1)S(1)}, bf16[288,128]{1,0:T(8,128)(2,1)S(1)}, u32[]{:S(2)}, u32[]{:S(2)}) collective-permute-start(bf16[288,128]{1,0:T(8,128)(2,1)S(1)} %collective-permute-done.refs_0_), channel_id=1, source_target_pairs={{0,48},{16,32},{32,16},{48,0},{1,49},{17,33},{33,17},{49,1},{2,50}... | collective-permute-start | bytes 221192 | tf_op jit(solution)/shard_map/ppermute | solution.py:351
  34.7 7.3 %collective-permute-start.2 = (bf16[288,128]{1,0:T(8,128)(2,1)S(1)}, bf16[288,128]{1,0:T(8,128)(2,1)S(1)}, u32[]{:S(2)}, u32[]{:S(2)}) collective-permute-start(bf16[288,128]{1,0:T(8,128)(2,1)S(1)} %collective-permute-done.refs_0_), channel_id=1, source_target_pairs={{0,32},{16,48},{32,0},{48,16},{1,33},{17,49},{33,1},{49,17},{2,34}... | collective-permute-start | bytes 221192 | tf_op jit(solution)/shard_map/ppermute | solution.py:351
  36.8 6.2 %collective-permute-start.1 = (bf16[288,128]{1,0:T(8,128)(2,1)S(1)}, bf16[288,128]{1,0:T(8,128)(2,1)S(1)}, u32[]{:S(2)}, u32[]{:S(2)}) collective-permute-start(bf16[288,128]{1,0:T(8,128)(2,1)S(1)} %collective-permute-done.refs_0_), channel_id=1, source_target_pairs={{0,16},{16,0},{32,48},{48,32},{1,17},{17,1},{33,49},{49,33},{2,18}... | collective-permute-start | bytes 221192 | tf_op jit(solution)/shard_map/ppermute | solution.py:351
  44.3 4.3 %copy-start.12 = (s32[32]{0:T(128)S(1)}, s32[32]{0:T(128)}, u32[]{:S(2)}) copy-start(s32[32]{0:T(128)} %param.20) | copy-start | bytes 388
  44.3 4.9 %copy-start.11 = (s32[8192]{0:T(1024)S(1)}, s32[8192]{0:T(1024)}, u32[]{:S(2)}) copy-start(s32[8192]{0:T(1024)} %param.19) | copy-start | bytes 98308
  44.3 5.0 %copy-start.10 = (s32[8192]{0:T(1024)S(1)}, s32[8192]{0:T(1024)}, u32[]{:S(2)}) copy-start(s32[8192]{0:T(1024)} %param.18) | copy-start | bytes 98308
  44.3 5.7 %copy-start.9 = (bf16[80,256]{1,0:T(8,128)(2,1)S(1)}, bf16[80,256]{1,0:T(8,128)(2,1)}, u32[]{:S(2)}) copy-start(bf16[80,256]{1,0:T(8,128)(2,1)} %param.15) | copy-start | bytes 122884
  44.3 18.2 %all-to-all-start.2 = ((bf16[4,4,288,128]{3,2,1,0:T(8,128)(2,1)}), bf16[4,4,288,128]{3,2,1,0:T(8,128)(2,1)}, u32[]{:S(2)}, u32[]{:S(2)}) async-start(bf16[4,4,288,128]{3,2,1,0:T(8,128)(2,1)} %spread_far.1), calls=%async_computation.2 | async-start | bytes 2359296 | tf_op jit(solution)/shard_map/all_to_all | solution.py:362
  48.9 8.0 %copy-start.5 = (bf16[80,1024]{1,0:T(8,128)(2,1)S(1)}, bf16[80,1024]{1,0:T(8,128)(2,1)}, u32[]{:S(2)}) copy-start(bf16[80,1024]{1,0:T(8,128)(2,1)} %w_ref.3) | copy-start | bytes 491524
  48.9 8.0 %copy-start.7 = (f32[5120]{0:T(1024)S(1)}, f32[5120]{0:T(1024)}, u32[]{:S(2)}) copy-start(f32[5120]{0:T(1024)} %param.16) | copy-start | bytes 61444
  48.9 8.0 %copy-start.8 = (s32[1,1280]{1,0:T(1,128)S(1)}, s32[1,1280]{1,0:T(1,128)}, u32[]{:S(2)}) copy-start(s32[1,1280]{1,0:T(1,128)} %constant.87.clone.source_ref) | copy-start | bytes 15364
  52.3 15.8 %collective-permute-start.4 = (bf16[4,4,288,128]{3,2,1,0:T(8,128)(2,1)}, bf16[4,4,288,128]{3,2,1,0:T(8,128)(2,1)}, u32[]{:S(2)}, u32[]{:S(2)}) collective-permute-start(bf16[4,4,288,128]{3,2,1,0:T(8,128)(2,1)} %all-to-all-done.1.near), channel_id=1, source_target_pairs={{0,8},{8,0},{1,9},{9,1},{2,10},{10,2},{3,11},{11,3},{4,12},{12,4},... | collective-permute-start | bytes 3538952 | tf_op jit(solution)/shard_map/ppermute | solution.py:406
  56.8 1.7 copy-start.6
  62.5 8.1 %collective-permute-start.5 = (bf16[4,4,288,128]{3,2,1,0:T(8,128)(2,1)}, bf16[4,4,288,128]{3,2,1,0:T(8,128)(2,1)S(1)}, u32[]{:S(2)}, u32[]{:S(2)}) collective-permute-start(bf16[4,4,288,128]{3,2,1,0:T(8,128)(2,1)} %all-to-all-done.2.far), channel_id=1, source_target_pairs={{0,8},{8,0},{1,9},{9,1},{2,10},{10,2},{3,11},{11,3},{4,12},{12,4},... | collective-permute-start | bytes 3538952 | tf_op jit(solution)/shard_map/ppermute | solution.py:409
  68.1 42.3 %copy-start.4 = (bf16[128,1024]{1,0:T(8,128)(2,1)S(1)}, bf16[128,1024]{1,0:T(8,128)(2,1)}, u32[]{:S(2)}) copy-start(bf16[128,1024]{1,0:T(8,128)(2,1)} %q_ref.5) | copy-start | bytes 786436
  70.7 18.3 %copy-start.1 = (bf16[4,4,288,128]{3,2,1,0:T(8,128)(2,1)}, bf16[4,4,288,128]{3,2,1,0:T(8,128)(2,1)S(1)}, u32[]{:S(2)}) copy-start(bf16[4,4,288,128]{3,2,1,0:T(8,128)(2,1)S(1)} %collective-permute-done.5.far_other) | copy-start | bytes 3538948
  98.3 24.0 %all-to-all-start.4 = ((bf16[16,40,128]{2,1,0:T(8,128)(2,1)}), bf16[16,40,128]{2,1,0:T(8,128)(2,1)S(1)}, u32[]{:S(2)}, u32[]{:S(2)}) async-start(bf16[16,40,128]{2,1,0:T(8,128)(2,1)} %get-tuple-element.56), calls=%async_computation.4 | async-start | bytes 327680 | tf_op jit(solution)/shard_map/all_to_all | solution.py:452
  110.4 1.3 copy-start.2
  123.5 19.0 %all-to-all-start.5 = ((bf16[16,320,128]{2,1,0:T(8,128)(2,1)}), bf16[16,320,128]{2,1,0:T(8,128)(2,1)}, u32[]{:S(2)}, u32[]{:S(2)}) async-start(bf16[16,320,128]{2,1,0:T(8,128)(2,1)} %copy-done), calls=%async_computation.5 | async-start | bytes 2621440 | tf_op jit(solution)/shard_map/all_to_all | solution.py:457
  142.5 11.9 %collective-permute-start.6 = (bf16[4,2,640,128]{3,2,1,0:T(8,128)(2,1)}, bf16[4,2,640,128]{3,2,1,0:T(8,128)(2,1)}, u32[]{:S(2)}, u32[]{:S(2)}) collective-permute-start(bf16[4,2,640,128]{3,2,1,0:T(8,128)(2,1)} %bitcast.29.own_ref), channel_id=1, source_target_pairs={{0,8},{8,0},{1,9},{9,1},{2,10},{10,2},{3,11},{11,3},{4,12},{12,4},... | collective-permute-start | bytes 3932168 | tf_op jit(solution)/shard_map/ppermute | solution.py:459
  168.3 19.2 %all-to-all-start.7 = ((f32[16,8,128]{2,1,0:T(8,128)}), f32[16,8,128]{2,1,0:T(8,128)S(1)}, u32[]{:S(2)}, u32[]{:S(2)}) async-start(f32[16,8,128]{2,1,0:T(8,128)} %merge.1), calls=%async_computation.7 | async-start | bytes 131072 | tf_op jit(solution)/shard_map/all_to_all | solution.py:475
  (2 other events, 2.3 us)
